TPU v7x, 32 devices: a whole 2x2x4 slice. The times are simulated.
32 devices in a mesh: fsdp: 4 (over z), tp: 4 (over y, core), rep: 2 (over x).
Axes of the slice: x: 2, y: 2, z: 4, core: 2. Of those that a mesh axis runs over, the one named last changes fastest.
Arguments:
- hidden: bfloat16 [1024, 16384], P(('rep', 'fsdp')), parts along dimension 0, may hold values from -400 to 400
- base_weight: bfloat16 [32768, 16384], P(('rep', 'fsdp', 'tp')), parts along dimension 0, may hold values from -1 to 1
- adapter_down: bfloat16 [32768, 32], P(('rep', 'fsdp', 'tp')), parts along dimension 0, may hold values from -0.046875 to 0.046875
- adapter_up: bfloat16 [64, 16384], P('rep'), parts along dimension 0, may hold values from -0.1796875 to 0.1796875
- norm_gain: bfloat16 [32768], P('rep'), parts along dimension 0, may hold values from 0.25 to 1.75
- positions: int32 [1024], P(('rep', 'fsdp')), parts along dimension 0, may hold values from 0 to 4606, as said below
Outputs:
- queries: bfloat16 [1024, 16384], P(('rep', 'fsdp'), 'tp'), parts along dimension 0
There are 2 independent parts, one for each index of `rep`. A program takes and returns all parts, laid end to end along the dimension named above; each array names one. Nothing has to cross between parts.
Inputs may be any that keep to these rules, and one draw needn't show every extreme that they name: Within a document positions rise by one from token to token; every document after the first starts at 0; the first document continues an earlier one and its last token has position 4606.
All inputs are finite; a program needn't handle non-finite values.
Results may differ from a plain program's by a relative error of at most 0.018.
Values may be sent and summed in bfloat16 or wider, within the bound.
No kernel may reach another device: no remote copies, remote signals or barrier semaphores. Data moves between devices by JAX's collectives and lax.ppermute only.
A program may use at most 320 MiB of HBM per device.

v0:
```python
import math

import jax
import jax.numpy as jnp
from jax import lax
from jax.sharding import PartitionSpec as P

HEAD = 128
BLOCK = 128


norm_epsilon = 1e-05
scale_epsilon = 1e-06
code_limit = 15.0
adapter_scale = 2.0
rope_theta = 500000.0
rope_factor = 8.0
low_factor = 1.0
high_factor = 4.0
initial_context = 8192.0


def normalize(hidden, norm_gain):
    values = hidden.astype(jnp.float32)
    mean_square = jnp.mean(values * values, axis=1, keepdims=True)
    return (
        values * lax.rsqrt(mean_square + norm_epsilon) * norm_gain.astype(jnp.float32)[None, :]
    ).astype(jnp.bfloat16)


def quantize(base_rows, low_rank):
    merged = base_rows.astype(jnp.float32) + adapter_scale * low_rank
    row_count, col_count = merged.shape
    tiles = merged.reshape(row_count // BLOCK, BLOCK, col_count // BLOCK, BLOCK)
    largest = jnp.max(jnp.abs(tiles), axis=(1, 3))
    exponent = jnp.ceil(jnp.log2((largest + scale_epsilon) / code_limit))
    scales = jnp.exp2(exponent).astype(jnp.bfloat16)
    quantized = jnp.floor(tiles / scales.astype(jnp.float32)[:, None, :, None] + 0.5).astype(
        jnp.bfloat16
    )
    return (quantized.reshape(row_count, col_count), scales)


def dequantize(quantized, scales):
    row_count, col_count = quantized.shape
    tiles = quantized.reshape(row_count // BLOCK, BLOCK, col_count // BLOCK, BLOCK).astype(
        jnp.float32
    )
    return (
        (tiles * scales.astype(jnp.float32)[:, None, :, None])
        .astype(jnp.bfloat16)
        .reshape(row_count, col_count)
    )


def frequencies(positions):
    pair_index = jnp.arange(HEAD // 2, dtype=jnp.float32)
    inverse = jnp.exp(pair_index * (-2.0 * math.log(rope_theta) / HEAD))
    wavelength = 2.0 * math.pi / inverse
    blend = (initial_context / wavelength - low_factor) / (high_factor - low_factor)
    middle = (1.0 - blend) * inverse / rope_factor + blend * inverse
    adjusted = jnp.where(
        wavelength < initial_context / high_factor,
        inverse,
        jnp.where(wavelength > initial_context / low_factor, inverse / rope_factor, middle),
    )
    angles = positions.astype(jnp.float32)[:, None] * adjusted[None, :]
    return (jnp.cos(angles), jnp.sin(angles))


def rotate(projected, positions):
    cosine, sine_part = frequencies(positions)
    row_count, full_width = projected.shape
    half_head = HEAD // 2
    per_head = projected.reshape(row_count, full_width // HEAD, HEAD)
    first_half = per_head[:, :, :half_head]
    second_half = per_head[:, :, half_head:]
    cosine = cosine[:, None, :]
    sine_part = sine_part[:, None, :]
    turned = jnp.concatenate(
        [
            first_half * cosine - second_half * sine_part,
            second_half * cosine + first_half * sine_part,
        ],
        axis=2,
    )
    return turned.reshape(row_count, full_width)


def shards(hidden, base_weight, adapter_down, adapter_up, norm_gain, positions):
    normed = normalize(hidden, norm_gain)
    low_rank = jnp.dot(adapter_down, adapter_up, preferred_element_type=jnp.float32)
    quantized, scales = quantize(base_weight, low_rank)
    quantized, scales = (
        lax.all_to_all(quantized, "tp", split_axis=1, concat_axis=0, tiled=True),
        lax.all_to_all(scales, "tp", split_axis=1, concat_axis=0, tiled=True),
    )
    weight = dequantize(quantized, scales)
    gathered = lax.all_to_all(normed, "fsdp", split_axis=1, concat_axis=0, tiled=True)
    projected = lax.psum_scatter(
        jnp.dot(gathered, weight, preferred_element_type=jnp.float32).astype(jnp.bfloat16),
        "fsdp",
        scatter_dimension=0,
        tiled=True,
    ).astype(jnp.float32)
    return rotate(projected, positions).astype(jnp.bfloat16)


def solution(mesh):
    placed = (
        P(("rep", "fsdp"), None),
        P(("rep", "fsdp", "tp"), None),
        P(("rep", "fsdp", "tp"), None),
        P("rep", None),
        P("rep"),
        P(("rep", "fsdp")),
    )
    return jax.shard_map(
        shards, mesh=mesh, in_specs=placed, out_specs=P(("rep", "fsdp"), "tp"), check_vma=False
    )
```

profile of v0, /device:TPU:0, one launch (start us, length us, event | category | flops | bytes accessed | tf_op | source)
XLA Modules:
  0.0 889.0 jit_solution(4219219824015037547)
XLA Ops:
  6.5 1.2 copy-done
  7.8 24.8 %fusion.13 = f32[1024,16384]{1,0:T(8,128)} fusion(bf16[1024,32]{0,1:T(8,128)(2,1)} %param.8, bf16[32,16384]{1,0:T(8,128)(2,1)S(1)} %copy-done), kind=kOutput, calls=%fused_computation.32 | convolution fusion | flops 1073741824 | bytes 68222976 | tf_op jit(solution)/shard_map/dot_general | solution.py:92
  32.6 52.8 %abs_bitcast_fusion = f32[128,8,128,128]{3,1,2,0:T(8,128)} fusion(f32[1024,16384]{1,0:T(8,128)} %fusion.13, bf16[1024,16384]{1,0:T(8,128)(2,1)} %param.7), kind=kLoop, calls=%fused_computation.7 | loop fusion | flops 67108864 | bytes 167772160
  85.4 44.1 %copy.17 = f32[128,8,128,128]{3,2,1,0:T(8,128)} copy(f32[128,8,128,128]{3,1,2,0:T(8,128)} %abs_bitcast_fusion) | data formatting | bytes 134217728
  129.4 20.7 %bitcast_reduce_fusion = f32[8,128]{1,0:T(8,128)S(1)} fusion(f32[8,128,128,128]{3,2,1,0:T(8,128)} %bitcast.57), kind=kLoop, calls=%fused_computation.6 | loop fusion | flops 16776192 | bytes 67112960 | tf_op jit(solution)/shard_map/reduce_max | solution.py:35
  150.2 0.1 reshape.152
  150.3 0.7 reshape.154
  150.9 4.2 all-to-all-start.2
  155.2 6.4 copy.12
  161.5 3.8 fusion.7
  165.3 5.8 fusion.9
  171.2 5.3 all-to-all-start
  176.5 21.1 %div.54 = f32[8,128,128,128]{3,2,1,0:T(8,128)} broadcast(bf16[8,128]{1,0:T(8,128)(2,1)S(1)} %exponential_convert_fusion), dimensions={0,2} | broadcast | bytes 67110912 | tf_op jit(solution)/shard_map/div | solution.py:38
  197.6 73.8 %fusion.3 = bf16[1024,16384]{1,0:T(8,128)(2,1)} fusion(f32[128,8,128,128]{3,2,1,0:T(8,128)} %bitcast.13, f32[1024,16384]{1,0:T(8,128)} %fusion.13, bf16[1024,16384]{1,0:T(8,128)(2,1)} %param.7), kind=kLoop, calls=%fused_computation.5 | loop fusion | flops 117440512 | bytes 201326592 | tf_op jit(solution)/shard_map/convert_element_type | solution.py:38
  271.4 22.9 %copy.33 = bf16[128,4,8,4096]{3,2,0,1:T(8,128)(2,1)} copy(bf16[128,4,8,4096]{3,2,1,0:T(8,128)(2,1)} %bitcast.59) | data formatting | bytes 67108864 | tf_op jit(solution)/shard_map/all_to_all | solution.py:95
  294.3 9.9 %all-to-all-start.1 = ((bf16[1024,4,4096]{2,0,1:T(8,128)(2,1)}), bf16[1024,4,4096]{2,0,1:T(8,128)(2,1)}, u32[]{:S(2)}, u32[]{:S(2)}) async-start(bf16[1024,4,4096]{2,0,1:T(8,128)(2,1)} %bitcast.58), calls=%async_computation.1 | async-start | bytes 67108864 | tf_op jit(solution)/shard_map/all_to_all | solution.py:95
  304.2 0.0 reduce-scatter.2.cloned.1.call-start
  304.3 0.1 reshape.155
  304.4 6.4 copy.13
  310.8 356.3 %all-to-all-done.1 = bf16[1024,4,4096]{2,0,1:T(8,128)(2,1)} async-done(((bf16[1024,4,4096]{2,0,1:T(8,128)(2,1)}), bf16[1024,4,4096]{2,0,1:T(8,128)(2,1)}, u32[]{:S(2)}, u32[]{:S(2)}) %all-to-all-start.1) | async-done | bytes 33554464 | tf_op jit(solution)/shard_map/all_to_all | solution.py:95
  667.0 32.4 %convert_element_type.108 = f32[1024,4,4096]{2,0,1:T(8,128)} convert(bf16[1024,4,4096]{2,0,1:T(8,128)(2,1)} %all-to-all-done.1) | non-fusion elementwise | flops 16777216 | bytes 100663296 | tf_op jit(solution)/shard_map/convert_element_type | solution.py:46
  699.5 43.9 %copy.19 = f32[512,8,32,128]{3,2,1,0:T(8,128)} copy(f32[512,8,32,128]{3,1,2,0:T(8,128)} %bitcast.16) | data formatting | bytes 134217728
  743.3 32.8 %fusion = bf16[32,128,32,128]{3,2,1,0:T(8,128)(2,1)} fusion(f32[32,32]{1,0:T(8,128)S(1)} %convert_bitcast_fusion.1, f32[32,128,32,128]{3,2,1,0:T(8,128)} %bitcast.56), kind=kLoop, calls=%fused_computation.1 | loop fusion | flops 33554432 | bytes 100667392 | tf_op jit(solution)/shard_map/convert_element_type | solution.py:51
  776.2 23.9 %fusion.10 = bf16[512,4096]{1,0:T(8,128)(2,1)} fusion(bf16[512,4096]{1,0:T(8,128)(2,1)} %bitcast.64, bf16[512,8,32,128]{3,2,1,0:T(8,128)(2,1)} %bitcast.60), kind=kOutput, calls=%fused_computation.18 | convolution fusion | flops 17181966336 | bytes 41943040 | tf_op jit(solution)/shard_map/dot_general | solution.py:101
  800.1 0.0 reduce-scatter.2.cloned.1.call-update
  800.1 0.3 multiply_cosine_fusion
  800.5 77.1 %reduce-scatter.2.cloned.1.call-done = bf16[128,4096]{1,0:T(8,128)(2,1)} async-done(((bf16[512,4096]{1,0:T(8,128)(2,1)}), bf16[128,4096]{1,0:T(8,128)(2,1)}) %reduce-scatter.2.cloned.1.call-update) | async-done | bytes 1048592 | tf_op jit(solution)/shard_map/reduce_scatter | solution.py:100
  877.5 1.4 convert_bitcast_fusion
  878.9 0.4 copy.21
  879.3 0.8 subtract_convert_fusion
  880.1 0.6 pad_maximum_fusion
  880.7 1.4 copy.34
  (16 shorter events, 0.1 us)
Async XLA Ops:
  6.5 1.2 copy-start
  129.4 35.9 %copy-start.2 = (bf16[16384]{0:T(1024)(128)(2,1)S(1)}, bf16[16384]{0:T(1024)(128)(2,1)}, u32[]{:S(2)}) copy-start(bf16[16384]{0:T(1024)(128)(2,1)} %param.10) | copy-start | bytes 98308
  150.9 20.2 %all-to-all-start.2 = ((bf16[4,2,128]{2,1,0:T(2,128)(2,1)}), bf16[4,2,128]{2,1,0:T(2,128)(2,1)S(1)}, u32[]{:S(2)}, u32[]{:S(2)}) async-start(bf16[4,2,128]{2,1,0:T(2,128)(2,1)} %reshape.154), calls=%async_computation.2 | async-start | bytes 4096 | tf_op jit(solution)/shard_map/all_to_all | solution.py:96
  171.2 123.1 %all-to-all-start = ((bf16[128,4,4096]{0,2,1:T(8,128)(2,1)}), bf16[128,4,4096]{0,2,1:T(8,128)(2,1)}, u32[]{:S(2)}, u32[]{:S(2)}) async-start(bf16[128,4,4096]{0,2,1:T(8,128)(2,1)} %bitcast.62), calls=%async_computation | async-start | bytes 8388608 | tf_op jit(solution)/shard_map/all_to_all | solution.py:99
  294.3 372.7 %all-to-all-start.1 = ((bf16[1024,4,4096]{2,0,1:T(8,128)(2,1)}), bf16[1024,4,4096]{2,0,1:T(8,128)(2,1)}, u32[]{:S(2)}, u32[]{:S(2)}) async-start(bf16[1024,4,4096]{2,0,1:T(8,128)(2,1)} %bitcast.58), calls=%async_computation.1 | async-start | bytes 67108864 | tf_op jit(solution)/shard_map/all_to_all | solution.py:95
  304.2 573.3 %reduce-scatter.2.cloned.1.call-start = ((), (), s32[]{:S(2)}) async-start(), calls=%async_computation.4 | async-start | bytes 5242880 | tf_op jit(solution)/shard_map/reduce_scatter | solution.py:100
  776.1 23.9 %copy-start.3 = (s32[128]{0:T(128)S(1)}, s32[128]{0:T(128)}, u32[]{:S(2)}) copy-start(s32[128]{0:T(128)} %param.11) | copy-start | bytes 1540
  776.2 106.0 %copy-start.1 = (bf16[32,16384]{1,0:T(8,128)(2,1)S(1)}, bf16[32,16384]{1,0:T(8,128)(2,1)}, u32[]{:S(2)}) copy-start(bf16[32,16384]{1,0:T(8,128)(2,1)} %param.9) | copy-start | bytes 3145732
Sparse Core Ops, SparseCore 0:
  800.2 77.2 reduce-scatter.1
where the time goes:
time: 890 us; the launch traced here: 889 us
  waiting for transfers between devices  433 us (49%)
  other arithmetic  225 us (25%)
  local copies, waits for them, and re-layouts  149 us (17%)
  matrix products  48.7 us (5%)
  starting transfers between devices  19.5 us (2%)
  between operations  13.5 us (2%)
    all_to_all x1, waiting for transfers between devices, shards(): lax.all_to_all(quantized, 'tp', split_axis=1, concat_axis=0, tiled=True)  356 us
    unnamed x15, local copies, waits for them, and re-layouts  98.1 us
    reduce_scatter x1, waiting for transfers between devices, shards(): lax.psum_scatter(jnp.dot(gathered, weight, preferred_element_type=jnp.flo...  77.1 us
    convert_element_type x1, other arithmetic, quantize(): jnp.floor(tiles / scales.astype(jnp.float32)[:, None, :, None] + 0.5)  73.8 us
    unnamed x2, other arithmetic  54.2 us
    convert_element_type x1, other arithmetic, dequantize(): return (tiles * scales.astype(jnp.float32)[:, None, :, None]).astype(jnp....  32.8 us
    convert_element_type x1, other arithmetic, dequantize(): quantized.reshape(row_count // BLOCK, BLOCK, col_count // BLOCK, BLOCK)  32.4 us
    dot_general x1, matrix products, shards(): jnp.dot(adapter_down, adapter_up, preferred_element_type=jnp.float32)  24.8 us
  transfers between devices with their start and end apart: 4, of which 2 were waited for; matrix products, arithmetic and copies ran while one was open for 16% of the time, Pallas kernels for 0%

commit v1 on v0

v1 whole, which is shorter than its diff:
```python
import functools
import math

import jax
import jax.numpy as jnp
from jax import lax
from jax.experimental import pallas as pl
from jax.experimental.pallas import tpu as pltpu
from jax.sharding import PartitionSpec as P

HEAD = 128
BLOCK = 128
CHUNKS = 4


norm_epsilon = 1e-05
scale_epsilon = 1e-06
code_limit = 15.0
adapter_scale = 2.0
rope_theta = 500000.0
rope_factor = 8.0
low_factor = 1.0
high_factor = 4.0
initial_context = 8192.0
feature_scale = 1024.0

VMEM_LIMIT = 48 << 20
ANY = pl.BlockSpec(memory_space=pl.ANY)


def params():
    return pltpu.CompilerParams(vmem_limit_bytes=VMEM_LIMIT)


def cost(flops, nbytes):
    return pl.CostEstimate(flops=int(flops), bytes_accessed=int(nbytes), transcendentals=0)


def like(shape, dtype=jnp.bfloat16):
    return jax.ShapeDtypeStruct(shape, dtype)


def frequencies(positions):
    pair_index = jnp.arange(HEAD // 2, dtype=jnp.float32)
    inverse = jnp.exp(pair_index * (-2.0 * math.log(rope_theta) / HEAD))
    wavelength = 2.0 * math.pi / inverse
    blend = (initial_context / wavelength - low_factor) / (high_factor - low_factor)
    middle = (1.0 - blend) * inverse / rope_factor + blend * inverse
    adjusted = jnp.where(
        wavelength < initial_context / high_factor,
        inverse,
        jnp.where(wavelength > initial_context / low_factor, inverse / rope_factor, middle),
    )
    angles = positions.astype(jnp.float32)[:, None] * adjusted[None, :]
    return (jnp.cos(angles), jnp.sin(angles))


def turn_tables(hidden, positions):
    values = hidden.astype(jnp.float32)
    mean_square = jnp.mean(values * values, axis=1, keepdims=True)
    factor = lax.rsqrt(mean_square + norm_epsilon) * (1.0 / feature_scale)
    cosine, sine_part = frequencies(positions)
    return (
        jnp.concatenate([cosine, cosine], axis=1) * factor,
        jnp.concatenate([-sine_part, sine_part], axis=1) * factor,
    )


def pick_kernel(table, *refs):
    count = len(refs) // 3
    for i in range(count):
        values, gain, out = refs[i], refs[count + i], refs[2 * count + i]
        scaled = values[...].astype(jnp.float32) * (gain[...].astype(jnp.float32) * feature_scale)
        out[...] = scaled.astype(jnp.bfloat16)


def pick(hidden, norm_gain, table, count, width):
    tokens = hidden.shape[0]

    def spec(rows, i):
        return pl.BlockSpec((rows, width), lambda step, table: (0, table[i]))

    return pl.pallas_call(
        pick_kernel,
        grid_spec=pltpu.PrefetchScalarGridSpec(
            num_scalar_prefetch=1,
            grid=(1,),
            in_specs=[spec(tokens, i) for i in range(count)] + [spec(1, i) for i in range(count)],
            out_specs=[pl.BlockSpec((tokens, width), lambda step, table: (0, 0))] * count,
        ),
        out_shape=[like((tokens, width))] * count,
        compiler_params=params(),
        name="pick_features",
    )(table, *([hidden] * count), *([norm_gain] * count))


def scales_of(largest):
    ratio = (largest + scale_epsilon) / code_limit
    scale = jnp.exp2(jnp.ceil(jnp.log2(ratio))).astype(jnp.bfloat16).astype(jnp.float32)
    scale = jnp.where(ratio > scale, scale * 2.0, scale)
    return jnp.where(ratio <= scale * 0.5, scale * 0.5, scale)


def quantize_tile(base, down, up, weight, merged, scale_scratch):
    rows, width = base.shape
    row_blocks = rows // BLOCK
    tops = []
    for i in range(row_blocks):
        block_rows = pl.ds(i * BLOCK, BLOCK)
        low_rank = jnp.dot(down[block_rows, :], up[...], preferred_element_type=jnp.float32)
        total = base[block_rows, :].astype(jnp.float32) + low_rank
        merged[block_rows, :] = total
        tops.append(jnp.max(jnp.abs(total), axis=0, keepdims=True))
    top = jnp.concatenate(tops, axis=0)
    for j in range(width // BLOCK):
        cols = slice(j * BLOCK, (j + 1) * BLOCK)
        largest = jnp.max(top[:, cols], axis=1, keepdims=True)
        scale = scales_of(jnp.broadcast_to(largest, (row_blocks, BLOCK)))
        scale_scratch[0, :, cols] = scale
        scale_scratch[1, :, cols] = 1.0 / scale
    for i in range(row_blocks):
        block_rows = pl.ds(i * BLOCK, BLOCK)
        scale = scale_scratch[0, pl.ds(i, 1), :]
        inverse = scale_scratch[1, pl.ds(i, 1), :]
        codes = jnp.floor(merged[block_rows, :] * inverse + 0.5)
        weight[block_rows, :] = codes.astype(jnp.bfloat16) * scale.astype(jnp.bfloat16)


def store_pieces(product, steps_each, parts, outs):
    groups = len(outs) // parts
    tokens = product.shape[0] // parts
    for group in range(groups):

        @pl.when(pl.program_id(0) // steps_each == group)
        def _():
            for i in range(parts):
                outs[group * parts + i][...] = product[i * tokens : (i + 1) * tokens, :]


def piece_specs(tokens, width, steps_each, parts, groups):
    def spec(group):
        first = group * steps_each
        return pl.BlockSpec(
            (tokens // parts, width),
            lambda i, *_: (0, jnp.clip(i - first, 0, steps_each - 1)),
        )

    shape = like((tokens // parts, steps_each * width))
    specs = [spec(group) for group in range(groups) for _ in range(parts)]
    return specs, [shape] * (parts * groups)


def quantize_kernel(steps_each, with_received, table, base, down, up, x, *refs):
    received = refs[0] if with_received else None
    merged, scale_scratch = refs[-2:]
    groups = pl.num_programs(0) // steps_each
    weight, outs = refs[-3 - groups], refs[-2 - groups : -2]
    quantize_tile(base, down, up, weight, merged, scale_scratch)
    product = jnp.dot(x[...], weight[...], preferred_element_type=jnp.float32)
    if with_received:
        product = product + received[...].astype(jnp.float32)
    store_pieces(product.astype(jnp.bfloat16), steps_each, 1, outs)


def quantize_and_project(
    base, down, up, x, table, steps, width, groups=1, received=None, after=()
):
    rows, rank = down.shape
    tokens = x.shape[0]

    def fixed(shape):
        return pl.BlockSpec(shape, lambda i, table: (0, 0))

    def picked(height):
        return pl.BlockSpec((height, width), lambda i, table: (0, table[i]))

    def in_order(height):
        return pl.BlockSpec((height, width), lambda i, table: (0, i))

    in_specs = [picked(rows), fixed((rows, rank)), picked(rank), fixed((tokens, rows))]
    operands = [base, down, up, x]
    if received is not None:
        in_specs.append(in_order(tokens))
        operands.append(received)
    in_specs += [ANY] * len(after)
    operands += after
    piece_blocks, piece_shapes = piece_specs(tokens, width, steps // groups, 1, groups)
    return pl.pallas_call(
        functools.partial(quantize_kernel, steps // groups, received is not None),
        grid_spec=pltpu.PrefetchScalarGridSpec(
            num_scalar_prefetch=1,
            grid=(steps,),
            in_specs=in_specs,
            out_specs=[in_order(rows), *piece_blocks],
            scratch_shapes=[
                pltpu.VMEM((rows, width), jnp.float32),
                pltpu.VMEM((2, rows // BLOCK, width), jnp.float32),
            ],
        ),
        out_shape=[like((rows, steps * width)), *piece_shapes],
        cost_estimate=cost(2 * tokens * rows * steps * width * 4, 4 * rows * steps * width),
        compiler_params=params(),
        name="quantize_and_project",
    )(table, *operands)


def project_kernel(steps_each, parts, groups, with_received, x, weight, *refs):
    received = refs[0] if with_received else None
    product = jnp.dot(x[...], weight[...], preferred_element_type=jnp.float32)
    if with_received:
        product = product + received[...].astype(jnp.float32)
    store_pieces(product.astype(jnp.bfloat16), steps_each, parts, refs[-parts * groups :])


def project(x, weight, steps, parts=1, groups=1, received=None, after=()):
    tokens, rows = x.shape
    width = weight.shape[1] // steps
    in_specs = [
        pl.BlockSpec((tokens, rows), lambda i: (0, 0)),
        pl.BlockSpec((rows, width), lambda i: (0, i)),
    ]
    operands = [x, weight]
    if received is not None:
        in_specs.append(pl.BlockSpec((tokens, width), lambda i: (0, i)))
        operands.append(received)
    in_specs += [ANY] * len(after)
    operands += after
    piece_blocks, piece_shapes = piece_specs(tokens, width, steps // groups, parts, groups)
    return pl.pallas_call(
        functools.partial(project_kernel, steps // groups, parts, groups, received is not None),
        grid=(steps,),
        in_specs=in_specs,
        out_specs=piece_blocks,
        out_shape=piece_shapes,
        cost_estimate=cost(2 * tokens * rows * steps * width, 2 * rows * steps * width),
        compiler_params=params(),
        name="project",
    )(*operands)


def turn_kernel(count, cosine, sine_part, *refs):
    out = refs[-1]
    for j in range(out.shape[1] // HEAD):
        cols = slice(j * HEAD, (j + 1) * HEAD)
        total = refs[0][:, cols].astype(jnp.float32)
        for term in refs[1:count]:
            total = total + term[:, cols].astype(jnp.float32)
        swapped = pltpu.roll(total, HEAD // 2, 1)
        turned = total * cosine[...] + swapped * sine_part[...]
        out[:, cols] = turned.astype(jnp.bfloat16)


def turn(cosine, sine_part, terms, place, places, into):
    tokens, width = terms[0].shape
    whole = pl.BlockSpec((tokens, width), lambda i: (0, 0))
    table = pl.BlockSpec((tokens, HEAD), lambda i: (0, 0))
    extra = [] if into is None else [into]
    count = len(terms)
    return pl.pallas_call(
        functools.partial(turn_kernel, count),
        grid=(1,),
        in_specs=[table] * 2 + [whole] * count + [ANY] * len(extra),
        out_specs=pl.BlockSpec((tokens, width), lambda i: (0, place)),
        out_shape=like((tokens, places * width)),
        input_output_aliases={2 + count: 0} if extra else {},
        compiler_params=params(),
        name="turn",
    )(cosine, sine_part, *terms, *extra)


def added(*terms):
    total = terms[0].astype(jnp.float32)
    for term in terms[1:]:
        total = total + term.astype(jnp.float32)
    return total.astype(jnp.bfloat16)


def tile_width(columns):
    width = min(columns, 1024)
    while columns % width:
        width //= 2
    return width


def line_shards(hidden, base, down, up, norm_gain, positions):
    tp = lax.axis_index("tp")
    z = lax.axis_index("fsdp")
    rows, all_columns = base.shape
    tokens = hidden.shape[0]
    quarter = all_columns // 4
    piece = quarter // CHUNKS
    width = tile_width(piece)
    half = piece // width

    blocks = jnp.stack([((z + d) % 4) * 4 + tp for d in range(4)]).astype(jnp.int32)
    own_x, *others = pick(hidden, norm_gain[None, :], blocks, 4, rows)
    x1, x2, x3 = [
        lax.ppermute(others[d - 1], "fsdp", [(i, (i + d) % 4) for i in range(4)]) for d in (1, 2, 3)
    ]
    low = z < 2
    rest_x = jnp.concatenate([jnp.where(low, x1, x3), x2, jnp.where(low, x3, x1)], axis=0)
    up2 = up * jnp.bfloat16(adapter_scale)
    cosine, sine_part = turn_tables(hidden, positions)

    def tiles(owners, chunk):
        offsets = jnp.arange(half, dtype=jnp.int32) + chunk * half
        tiles_of = quarter // width
        return jnp.concatenate([owner * tiles_of + offsets for owner in owners]).astype(jnp.int32)

    other_core, other_chip, other_both = tp ^ 1, tp ^ 2, tp ^ 3
    over_core = functools.partial(lax.ppermute, axis_name="tp", perm=[(i, i ^ 1) for i in range(4)])
    over_y = functools.partial(lax.ppermute, axis_name="tp", perm=[(i, i ^ 2) for i in range(4)])

    def over_z(values, pairs):
        return lax.ppermute(values, "fsdp", pairs)

    state = {"last": ()}
    own = {}
    rest = {}

    def do_own(chunk):
        weight_a, for_core = quantize_and_project(
            base, down, up2, own_x, tiles((other_both, other_core), chunk), 2 * half, width,
            after=state["last"],
        )
        weight_b, to_send, kept = quantize_and_project(
            base, down, up2, own_x, tiles((other_chip, tp), chunk), 2 * half, width, groups=2,
            received=over_core(for_core),
        )
        state["last"] = (kept,)
        own[chunk] = (weight_a, weight_b, kept, over_y(to_send))

    def do_rest(chunk):
        weight_a, weight_b, _, _ = own[chunk]
        (for_core,) = project(rest_x, weight_a, 2 * half, after=state["last"])
        received = over_core(for_core)
        outs = project(rest_x, weight_b, 2 * half, parts=3, groups=2, received=received)
        state["last"] = (outs[-1],)
        rest[chunk] = (outs[3:], [over_y(value) for value in outs[:3]])

    for chunk in range(2):
        do_own(chunk)
    for chunk in range(2):
        do_rest(chunk)
    for chunk in range(2, CHUNKS):
        do_own(chunk)
        do_rest(chunk)

    out = None
    for chunk in range(CHUNKS):
        (a, b, c), (ya, yb, yc) = rest[chunk]
        first = over_z(added(a, ya), [(0, 1), (3, 2)])
        second = added(b, yb, first)
        right = over_z(second, [(0, 1), (1, 2)])
        left = over_z(second, [(3, 2), (2, 1)])
        far, near = (a, ya), (c, yc)
        to_right = added(*[jnp.where(low, n, f) for f, n in zip(far, near)], right)
        to_left = added(*[jnp.where(low, f, n) for f, n in zip(far, near)], left)
        right = over_z(to_right, [(0, 1), (1, 2), (2, 3)])
        left = over_z(to_left, [(3, 2), (2, 1), (1, 0)])
        _, _, kept, y_kept = own[chunk]
        out = turn(cosine, sine_part, (kept, y_kept, right, left), chunk, CHUNKS, out)
    return out


def any_shards(fsdp, tp_size, hidden, base, down, up, norm_gain, positions):
    tp = lax.axis_index("tp")
    rows, all_columns = base.shape
    tokens = hidden.shape[0]
    share = all_columns // tp_size
    chunks = max(1, share // 256)
    piece = share // chunks
    width = tile_width(piece)
    steps = piece // width

    blocks = (jnp.arange(fsdp) * tp_size + tp).astype(jnp.int32)
    picked = pick(hidden, norm_gain[None, :], blocks, fsdp, rows)
    x = lax.all_to_all(jnp.stack(picked), "fsdp", 0, 0, tiled=True)
    x = x.reshape(fsdp * tokens, rows)
    up2 = up * jnp.bfloat16(adapter_scale)
    cosine, sine_part = turn_tables(hidden, positions)
    out = None
    after = ()
    for chunk in range(chunks):
        owners = jnp.arange(tp_size, dtype=jnp.int32)[:, None] * (share // width)
        offsets = jnp.arange(steps, dtype=jnp.int32)[None, :] + chunk * steps
        _, *parts = quantize_and_project(
            base, down, up2, x, (owners + offsets).reshape(-1), tp_size * steps, width,
            groups=tp_size, after=after,
        )
        mine = lax.psum_scatter(jnp.stack(parts), "tp", scatter_dimension=0, tiled=True)[0]
        mine = lax.psum_scatter(mine, "fsdp", scatter_dimension=0, tiled=True)
        out = turn(cosine, sine_part, (mine,), chunk, chunks, out)
        after = (mine,)
    return out


def solution(mesh):
    fsdp, tp = mesh.shape["fsdp"], mesh.shape["tp"]
    if (fsdp, tp) == (4, 4):
        shards = line_shards
    else:
        shards = functools.partial(any_shards, fsdp, tp)
    placed = (
        P(("rep", "fsdp"), None),
        P(("rep", "fsdp", "tp"), None),
        P(("rep", "fsdp", "tp"), None),
        P("rep", None),
        P("rep"),
        P(("rep", "fsdp")),
    )
    return jax.shard_map(
        shards, mesh=mesh, in_specs=placed, out_specs=P(("rep", "fsdp"), "tp"), check_vma=False
    )
```

time: 890 us -> 237 us (0.27)
  waiting for transfers between devices: 433 us -> 58.2 us
  other arithmetic: 225 us -> 9.01 us
  local copies, waits for them, and re-layouts: 149 us -> 4 us
  Pallas kernels: 0 us -> 91.9 us
  starting transfers between devices: 19.5 us -> 72.4 us
  matrix products: 48.7 us -> 0 us
  between operations: 13.5 us -> 0.52 us
    all_to_all x3 -> x0, waiting for transfers between devices: 356 us -> none  [the longest x1 356 us: shards(): lax.all_to_all(quantized, 'tp', split_axis=1, concat_axis=0, tiled=True)]
    convert_element_type x7 -> x12, other arithmetic: 145 us -> 3.62 us  [added(): return total.astype(jnp.bfloat16)]
    unnamed x15 -> x7, local copies, waits for them, and re-layouts: 98.1 us -> 3.21 us
    pallas_call x0 -> x21, Pallas kernels: none -> 91.9 us  [the longest x8 56.2 us: quantize_and_project(): pl.pallas_call(functools.partial(quantize_kernel, steps // groups, receiv...]
    reduce_scatter x1 -> x0, waiting for transfers between devices: 77.1 us -> none  [shards(): lax.psum_scatter(jnp.dot(gathered, weight, preferred_element_type=jnp.flo...]
    ppermute x0 -> x47, starting transfers between devices: none -> 72.4 us  [the longest x20 45.9 us: over_z(): return lax.ppermute(values, 'fsdp', pairs)]
    ppermute x0 -> x47, waiting for transfers between devices: none -> 58.2 us  [the longest x12 29.9 us: do_rest(): rest[chunk] = (outs[3:], [over_y(value) for value in outs[:3]])]
    unnamed x2 -> x0, other arithmetic: 54.2 us -> none
  transfers between devices with their start and end apart: 4 -> 47, of which waited for: 2 -> 17; matrix products, arithmetic and copies ran while one was open for 16% -> 3% of each run, Pallas kernels for 0% -> 13%
where the time goes in v1:
time: 237 us; the launch traced here: 236 us
  Pallas kernels  91.9 us (39%)
  starting transfers between devices  72.4 us (31%)
  waiting for transfers between devices  58.2 us (25%)
  other arithmetic  9.01 us (4%)
  local copies, waits for them, and re-layouts  4 us (2%)
    pallas_call x8, Pallas kernels, quantize_and_project(): pl.pallas_call(functools.partial(quantize_kernel, steps // groups, receiv...  56.2 us
    ppermute x20, starting transfers between devices, over_z(): return lax.ppermute(values, 'fsdp', pairs)  45.9 us
    pallas_call x8, Pallas kernels, project(): pl.pallas_call(functools.partial(project_kernel, steps // groups, parts,...  30.5 us
    ppermute x12, waiting for transfers between devices, do_rest(): rest[chunk] = (outs[3:], [over_y(value) for value in outs[:3]])  29.9 us
    ppermute x12, starting transfers between devices, do_rest(): rest[chunk] = (outs[3:], [over_y(value) for value in outs[:3]])  13.7 us
    ppermute x3, waiting for transfers between devices, line_shards(): lax.ppermute(others[d - 1], 'fsdp', [(i, (i + d) % 4) for i in range(4)])  12.6 us
    ppermute x4, waiting for transfers between devices, do_rest(): received = over_core(for_core)  9.73 us
    ppermute x4, starting transfers between devices, do_own(): own[chunk] = (weight_a, weight_b, kept, over_y(to_send))  5.76 us
  transfers between devices with their start and end apart: 47, of which 17 were waited for; matrix products, arithmetic and copies ran while one was open for 3% of the time, Pallas kernels for 13%

profile of v1, /device:TPU:0, one launch (start us, length us, event | category | flops | bytes accessed | tf_op | source)
XLA Modules:
  0.0 236.1 jit_solution(18144395978101472561)
XLA Ops:
  6.8 7.0 %quantize_and_project.8 = (bf16[1024,2048]{1,0:T(8,128)(2,1)}, bf16[128,2048]{1,0:T(8,128)(2,1)S(1)}) custom-call(s32[2]{0:T(128)S(1)} %pad_add_fusion.8.table, bf16[1024,16384]{1,0:T(8,128)(2,1)} %base.15, bf16[1024,32]{1,0:T(8,128)(2,1)S(1)} %copy.17.down, bf16[32,16384]{1,0:T(8,128)(2,1)S(1)} %broadcast_multiply_fusion.up, ...), custom_call_target="tpu_custom_call" | custom-call | flops 2147483648 | bytes 8388608 | tf_op jit(solution)/shard_map/quantize_and_project/pallas_call | solution.py:188
  19.3 7.0 %quantize_and_project.9 = (bf16[1024,2048]{1,0:T(8,128)(2,1)}, bf16[128,1024]{1,0:T(8,128)(2,1)S(1)}, bf16[128,1024]{1,0:T(8,128)(2,1)S(1)}) custom-call(s32[2]{0:T(128)S(1)} %pad_add_fusion.7.table, bf16[1024,16384]{1,0:T(8,128)(2,1)} %base.15, bf16[1024,32]{1,0:T(8,128)(2,1)S(1)} %copy.17.down, bf16[32,16384]{1,0:T(8,128)(2,1)S(1)} %broadcast_multiply_fusion.up, ...), custom_call_target="tpu_custom_call" | custom-call | flops 2147483648 | bytes 8388608 | tf_op jit(solution)/shard_map/quantize_and_project/pallas_call | solution.py:188
  26.3 7.0 %quantize_and_project.10 = (bf16[1024,2048]{1,0:T(8,128)(2,1)}, bf16[128,2048]{1,0:T(8,128)(2,1)S(1)}) custom-call(s32[2]{0:T(128)S(1)} %pad_add_fusion.6.table, bf16[1024,16384]{1,0:T(8,128)(2,1)} %base.15, bf16[1024,32]{1,0:T(8,128)(2,1)S(1)} %copy.17.down, bf16[32,16384]{1,0:T(8,128)(2,1)S(1)} %broadcast_multiply_fusion.up, ...), custom_call_target="tpu_custom_call" | custom-call | flops 2147483648 | bytes 8388608 | tf_op jit(solution)/shard_map/quantize_and_project/pallas_call | solution.py:188
  35.3 12.6 %collective-permute-done.2 = bf16[128,1024]{1,0:T(8,128)(2,1)} collective-permute-done((bf16[128,1024]{1,0:T(8,128)(2,1)S(1)}, bf16[128,1024]{1,0:T(8,128)(2,1)}, u32[]{:S(2)}, u32[]{:S(2)}) %collective-permute-start.2) | collective-permute-done | bytes 262176 | tf_op jit(solution)/shard_map/ppermute | solution.py:298
  48.9 7.0 %quantize_and_project.11 = (bf16[1024,2048]{1,0:T(8,128)(2,1)}, bf16[128,1024]{1,0:T(8,128)(2,1)S(1)}, bf16[128,1024]{1,0:T(8,128)(2,1)S(1)}) custom-call(s32[2]{0:T(128)S(1)} %pad_add_fusion.5.table, bf16[1024,16384]{1,0:T(8,128)(2,1)} %base.15, bf16[1024,32]{1,0:T(8,128)(2,1)S(1)} %copy.17.down, bf16[32,16384]{1,0:T(8,128)(2,1)S(1)} %broadcast_multiply_fusion.up, ...), custom_call_target="tpu_custom_call" | custom-call | flops 2147483648 | bytes 8388608 | tf_op jit(solution)/shard_map/quantize_and_project/pallas_call | solution.py:188
  55.9 3.8 %project.8 = bf16[384,2048]{1,0:T(8,128)(2,1)S(1)} custom-call(bf16[384,1024]{1,0:T(8,128)(2,1)S(1)} %pad_maximum_fusion.x, bf16[1024,2048]{1,0:T(8,128)(2,1)} %get-tuple-element.63.weight, bf16[128,1024]{1,0:T(8,128)(2,1)S(1)} %get-tuple-element.64.refs_0_), custom_call_target="tpu_custom_call" | custom-call | flops 1610612736 | bytes 4194304 | tf_op jit(solution)/shard_map/project/pallas_call | solution.py:229
  59.9 3.3 %collective-permute-done.5.refs_0_ = bf16[384,2048]{1,0:T(8,128)(2,1)S(1)} collective-permute-done((bf16[384,2048]{1,0:T(8,128)(2,1)S(1)}, bf16[384,2048]{1,0:T(8,128)(2,1)S(1)}, u32[]{:S(2)}, u32[]{:S(2)}) %collective-permute-start.5) | collective-permute-done | bytes 1572896 | tf_op jit(solution)/shard_map/ppermute | solution.py:336
  63.2 3.7 %project.9 = (bf16[128,1024]{1,0:T(8,128)(2,1)S(1)}, bf16[128,1024]{1,0:T(8,128)(2,1)S(1)}, bf16[128,1024]{1,0:T(8,128)(2,1)S(1)}, bf16[128,1024]{1,0:T(8,128)(2...) custom-call(bf16[384,1024]{1,0:T(8,128)(2,1)S(1)} %pad_maximum_fusion.x, ...), custom_call_target="tpu_custom_call" | custom-call | flops 1610612736 | bytes 4194304 | tf_op jit(solution)/shard_map/project/pallas_call | solution.py:229
  67.0 3.9 %project.10 = bf16[384,2048]{1,0:T(8,128)(2,1)S(1)} custom-call(bf16[384,1024]{1,0:T(8,128)(2,1)S(1)} %pad_maximum_fusion.x, bf16[1024,2048]{1,0:T(8,128)(2,1)} %get-tuple-element.61.weight, bf16[128,1024]{1,0:T(8,128)(2,1)S(1)} %get-tuple-element.65.refs_0_), custom_call_target="tpu_custom_call" | custom-call | flops 1610612736 | bytes 4194304 | tf_op jit(solution)/shard_map/project/pallas_call | solution.py:229
  71.1 3.2 %collective-permute-done.6.refs_0_ = bf16[384,2048]{1,0:T(8,128)(2,1)S(1)} collective-permute-done((bf16[384,2048]{1,0:T(8,128)(2,1)S(1)}, bf16[384,2048]{1,0:T(8,128)(2,1)S(1)}, u32[]{:S(2)}, u32[]{:S(2)}) %collective-permute-start.6) | collective-permute-done | bytes 1572896 | tf_op jit(solution)/shard_map/ppermute | solution.py:336
  74.3 3.7 %project.11 = (bf16[128,1024]{1,0:T(8,128)(2,1)S(1)}, bf16[128,1024]{1,0:T(8,128)(2,1)S(1)}, bf16[128,1024]{1,0:T(8,128)(2,1)S(1)}, bf16[128,1024]{1,0:T(8,128)(...) custom-call(bf16[384,1024]{1,0:T(8,128)(2,1)S(1)} %pad_maximum_fusion.x, ...), custom_call_target="tpu_custom_call" | custom-call | flops 1610612736 | bytes 4194304 | tf_op jit(solution)/shard_map/project/pallas_call | solution.py:229
  78.1 7.0 %quantize_and_project.12 = (bf16[1024,2048]{1,0:T(8,128)(2,1)}, bf16[128,2048]{1,0:T(8,128)(2,1)S(1)}) custom-call(s32[2]{0:T(128)S(1)} %pad_add_fusion.4.table, bf16[1024,16384]{1,0:T(8,128)(2,1)} %base.15, bf16[1024,32]{1,0:T(8,128)(2,1)S(1)} %copy.17.down, bf16[32,16384]{1,0:T(8,128)(2,1)S(1)} %broadcast_multiply_fusion.up, ...), custom_call_target="tpu_custom_call" | custom-call | flops 2147483648 | bytes 8388608 | tf_op jit(solution)/shard_map/quantize_and_project/pallas_call | solution.py:188
  87.0 7.0 %quantize_and_project.13 = (bf16[1024,2048]{1,0:T(8,128)(2,1)}, bf16[128,1024]{1,0:T(8,128)(2,1)S(1)}, bf16[128,1024]{1,0:T(8,128)(2,1)S(1)}) custom-call(s32[2]{0:T(128)S(1)} %pad_add_fusion.3.table, bf16[1024,16384]{1,0:T(8,128)(2,1)} %base.15, bf16[1024,32]{1,0:T(8,128)(2,1)S(1)} %copy.17.down, bf16[32,16384]{1,0:T(8,128)(2,1)S(1)} %broadcast_multiply_fusion.up, ...), custom_call_target="tpu_custom_call" | custom-call | flops 2147483648 | bytes 8388608 | tf_op jit(solution)/shard_map/quantize_and_project/pallas_call | solution.py:188
  94.0 3.8 %project.12 = bf16[384,2048]{1,0:T(8,128)(2,1)S(1)} custom-call(bf16[384,1024]{1,0:T(8,128)(2,1)S(1)} %pad_maximum_fusion.x, bf16[1024,2048]{1,0:T(8,128)(2,1)} %get-tuple-element.69.weight, bf16[128,1024]{1,0:T(8,128)(2,1)S(1)} %get-tuple-element.70.refs_0_), custom_call_target="tpu_custom_call" | custom-call | flops 1610612736 | bytes 4194304 | tf_op jit(solution)/shard_map/project/pallas_call | solution.py:229
  98.2 3.2 %collective-permute-done.8.refs_0_ = bf16[384,2048]{1,0:T(8,128)(2,1)S(1)} collective-permute-done((bf16[384,2048]{1,0:T(8,128)(2,1)S(1)}, bf16[384,2048]{1,0:T(8,128)(2,1)S(1)}, u32[]{:S(2)}, u32[]{:S(2)}) %collective-permute-start.8) | collective-permute-done | bytes 1572896 | tf_op jit(solution)/shard_map/ppermute | solution.py:336
  101.3 3.7 %project.13 = (bf16[128,1024]{1,0:T(8,128)(2,1)S(1)}, bf16[128,1024]{1,0:T(8,128)(2,1)S(1)}, bf16[128,1024]{1,0:T(8,128)(2,1)S(1)}, bf16[128,1024]{1,0:T(8,128)(...) custom-call(bf16[384,1024]{1,0:T(8,128)(2,1)S(1)} %pad_maximum_fusion.x, ...), custom_call_target="tpu_custom_call" | custom-call | flops 1610612736 | bytes 4194304 | tf_op jit(solution)/shard_map/project/pallas_call | solution.py:229
  105.1 7.0 %quantize_and_project.14 = (bf16[1024,2048]{1,0:T(8,128)(2,1)}, bf16[128,2048]{1,0:T(8,128)(2,1)S(1)}) custom-call(s32[2]{0:T(128)S(1)} %pad_add_fusion.2.table, bf16[1024,16384]{1,0:T(8,128)(2,1)} %base.15, bf16[1024,32]{1,0:T(8,128)(2,1)S(1)} %copy.17.down, bf16[32,16384]{1,0:T(8,128)(2,1)S(1)} %broadcast_multiply_fusion.up, ...), custom_call_target="tpu_custom_call" | custom-call | flops 2147483648 | bytes 8388608 | tf_op jit(solution)/shard_map/quantize_and_project/pallas_call | solution.py:188
  114.4 7.0 %collective-permute-done.40 = bf16[128,1024]{1,0:T(8,128)(2,1)S(1)} collective-permute-done((bf16[128,1024]{1,0:T(8,128)(2,1)S(1)}, bf16[128,1024]{1,0:T(8,128)(2,1)S(1)}, u32[]{:S(2)}, u32[]{:S(2)}) %collective-permute-start.40) | collective-permute-done | bytes 262176 | tf_op jit(solution)/shard_map/ppermute | solution.py:339
  124.4 7.0 %quantize_and_project.15 = (bf16[1024,2048]{1,0:T(8,128)(2,1)}, bf16[128,1024]{1,0:T(8,128)(2,1)S(1)}, bf16[128,1024]{1,0:T(8,128)(2,1)S(1)}) custom-call(s32[2]{0:T(128)S(1)} %pad_add_fusion.table, bf16[1024,16384]{1,0:T(8,128)(2,1)} %base.15, bf16[1024,32]{1,0:T(8,128)(2,1)S(1)} %copy.17.down, bf16[32,16384]{1,0:T(8,128)(2,1)S(1)} %broadcast_multiply_fusion.up, ...), custom_call_target="tpu_custom_call" | custom-call | flops 2147483648 | bytes 8388608 | tf_op jit(solution)/shard_map/quantize_and_project/pallas_call | solution.py:188
  131.4 4.0 %project.14 = bf16[384,2048]{1,0:T(8,128)(2,1)S(1)} custom-call(bf16[384,1024]{1,0:T(8,128)(2,1)S(1)} %pad_maximum_fusion.x, bf16[1024,2048]{1,0:T(8,128)(2,1)} %get-tuple-element.76.weight, bf16[128,1024]{1,0:T(8,128)(2,1)S(1)} %get-tuple-element.73.refs_0_), custom_call_target="tpu_custom_call" | custom-call | flops 1610612736 | bytes 4194304 | tf_op jit(solution)/shard_map/project/pallas_call | solution.py:229
  142.1 3.5 %collective-permute-done.39 = bf16[128,1024]{1,0:T(8,128)(2,1)S(1)} collective-permute-done((bf16[128,1024]{1,0:T(8,128)(2,1)S(1)}, bf16[128,1024]{1,0:T(8,128)(2,1)S(1)}, u32[]{:S(2)}, u32[]{:S(2)}) %collective-permute-start.39) | collective-permute-done | bytes 262176 | tf_op jit(solution)/shard_map/ppermute | solution.py:339
  151.2 3.4 %collective-permute-start.33 = (bf16[128,1024]{1,0:T(8,128)(2,1)S(1)}, bf16[128,1024]{1,0:T(8,128)(2,1)S(1)}, u32[]{:S(2)}, u32[]{:S(2)}) collective-permute-start(bf16[128,1024]{1,0:T(8,128)(2,1)S(1)} %add_convert_fusion.7), channel_id=1, source_target_pairs={{0,8},{24,16},{1,9},{25,17},{2,10},{26,18},{3,11},{27,19},{4,12},{... | collective-permute-start | bytes 786440 | tf_op jit(solution)/shard_map/ppermute | solution.py:315
  159.7 3.7 %project.15 = (bf16[128,1024]{1,0:T(8,128)(2,1)S(1)}, bf16[128,1024]{1,0:T(8,128)(2,1)S(1)}, bf16[128,1024]{1,0:T(8,128)(2,1)S(1)}, bf16[128,1024]{1,0:T(8,128)(...) custom-call(bf16[384,1024]{1,0:T(8,128)(2,1)S(1)} %pad_maximum_fusion.x, ...), custom_call_target="tpu_custom_call" | custom-call | flops 1610612736 | bytes 4194304 | tf_op jit(solution)/shard_map/project/pallas_call | solution.py:229
  166.0 7.6 %collective-permute-done.23 = bf16[128,1024]{1,0:T(8,128)(2,1)S(1)} collective-permute-done((bf16[128,1024]{1,0:T(8,128)(2,1)S(1)}, bf16[128,1024]{1,0:T(8,128)(2,1)S(1)}, u32[]{:S(2)}, u32[]{:S(2)}) %collective-permute-start.23) | collective-permute-done | bytes 262176 | tf_op jit(solution)/shard_map/ppermute | solution.py:339
  176.0 3.2 %collective-permute-done.13 = bf16[128,1024]{1,0:T(8,128)(2,1)S(1)} collective-permute-done((bf16[128,1024]{1,0:T(8,128)(2,1)S(1)}, bf16[128,1024]{1,0:T(8,128)(2,1)S(1)}, u32[]{:S(2)}, u32[]{:S(2)}) %collective-permute-start.13) | collective-permute-done | bytes 262176 | tf_op jit(solution)/shard_map/ppermute | solution.py:339
  182.9 4.7 %collective-permute-start.15 = (bf16[128,1024]{1,0:T(8,128)(2,1)S(1)}, bf16[128,1024]{1,0:T(8,128)(2,1)S(1)}, u32[]{:S(2)}, u32[]{:S(2)}) collective-permute-start(bf16[128,1024]{1,0:T(8,128)(2,1)S(1)} %add_convert_fusion.15), channel_id=1, source_target_pairs={{0,8},{24,16},{1,9},{25,17},{2,10},{26,18},{3,11},{27,19},{4,12},{... | collective-permute-start | bytes 786440 | tf_op jit(solution)/shard_map/ppermute | solution.py:315
  193.8 4.3 %collective-permute-start.16 = (bf16[128,1024]{1,0:T(8,128)(2,1)S(1)}, bf16[128,1024]{1,0:T(8,128)(2,1)S(1)}, u32[]{:S(2)}, u32[]{:S(2)}) collective-permute-start(bf16[128,1024]{1,0:T(8,128)(2,1)S(1)} %add_convert_fusion.14), channel_id=1, source_target_pairs={{0,8},{8,16},{1,9},{9,17},{2,10},{10,18},{3,11},{11,19},{4,12},{12... | collective-permute-start | bytes 786440 | tf_op jit(solution)/shard_map/ppermute | solution.py:315
  199.3 5.5 %collective-permute-start.44 = (bf16[128,1024]{1,0:T(8,128)(2,1)S(1)}, bf16[128,1024]{1,0:T(8,128)(2,1)S(1)}, u32[]{:S(2)}, u32[]{:S(2)}) collective-permute-start(bf16[128,1024]{1,0:T(8,128)(2,1)S(1)} %get-tuple-element.102), channel_id=1, source_target_pairs={{0,8},{8,16},{16,24},{1,9},{9,17},{17,25},{2,10},{10,18},{18,26},{... | collective-permute-start | bytes 786440 | tf_op jit(solution)/shard_map/ppermute | solution.py:315
  206.2 2.6 %collective-permute-done.12 = bf16[128,1024]{1,0:T(8,128)(2,1)S(1)} collective-permute-done((bf16[128,1024]{1,0:T(8,128)(2,1)S(1)}, bf16[128,1024]{1,0:T(8,128)(2,1)S(1)}, u32[]{:S(2)}, u32[]{:S(2)}) %collective-permute-start.12) | collective-permute-done | bytes 262176 | tf_op jit(solution)/shard_map/ppermute | solution.py:339
  215.1 5.9 %collective-permute-start.26 = (bf16[128,1024]{1,0:T(8,128)(2,1)S(1)}, bf16[128,1024]{1,0:T(8,128)(2,1)S(1)}, u32[]{:S(2)}, u32[]{:S(2)}) collective-permute-start(bf16[128,1024]{1,0:T(8,128)(2,1)S(1)} %get-tuple-element.106), channel_id=1, source_target_pairs={{0,8},{8,16},{16,24},{1,9},{9,17},{17,25},{2,10},{10,18},{18,26},{... | collective-permute-start | bytes 786440 | tf_op jit(solution)/shard_map/ppermute | solution.py:315
  222.3 4.6 %collective-permute-start.17 = (bf16[128,1024]{1,0:T(8,128)(2,1)S(1)}, bf16[128,1024]{1,0:T(8,128)(2,1)S(1)}, u32[]{:S(2)}, u32[]{:S(2)}) collective-permute-start(bf16[128,1024]{1,0:T(8,128)(2,1)S(1)} %get-tuple-element.108), channel_id=1, source_target_pairs={{0,8},{8,16},{16,24},{1,9},{9,17},{17,25},{2,10},{10,18},{18,26},{... | collective-permute-start | bytes 786440 | tf_op jit(solution)/shard_map/ppermute | solution.py:315
  232.4 2.7 %collective-permute-done.19.refs_3_ = bf16[128,1024]{1,0:T(8,128)(2,1)S(1)} collective-permute-done((bf16[128,1024]{1,0:T(8,128)(2,1)S(1)}, bf16[128,1024]{1,0:T(8,128)(2,1)S(1)}, u32[]{:S(2)}, u32[]{:S(2)}) %collective-permute-start.19) | collective-permute-done | bytes 262176 | tf_op jit(solution)/shard_map/ppermute | solution.py:315
  (121 shorter events, 71.6 us)
Async XLA Ops:
  14.3 19.9 %collective-permute-start = (bf16[128,1024]{1,0:T(8,128)(2,1)}, bf16[128,1024]{1,0:T(8,128)(2,1)}, u32[]{:S(2)}, u32[]{:S(2)}) collective-permute-start(bf16[128,1024]{1,0:T(8,128)(2,1)} %get-tuple-element.54), channel_id=1, source_target_pairs={{0,8},{8,16},{16,24},{24,0},{1,9},{9,17},{17,25},{25,1},{2,10},{10... | collective-permute-start | bytes 786440 | tf_op jit(solution)/shard_map/ppermute | solution.py:298
  16.9 17.3 %collective-permute-start.1 = (bf16[128,1024]{1,0:T(8,128)(2,1)}, bf16[128,1024]{1,0:T(8,128)(2,1)}, u32[]{:S(2)}, u32[]{:S(2)}) collective-permute-start(bf16[128,1024]{1,0:T(8,128)(2,1)} %get-tuple-element.55), channel_id=1, source_target_pairs={{0,24},{8,0},{16,8},{24,16},{1,25},{9,1},{17,9},{25,17},{2,26},{10... | collective-permute-start | bytes 786440 | tf_op jit(solution)/shard_map/ppermute | solution.py:298
  33.4 15.6 %collective-permute-start.4 = (bf16[128,2048]{1,0:T(8,128)(2,1)S(1)}, bf16[128,2048]{1,0:T(8,128)(2,1)S(1)}, u32[]{:S(2)}, u32[]{:S(2)}) collective-permute-start(bf16[128,2048]{1,0:T(8,128)(2,1)S(1)} %get-tuple-element.59), channel_id=1, source_target_pairs={{0,2},{2,0},{4,6},{6,4},{1,3},{3,1},{5,7},{7,5},{8,10},{10,8},{12,... | collective-permute-start | bytes 1572872 | tf_op jit(solution)/shard_map/ppermute | solution.py:328
  33.4 14.6 %collective-permute-start.2 = (bf16[128,1024]{1,0:T(8,128)(2,1)S(1)}, bf16[128,1024]{1,0:T(8,128)(2,1)}, u32[]{:S(2)}, u32[]{:S(2)}) collective-permute-start(bf16[128,1024]{1,0:T(8,128)(2,1)S(1)} %get-tuple-element.56), channel_id=1, source_target_pairs={{0,16},{8,24},{16,0},{24,8},{1,17},{9,25},{17,1},{25,9},{2,18},{10... | collective-permute-start | bytes 786440 | tf_op jit(solution)/shard_map/ppermute | solution.py:298
  112.1 12.2 %collective-permute-start.9 = (bf16[128,2048]{1,0:T(8,128)(2,1)S(1)}, bf16[128,2048]{1,0:T(8,128)(2,1)S(1)}, u32[]{:S(2)}, u32[]{:S(2)}) collective-permute-start(bf16[128,2048]{1,0:T(8,128)(2,1)S(1)} %get-tuple-element.72), channel_id=1, source_target_pairs={{0,2},{2,0},{4,6},{6,4},{1,3},{3,1},{5,7},{7,5},{8,10},{10,8},{12,... | collective-permute-start | bytes 1572872 | tf_op jit(solution)/shard_map/ppermute | solution.py:328
  113.9 24.1 %collective-permute-start.41 = (bf16[128,1024]{1,0:T(8,128)(2,1)S(1)}, bf16[128,1024]{1,0:T(8,128)(2,1)}, u32[]{:S(2)}, u32[]{:S(2)}) collective-permute-start(bf16[128,1024]{1,0:T(8,128)(2,1)S(1)} %get-tuple-element.100), channel_id=1, source_target_pairs={{0,4},{2,6},{4,0},{6,2},{1,5},{3,7},{5,1},{7,3},{8,12},{10,14},{12... | collective-permute-start | bytes 786440 | tf_op jit(solution)/shard_map/ppermute | solution.py:339
  122.2 15.8 %collective-permute-start.42 = (bf16[128,1024]{1,0:T(8,128)(2,1)}, bf16[128,1024]{1,0:T(8,128)(2,1)}, u32[]{:S(2)}, u32[]{:S(2)}) collective-permute-start(bf16[128,1024]{1,0:T(8,128)(2,1)} %add_convert_fusion.3), channel_id=1, source_target_pairs={{0,8},{24,16},{1,9},{25,17},{2,10},{26,18},{3,11},{27,19},{4,12},{... | collective-permute-start | bytes 786440 | tf_op jit(solution)/shard_map/ppermute | solution.py:315
  135.4 23.0 %collective-permute-start.11 = (bf16[384,2048]{1,0:T(8,128)(2,1)S(1)}, bf16[384,2048]{1,0:T(8,128)(2,1)S(1)}, u32[]{:S(2)}, u32[]{:S(2)}) collective-permute-start(bf16[384,2048]{1,0:T(8,128)(2,1)S(1)} %project.14), channel_id=1, source_target_pairs={{0,2},{2,0},{4,6},{6,4},{1,3},{3,1},{5,7},{7,5},{8,10},{10,8},{12,... | collective-permute-start | bytes 4718600 | tf_op jit(solution)/shard_map/ppermute | solution.py:336
  145.5 11.2 %collective-permute-start.22 = (bf16[128,1024]{1,0:T(8,128)(2,1)S(1)}, bf16[128,1024]{1,0:T(8,128)(2,1)S(1)}, u32[]{:S(2)}, u32[]{:S(2)}) collective-permute-start(bf16[128,1024]{1,0:T(8,128)(2,1)S(1)} %get-tuple-element.86), channel_id=1, source_target_pairs={{0,4},{2,6},{4,0},{6,2},{1,5},{3,7},{5,1},{7,3},{8,12},{10,14},{12... | collective-permute-start | bytes 786440 | tf_op jit(solution)/shard_map/ppermute | solution.py:339
  147.4 16.1 %collective-permute-start.32 = (bf16[128,1024]{1,0:T(8,128)(2,1)S(1)}, bf16[128,1024]{1,0:T(8,128)(2,1)S(1)}, u32[]{:S(2)}, u32[]{:S(2)}) collective-permute-start(bf16[128,1024]{1,0:T(8,128)(2,1)S(1)} %get-tuple-element.94), channel_id=1, source_target_pairs={{0,4},{2,6},{4,0},{6,2},{1,5},{3,7},{5,1},{7,3},{8,12},{10,14},{12... | collective-permute-start | bytes 786440 | tf_op jit(solution)/shard_map/ppermute | solution.py:339
  147.9 33.3 %collective-permute-start.30 = (bf16[128,1024]{1,0:T(8,128)(2,1)S(1)}, bf16[128,1024]{1,0:T(8,128)(2,1)S(1)}, u32[]{:S(2)}, u32[]{:S(2)}) collective-permute-start(bf16[128,1024]{1,0:T(8,128)(2,1)S(1)} %get-tuple-element.91), channel_id=1, source_target_pairs={{0,4},{2,6},{4,0},{6,2},{1,5},{3,7},{5,1},{7,3},{8,12},{10,14},{12... | collective-permute-start | bytes 786440 | tf_op jit(solution)/shard_map/ppermute | solution.py:339
  151.2 13.4 %collective-permute-start.33 = (bf16[128,1024]{1,0:T(8,128)(2,1)S(1)}, bf16[128,1024]{1,0:T(8,128)(2,1)S(1)}, u32[]{:S(2)}, u32[]{:S(2)}) collective-permute-start(bf16[128,1024]{1,0:T(8,128)(2,1)S(1)} %add_convert_fusion.7), channel_id=1, source_target_pairs={{0,8},{24,16},{1,9},{25,17},{2,10},{26,18},{3,11},{27,19},{4,12},{... | collective-permute-start | bytes 786440 | tf_op jit(solution)/shard_map/ppermute | solution.py:315
  156.8 16.9 %collective-permute-start.23 = (bf16[128,1024]{1,0:T(8,128)(2,1)S(1)}, bf16[128,1024]{1,0:T(8,128)(2,1)S(1)}, u32[]{:S(2)}, u32[]{:S(2)}) collective-permute-start(bf16[128,1024]{1,0:T(8,128)(2,1)S(1)} %get-tuple-element.88), channel_id=1, source_target_pairs={{0,4},{2,6},{4,0},{6,2},{1,5},{3,7},{5,1},{7,3},{8,12},{10,14},{12... | collective-permute-start | bytes 786440 | tf_op jit(solution)/shard_map/ppermute | solution.py:339
  158.4 15.9 %collective-permute-start.24 = (bf16[128,1024]{1,0:T(8,128)(2,1)S(1)}, bf16[128,1024]{1,0:T(8,128)(2,1)S(1)}, u32[]{:S(2)}, u32[]{:S(2)}) collective-permute-start(bf16[128,1024]{1,0:T(8,128)(2,1)S(1)} %add_convert_fusion.11), channel_id=1, source_target_pairs={{0,8},{24,16},{1,9},{25,17},{2,10},{26,18},{3,11},{27,19},{4,12},{... | collective-permute-start | bytes 786440 | tf_op jit(solution)/shard_map/ppermute | solution.py:315
  163.5 15.8 %collective-permute-start.13 = (bf16[128,1024]{1,0:T(8,128)(2,1)S(1)}, bf16[128,1024]{1,0:T(8,128)(2,1)S(1)}, u32[]{:S(2)}, u32[]{:S(2)}) collective-permute-start(bf16[128,1024]{1,0:T(8,128)(2,1)S(1)} %get-tuple-element.80), channel_id=1, source_target_pairs={{0,4},{2,6},{4,0},{6,2},{1,5},{3,7},{5,1},{7,3},{8,12},{10,14},{12... | collective-permute-start | bytes 786440 | tf_op jit(solution)/shard_map/ppermute | solution.py:339
  164.7 17.2 %collective-permute-start.34 = (bf16[128,1024]{1,0:T(8,128)(2,1)S(1)}, bf16[128,1024]{1,0:T(8,128)(2,1)S(1)}, u32[]{:S(2)}, u32[]{:S(2)}) collective-permute-start(bf16[128,1024]{1,0:T(8,128)(2,1)S(1)} %add_convert_fusion.6), channel_id=1, source_target_pairs={{0,8},{8,16},{1,9},{9,17},{2,10},{10,18},{3,11},{11,19},{4,12},{12... | collective-permute-start | bytes 786440 | tf_op jit(solution)/shard_map/ppermute | solution.py:315
  174.3 18.9 %collective-permute-start.21 = (bf16[128,1024]{1,0:T(8,128)(2,1)S(1)}, bf16[128,1024]{1,0:T(8,128)(2,1)S(1)}, u32[]{:S(2)}, u32[]{:S(2)}) collective-permute-start(bf16[128,1024]{1,0:T(8,128)(2,1)S(1)} %get-tuple-element.85), channel_id=1, source_target_pairs={{0,4},{2,6},{4,0},{6,2},{1,5},{3,7},{5,1},{7,3},{8,12},{10,14},{12... | collective-permute-start | bytes 786440 | tf_op jit(solution)/shard_map/ppermute | solution.py:339
  179.2 14.6 %collective-permute-start.25 = (bf16[128,1024]{1,0:T(8,128)(2,1)S(1)}, bf16[128,1024]{1,0:T(8,128)(2,1)S(1)}, u32[]{:S(2)}, u32[]{:S(2)}) collective-permute-start(bf16[128,1024]{1,0:T(8,128)(2,1)S(1)} %add_convert_fusion.10), channel_id=1, source_target_pairs={{0,8},{8,16},{1,9},{9,17},{2,10},{10,18},{3,11},{11,19},{4,12},{12... | collective-permute-start | bytes 786440 | tf_op jit(solution)/shard_map/ppermute | solution.py:315
  181.2 17.0 %collective-permute-start.27 = (bf16[128,1024]{1,0:T(8,128)(2,1)S(1)}, bf16[128,1024]{1,0:T(8,128)(2,1)S(1)}, u32[]{:S(2)}, u32[]{:S(2)}) collective-permute-start(bf16[128,1024]{1,0:T(8,128)(2,1)S(1)} %add_convert_fusion.10), channel_id=1, source_target_pairs={{24,16},{16,8},{25,17},{17,9},{26,18},{18,10},{27,19},{19,11},{28,... | collective-permute-start | bytes 786440 | tf_op jit(solution)/shard_map/ppermute | solution.py:315
  191.6 13.3 %collective-permute-start.29 = (bf16[128,1024]{1,0:T(8,128)(2,1)S(1)}, bf16[128,1024]{1,0:T(8,128)(2,1)S(1)}, u32[]{:S(2)}, u32[]{:S(2)}) collective-permute-start(bf16[128,1024]{1,0:T(8,128)(2,1)S(1)} %get-tuple-element.89), channel_id=1, source_target_pairs={{0,4},{2,6},{4,0},{6,2},{1,5},{3,7},{5,1},{7,3},{8,12},{10,14},{12... | collective-permute-start | bytes 786440 | tf_op jit(solution)/shard_map/ppermute | solution.py:331
  193.2 15.7 %collective-permute-start.12 = (bf16[128,1024]{1,0:T(8,128)(2,1)S(1)}, bf16[128,1024]{1,0:T(8,128)(2,1)S(1)}, u32[]{:S(2)}, u32[]{:S(2)}) collective-permute-start(bf16[128,1024]{1,0:T(8,128)(2,1)S(1)} %get-tuple-element.79), channel_id=1, source_target_pairs={{0,4},{2,6},{4,0},{6,2},{1,5},{3,7},{5,1},{7,3},{8,12},{10,14},{12... | collective-permute-start | bytes 786440 | tf_op jit(solution)/shard_map/ppermute | solution.py:339
  193.8 16.8 %collective-permute-start.16 = (bf16[128,1024]{1,0:T(8,128)(2,1)S(1)}, bf16[128,1024]{1,0:T(8,128)(2,1)S(1)}, u32[]{:S(2)}, u32[]{:S(2)}) collective-permute-start(bf16[128,1024]{1,0:T(8,128)(2,1)S(1)} %add_convert_fusion.14), channel_id=1, source_target_pairs={{0,8},{8,16},{1,9},{9,17},{2,10},{10,18},{3,11},{11,19},{4,12},{12... | collective-permute-start | bytes 786440 | tf_op jit(solution)/shard_map/ppermute | solution.py:315
  198.2 14.2 %collective-permute-start.18 = (bf16[128,1024]{1,0:T(8,128)(2,1)S(1)}, bf16[128,1024]{1,0:T(8,128)(2,1)S(1)}, u32[]{:S(2)}, u32[]{:S(2)}) collective-permute-start(bf16[128,1024]{1,0:T(8,128)(2,1)S(1)} %add_convert_fusion.14), channel_id=1, source_target_pairs={{24,16},{16,8},{25,17},{17,9},{26,18},{18,10},{27,19},{19,11},{28,... | collective-permute-start | bytes 786440 | tf_op jit(solution)/shard_map/ppermute | solution.py:315
  199.3 14.7 %collective-permute-start.44 = (bf16[128,1024]{1,0:T(8,128)(2,1)S(1)}, bf16[128,1024]{1,0:T(8,128)(2,1)S(1)}, u32[]{:S(2)}, u32[]{:S(2)}) collective-permute-start(bf16[128,1024]{1,0:T(8,128)(2,1)S(1)} %get-tuple-element.102), channel_id=1, source_target_pairs={{0,8},{8,16},{16,24},{1,9},{9,17},{17,25},{2,10},{10,18},{18,26},{... | collective-permute-start | bytes 786440 | tf_op jit(solution)/shard_map/ppermute | solution.py:315
  204.9 10.1 %collective-permute-start.46 = (bf16[128,1024]{1,0:T(8,128)(2,1)S(1)}, bf16[128,1024]{1,0:T(8,128)(2,1)S(1)}, u32[]{:S(2)}, u32[]{:S(2)}) collective-permute-start(bf16[128,1024]{1,0:T(8,128)(2,1)S(1)} %get-tuple-element.101), channel_id=1, source_target_pairs={{24,16},{16,8},{8,0},{25,17},{17,9},{9,1},{26,18},{18,10},{10,2},{... | collective-permute-start | bytes 786440 | tf_op jit(solution)/shard_map/ppermute | solution.py:315
  208.9 12.1 %collective-permute-start.20 = (bf16[128,1024]{1,0:T(8,128)(2,1)S(1)}, bf16[128,1024]{1,0:T(8,128)(2,1)S(1)}, u32[]{:S(2)}, u32[]{:S(2)}) collective-permute-start(bf16[128,1024]{1,0:T(8,128)(2,1)S(1)} %get-tuple-element.83), channel_id=1, source_target_pairs={{0,4},{2,6},{4,0},{6,2},{1,5},{3,7},{5,1},{7,3},{8,12},{10,14},{12... | collective-permute-start | bytes 786440 | tf_op jit(solution)/shard_map/ppermute | solution.py:331
  210.6 11.7 %collective-permute-start.35 = (bf16[128,1024]{1,0:T(8,128)(2,1)S(1)}, bf16[128,1024]{1,0:T(8,128)(2,1)S(1)}, u32[]{:S(2)}, u32[]{:S(2)}) collective-permute-start(bf16[128,1024]{1,0:T(8,128)(2,1)S(1)} %get-tuple-element.104), channel_id=1, source_target_pairs={{0,8},{8,16},{16,24},{1,9},{9,17},{17,25},{2,10},{10,18},{18,26},{... | collective-permute-start | bytes 786440 | tf_op jit(solution)/shard_map/ppermute | solution.py:315
  212.4 14.4 %collective-permute-start.37 = (bf16[128,1024]{1,0:T(8,128)(2,1)S(1)}, bf16[128,1024]{1,0:T(8,128)(2,1)S(1)}, u32[]{:S(2)}, u32[]{:S(2)}) collective-permute-start(bf16[128,1024]{1,0:T(8,128)(2,1)S(1)} %get-tuple-element.103), channel_id=1, source_target_pairs={{24,16},{16,8},{8,0},{25,17},{17,9},{9,1},{26,18},{18,10},{10,2},{... | collective-permute-start | bytes 786440 | tf_op jit(solution)/shard_map/ppermute | solution.py:315
  214.0 18.4 %collective-permute-start.10 = (bf16[128,1024]{1,0:T(8,128)(2,1)S(1)}, bf16[128,1024]{1,0:T(8,128)(2,1)S(1)}, u32[]{:S(2)}, u32[]{:S(2)}) collective-permute-start(bf16[128,1024]{1,0:T(8,128)(2,1)S(1)} %get-tuple-element.74), channel_id=1, source_target_pairs={{0,4},{2,6},{4,0},{6,2},{1,5},{3,7},{5,1},{7,3},{8,12},{10,14},{12... | collective-permute-start | bytes 786440 | tf_op jit(solution)/shard_map/ppermute | solution.py:331
  215.1 15.2 %collective-permute-start.26 = (bf16[128,1024]{1,0:T(8,128)(2,1)S(1)}, bf16[128,1024]{1,0:T(8,128)(2,1)S(1)}, u32[]{:S(2)}, u32[]{:S(2)}) collective-permute-start(bf16[128,1024]{1,0:T(8,128)(2,1)S(1)} %get-tuple-element.106), channel_id=1, source_target_pairs={{0,8},{8,16},{16,24},{1,9},{9,17},{17,25},{2,10},{10,18},{18,26},{... | collective-permute-start | bytes 786440 | tf_op jit(solution)/shard_map/ppermute | solution.py:315
  221.0 10.4 %collective-permute-start.28 = (bf16[128,1024]{1,0:T(8,128)(2,1)S(1)}, bf16[128,1024]{1,0:T(8,128)(2,1)S(1)}, u32[]{:S(2)}, u32[]{:S(2)}) collective-permute-start(bf16[128,1024]{1,0:T(8,128)(2,1)S(1)} %get-tuple-element.105), channel_id=1, source_target_pairs={{24,16},{16,8},{8,0},{25,17},{17,9},{9,1},{26,18},{18,10},{10,2},{... | collective-permute-start | bytes 786440 | tf_op jit(solution)/shard_map/ppermute | solution.py:315
  222.3 10.1 %collective-permute-start.17 = (bf16[128,1024]{1,0:T(8,128)(2,1)S(1)}, bf16[128,1024]{1,0:T(8,128)(2,1)S(1)}, u32[]{:S(2)}, u32[]{:S(2)}) collective-permute-start(bf16[128,1024]{1,0:T(8,128)(2,1)S(1)} %get-tuple-element.108), channel_id=1, source_target_pairs={{0,8},{8,16},{16,24},{1,9},{9,17},{17,25},{2,10},{10,18},{18,26},{... | collective-permute-start | bytes 786440 | tf_op jit(solution)/shard_map/ppermute | solution.py:315
  (18 other events, 116.0 us)

commit v2 on v1

v2 whole, which is shorter than its diff:
```python
import functools
import math

import jax
import jax.numpy as jnp
from jax import lax
from jax.experimental import pallas as pl
from jax.experimental.pallas import tpu as pltpu
from jax.sharding import PartitionSpec as P

HEAD = 128
BLOCK = 128
PIECES = 4
TILE = 512


norm_epsilon = 1e-05
scale_epsilon = 1e-06
code_limit = 15.0
adapter_scale = 2.0
rope_theta = 500000.0
rope_factor = 8.0
low_factor = 1.0
high_factor = 4.0
initial_context = 8192.0
feature_scale = 1024.0

ANY = pl.BlockSpec(memory_space=pl.ANY)


def params(mebibytes):
    return pltpu.CompilerParams(vmem_limit_bytes=mebibytes << 20)


def cost(flops, nbytes):
    return pl.CostEstimate(flops=int(flops), bytes_accessed=int(nbytes), transcendentals=0)


def like(shape, dtype=jnp.bfloat16):
    return jax.ShapeDtypeStruct(shape, dtype)


def frequencies(positions):
    pair_index = jnp.arange(HEAD // 2, dtype=jnp.float32)
    inverse = jnp.exp(pair_index * (-2.0 * math.log(rope_theta) / HEAD))
    wavelength = 2.0 * math.pi / inverse
    blend = (initial_context / wavelength - low_factor) / (high_factor - low_factor)
    middle = (1.0 - blend) * inverse / rope_factor + blend * inverse
    adjusted = jnp.where(
        wavelength < initial_context / high_factor,
        inverse,
        jnp.where(wavelength > initial_context / low_factor, inverse / rope_factor, middle),
    )
    angles = positions.astype(jnp.float32)[:, None] * adjusted[None, :]
    return (jnp.cos(angles), jnp.sin(angles))


def turn_tables(hidden, positions):
    values = hidden.astype(jnp.float32)
    mean_square = jnp.mean(values * values, axis=1, keepdims=True)
    factor = lax.rsqrt(mean_square + norm_epsilon) * (1.0 / feature_scale)
    cosine, sine_part = frequencies(positions)
    return (
        jnp.concatenate([cosine, cosine], axis=1) * factor,
        jnp.concatenate([-sine_part, sine_part], axis=1) * factor,
    )


def pick_kernel(table, *refs):
    count = len(refs) // 3
    for i in range(count):
        values, gain, out = refs[i], refs[count + i], refs[2 * count + i]
        scaled = values[...].astype(jnp.float32) * (gain[...].astype(jnp.float32) * feature_scale)
        out[...] = scaled.astype(jnp.bfloat16)


def pick(hidden, norm_gain, table, count, width):
    tokens = hidden.shape[0]

    def spec(rows, i):
        return pl.BlockSpec((rows, width), lambda step, table: (0, table[i]))

    return pl.pallas_call(
        pick_kernel,
        grid_spec=pltpu.PrefetchScalarGridSpec(
            num_scalar_prefetch=1,
            grid=(1,),
            in_specs=[spec(tokens, i) for i in range(count)] + [spec(1, i) for i in range(count)],
            out_specs=[pl.BlockSpec((tokens, width), lambda step, table: (0, 0))] * count,
        ),
        out_shape=[like((tokens, width))] * count,
        compiler_params=params(60),
        name="pick_features",
    )(table, *([hidden] * count), *([norm_gain] * count))


def scales_of(largest):
    ratio = (largest + scale_epsilon) / code_limit
    scale = jnp.exp2(jnp.ceil(jnp.log2(ratio))).astype(jnp.bfloat16).astype(jnp.float32)
    scale = jnp.where(ratio > scale, scale * 2.0, scale)
    return jnp.where(ratio <= scale * 0.5, scale * 0.5, scale)


def quantize_tile(base, down, up, weight, first, merged, scale_scratch):
    rows, width = base.shape
    row_blocks = rows // BLOCK
    first_block = first // BLOCK
    tops = []
    for i in range(row_blocks):
        block_rows = pl.ds(i * BLOCK, BLOCK)
        here = pl.ds(first + i * BLOCK, BLOCK)
        low_rank = jnp.dot(down[here, :], up[...], preferred_element_type=jnp.float32)
        total = base[block_rows, :].astype(jnp.float32) + low_rank
        merged[here, :] = total
        tops.append(jnp.max(jnp.abs(total), axis=0, keepdims=True))
    top = jnp.concatenate(tops, axis=0)
    blocks = pl.ds(first_block, row_blocks)
    for j in range(width // BLOCK):
        cols = slice(j * BLOCK, (j + 1) * BLOCK)
        largest = jnp.max(top[:, cols], axis=1, keepdims=True)
        scale = scales_of(jnp.broadcast_to(largest, (row_blocks, BLOCK)))
        scale_scratch[0, blocks, cols] = scale
        scale_scratch[1, blocks, cols] = 1.0 / scale
    for i in range(row_blocks):
        here = pl.ds(first + i * BLOCK, BLOCK)
        scale = scale_scratch[0, pl.ds(first_block + i, 1), :]
        inverse = scale_scratch[1, pl.ds(first_block + i, 1), :]
        codes = jnp.floor(merged[here, :] * inverse + 0.5)
        weight[here, :] = codes.astype(jnp.bfloat16) * scale.astype(jnp.bfloat16)


def gather_features(pieces, x):
    @pl.when(pl.program_id(0) == 0)
    def _():
        row = 0
        for line in pieces:
            col = 0
            for piece in line:
                x[row : row + piece.shape[0], col : col + piece.shape[1]] = piece[...]
                col += piece.shape[1]
            row += line[0].shape[0]


def store_rows(product, outs):
    first = 0
    for out in outs:
        out[...] = product[first : first + out.shape[0], :].astype(jnp.bfloat16)
        first += out.shape[0]


def split_lines(refs, shape):
    lines = []
    for length in shape:
        lines.append(refs[:length])
        refs = refs[length:]
    return lines, refs


def pass_kernel(sources, shape, late, after, keep, outs, carry, table, *refs):
    if carry:
        end = len(refs) - (3 if keep else 4)
        for k in range(carry):
            refs[end - carry + k][...] = refs[k][...]
        refs = refs[carry : end - carry] + refs[end:]
    bases, refs = refs[:sources], refs[sources:]
    (down, up), refs = refs[:2], refs[2:]
    kept, refs = (refs[0], refs[1:]) if late else (None, refs)
    lines, refs = split_lines(refs, shape)
    refs = refs[after:]
    place = 0 if keep else outs
    weight, refs = refs[place], refs[:place] + refs[place + 1 :]
    outs, (x, merged, scale_scratch) = refs[:outs], refs[outs:]
    if lines:
        gather_features(lines, x)
    products = []
    if late:
        tokens = lines[-1][0].shape[0]
        last = x[x.shape[0] - tokens :, :]
        products.append(jnp.dot(last, kept[...], preferred_element_type=jnp.float32))
    rows = bases[0].shape[0]
    for i, base in enumerate(bases):
        quantize_tile(base, down, up, weight, i * rows, merged, scale_scratch)
    if lines:
        products.append(jnp.dot(x[...], weight[...], preferred_element_type=jnp.float32))
        store_rows(jnp.concatenate(products, axis=0) if late else products[0], outs)


def row_outs(out_rows, steps, width):
    def spec(count, block):
        return pl.BlockSpec((count, width), lambda i, *_: (block, i))

    shapes = [like((total, steps * width)) for _, _, total in out_rows]
    return shapes, [spec(count, block) for count, block, _ in out_rows]


def merge_pass(
    bases, down, up, table, steps, width, lines=(), out_rows=(), kept=None, keep=False, carry=None,
    onto=None, after=(),
):
    rows = bases[0][0].shape[0]
    depth, rank = down.shape
    tokens = sum(line[0].shape[0] for line in lines)

    def fixed(shape):
        return pl.BlockSpec(shape, lambda i, table: (0, 0))

    def tile(height, place):
        if place is None:
            return pl.BlockSpec((height, width), lambda i, table: (0, table[i]))
        return pl.BlockSpec((height, width), lambda i, table: (0, place + i))

    operands = [base for base, _ in bases] + [down, up]
    in_specs = [tile(rows, place) for _, place in bases] + [fixed(down.shape), tile(rank, None)]
    if kept is not None:
        operands.append(kept)
        in_specs.append(tile(depth, 0))
    for line in lines:
        operands += line
        in_specs += [fixed(piece.shape) for piece in line]
    if onto is not None:
        after = (onto, *after)
    operands += after
    in_specs += [ANY] * len(after)
    out_shape, out_specs = row_outs(out_rows, steps, width)
    carried = 0
    if carry is not None:
        values, span, carried = carry
        block = (values.shape[0], span)

        def carry_spec(k):
            return pl.BlockSpec(block, lambda i, table: (0, table[steps + k * steps + i]))

        operands = [values] * carried + operands
        in_specs = [carry_spec(k) for k in range(carried)] + in_specs
    scratch = [
        pltpu.VMEM((max(tokens, 16), depth), jnp.bfloat16),
        pltpu.VMEM((depth, width), jnp.float32),
        pltpu.VMEM((2, depth // BLOCK, width), jnp.float32),
    ]
    if keep:
        out_shape.insert(0, like((depth, steps * width)))
        out_specs.insert(0, tile(depth, 0))
    else:
        scratch.insert(0, pltpu.VMEM((depth, width), jnp.bfloat16))
    if carry is not None:
        out_shape += [like((block[0], steps * span))] * carried
        out_specs += [pl.BlockSpec(block, lambda i, table: (0, i))] * carried
    return pl.pallas_call(
        functools.partial(
            pass_kernel, len(bases), [len(line) for line in lines], kept is not None, len(after),
            keep, len(out_rows), carried,
        ),
        grid_spec=pltpu.PrefetchScalarGridSpec(
            num_scalar_prefetch=1,
            grid=(steps,),
            in_specs=in_specs,
            out_specs=out_specs,
            scratch_shapes=scratch,
        ),
        out_shape=out_shape,
        input_output_aliases={} if onto is None else {1 + len(operands) - len(after): 0},
        cost_estimate=cost(2 * tokens * depth * steps * width, 4 * depth * steps * width),
        compiler_params=params(42 if carried else 28),
        name="merge_pass",
    )(table, *operands)


def project_kernel(shape, after, outs, weight, *refs):
    lines, refs = split_lines(refs, shape)
    outs, x = refs[after : after + outs], refs[-1]
    gather_features(lines, x)
    store_rows(jnp.dot(x[...], weight[...], preferred_element_type=jnp.float32), outs)


def project(weight, steps, lines, out_rows, after=()):
    depth, columns = weight.shape
    width = columns // steps
    tokens = sum(line[0].shape[0] for line in lines)
    pieces = [piece for line in lines for piece in line]
    out_shape, out_specs = row_outs(out_rows, steps, width)
    return pl.pallas_call(
        functools.partial(project_kernel, [len(line) for line in lines], len(after), len(out_rows)),
        grid=(steps,),
        in_specs=[pl.BlockSpec((depth, width), lambda i: (0, i))]
        + [pl.BlockSpec(piece.shape, lambda i: (0, 0)) for piece in pieces]
        + [ANY] * len(after),
        out_specs=out_specs,
        out_shape=out_shape,
        scratch_shapes=[pltpu.VMEM((tokens, depth), jnp.bfloat16)],
        cost_estimate=cost(2 * tokens * depth * columns, 2 * depth * columns),
        compiler_params=params(20),
        name="project",
    )(weight, *pieces, *after)


def take_kernel(table, values, *refs):
    refs[-1][...] = values[...]


def take_tiles(values, table, steps, width, after=()):
    rows = values.shape[0]
    return pl.pallas_call(
        take_kernel,
        grid_spec=pltpu.PrefetchScalarGridSpec(
            num_scalar_prefetch=1,
            grid=(steps,),
            in_specs=[pl.BlockSpec((rows, width), lambda i, table: (0, table[i]))]
            + [ANY] * len(after),
            out_specs=pl.BlockSpec((rows, width), lambda i, table: (0, i)),
        ),
        out_shape=like((rows, steps * width)),
        compiler_params=params(40),
        name="take_tiles",
    )(table, values, *after)


def turn_kernel(count, cosine, sine_part, *refs):
    out = refs[-1]
    for j in range(out.shape[1] // HEAD):
        cols = slice(j * HEAD, (j + 1) * HEAD)
        total = refs[0][:, cols].astype(jnp.float32)
        for term in refs[1:count]:
            total = total + term[:, cols].astype(jnp.float32)
        swapped = pltpu.roll(total, HEAD // 2, 1)
        turned = total * cosine[...] + swapped * sine_part[...]
        out[:, cols] = turned.astype(jnp.bfloat16)


def turn(cosine, sine_part, terms, place, places, into, after=()):
    tokens = cosine.shape[0]
    columns = terms[0][0].shape[1]
    width = math.gcd(columns, place) if place else columns
    table = pl.BlockSpec((tokens, HEAD), lambda i: (0, 0))

    def term_spec(block):
        return pl.BlockSpec((tokens, width), lambda i: (block, i))

    extra = [] if into is None else [into]
    count = len(terms)
    return pl.pallas_call(
        functools.partial(turn_kernel, count),
        grid=(columns // width,),
        in_specs=[table] * 2 + [term_spec(block) for _, block in terms]
        + [ANY] * (len(extra) + len(after)),
        out_specs=pl.BlockSpec((tokens, width), lambda i: (0, place // width + i)),
        out_shape=like((tokens, places)),
        input_output_aliases={2 + count: 0} if extra else {},
        compiler_params=params(12),
        name="turn",
    )(cosine, sine_part, *[term for term, _ in terms], *extra, *after)


def add_kernel(count, *refs):
    total = refs[0][...].astype(jnp.float32)
    for term in refs[1:count]:
        total = total + term[...].astype(jnp.float32)
    refs[-1][...] = total.astype(jnp.bfloat16)


def added(terms, rows, after=()):
    columns = terms[0][0].shape[1]
    width = tile_width(columns, 512)

    def term_spec(block):
        return pl.BlockSpec((rows, width), lambda i: (block, i))

    return pl.pallas_call(
        functools.partial(add_kernel, len(terms)),
        grid=(columns // width,),
        in_specs=[term_spec(block) for _, block in terms] + [ANY] * len(after),
        out_specs=term_spec(0),
        out_shape=like((rows, columns)),
        compiler_params=params(12),
        name="add_terms",
    )(*[term for term, _ in terms], *after)


def tile_width(columns, most):
    width = min(columns, most)
    while columns % width:
        width //= 2
    return width


def line_shards(hidden, base, down, up, norm_gain, positions):
    tp = lax.axis_index("tp")
    z = lax.axis_index("fsdp")
    rows, all_columns = base.shape
    tokens = hidden.shape[0]
    quarter = all_columns // 4
    other_core, other_chip, other_both = tp ^ 1, tp ^ 2, tp ^ 3

    def over(axis, distance):
        return functools.partial(
            lax.ppermute, axis_name=axis, perm=[(i, i ^ distance) for i in range(4)]
        )

    over_core, over_y = over("tp", 1), over("tp", 2)
    over_z1, over_z2 = over("fsdp", 1), over("fsdp", 2)

    piece = quarter // PIECES
    width = tile_width(piece, min(TILE, piece // 2))
    steps = piece // width

    def tiles(*places):
        offsets = jnp.arange(steps, dtype=jnp.int32)
        starts = [owner * (quarter // width) + i * steps for owner, i in places]
        return jnp.concatenate([start + offsets for start in starts]).astype(jnp.int32)

    blocks = [(z ^ d) * 4 + tp for d in range(4)] + [z * 4 + other_core]
    own_x, p1, p2, p3, own_other = pick(
        hidden, norm_gain[None, :], jnp.stack(blocks).astype(jnp.int32), 5, rows
    )
    x1, x2, x3 = over("fsdp", 1)(p1), over("fsdp", 2)(p2), over("fsdp", 3)(p3)
    first_lines = [[x1, over_core(x1)], [x3, over_core(x3)], [own_x, own_other]]
    all_lines = [*first_lines, [x2, over_core(x2)]]

    down2 = jnp.concatenate([down, over_core(down)], axis=0)
    up2 = up * jnp.bfloat16(adapter_scale)

    def spans(names, count):
        span = min(piece, piece * len(names) // count)
        each = piece // span
        owners = [(other_both if kind == "y" else other_core) for kind, _ in names]
        firsts = [(owner * PIECES + i) * each for owner, (_, i) in zip(owners, names)]
        blocks = [first + k for first in firsts for k in range(each)]
        return jnp.stack(blocks).astype(jnp.int32), span

    received = {}

    def send(taken, names):
        arrived = over_core(taken)
        for k, name in enumerate(names):
            received[name] = (arrived, k * steps)

    def take(names, after):
        table, span = spans(names, len(names))
        taken = take_tiles(base, table, len(names), span, after)
        send(taken, names)
        return taken

    taken = take([("y", 0)], (own_x,))
    taken = take([("y", 1), ("own", 0), ("y", 2)], (taken, down2))

    def run_pass(owner, i, kind, carried, **options):
        table = tiles((owner, i))
        carry = None
        if carried:
            blocks, span = spans(sum(carried, []), steps * len(carried))
            table = jnp.concatenate([table, blocks])
            carry = (base, span, len(carried))
        outs = merge_pass(
            [(base, None), received[kind, i]], down2, up2, table, steps, width, carry=carry, **options,
        )
        if carried:
            outs, taken = outs[: -len(carried)], outs[-len(carried) :]
            for value, names in zip(taken, carried):
                send(value, names)
        return outs

    first_rows = [(2 * tokens, 0, 2 * tokens), (tokens, 0, 2 * tokens)]
    second_rows = [(tokens, 1, 2 * tokens), (2 * tokens, 0, 2 * tokens)] + [(tokens, 0, tokens)] * 2
    weights, halves, far_y, mid_y = {}, {}, {}, {}
    near, own, far, near_z, far_z = {}, {}, {}, {}, {}

    def weigh(i, after, carried=()):
        (weights[i],) = run_pass(other_chip, i, "y", carried, keep=True, after=after)

    def send_first(i, outs):
        value, halves[i] = outs
        far_y[i] = over_y(value)
        return value

    def first(i, after):
        weights[i], *outs = run_pass(
            other_chip, i, "y", (), lines=first_lines, out_rows=first_rows, keep=True, after=after
        )
        return send_first(i, outs)

    def second(i, after):
        half, near[i], own[i], far[i] = run_pass(
            tp, i, "own", (), lines=all_lines, out_rows=second_rows, kept=weights[i],
            onto=halves[i], after=after,
        )
        mid_y[i] = over_y(half)
        return half

    def to_z1(i, after):
        operand = added([(near[i], 0), (far_y[i], 0)], 2 * tokens, after)
        near_z[i] = over_z1(operand)
        return operand

    def to_z2(i, after):
        operand = added([(far[i], 0), (mid_y[i], 1), (near_z[i], 1)], tokens, after)
        far_z[i] = over_z2(operand)
        return operand

    def finish(i, out, after):
        terms = [(own[i], 0), (mid_y[i], 0), (near_z[i], 0), (far_z[i], 0)]
        return turn(cosine, sine_part, terms, i * piece, quarter, out, after)

    early_xs = sum(first_lines, [])
    weigh(0, (taken, *early_xs), [[("own", 1), ("y", 3)], [("own", 2), ("own", 3)]])
    done = send_first(0, project(weights[0], steps, first_lines, first_rows))
    done = first(1, (done,))
    done = second(0, (done, received["own", 2][0]))
    done = to_z1(0, (done,))
    done = first(2, (done,))
    done = second(1, (done,))
    done = to_z1(1, (done,))
    done = to_z2(0, (done,))
    done = first(3, (done,))
    done = second(2, (done,))
    done = to_z1(2, (done,))
    cosine, sine_part = turn_tables(lax.optimization_barrier((hidden, done))[0], positions)
    out = finish(0, None, (done,))
    done = to_z2(1, (out,))
    done = second(3, (done,))
    done = to_z1(3, (done,))
    out = finish(1, out, (done,))
    done = to_z2(2, (out,))
    out = finish(2, out, (done,))
    done = to_z2(3, (out,))
    return finish(3, out, (done,))


def any_shards(fsdp, tp_size, hidden, base, down, up, norm_gain, positions):
    tp = lax.axis_index("tp")
    rows, all_columns = base.shape
    tokens = hidden.shape[0]
    share = all_columns // tp_size
    chunks = max(1, share // 256)
    piece = share // chunks
    width = tile_width(piece, TILE)
    steps = piece // width

    blocks = (jnp.arange(fsdp) * tp_size + tp).astype(jnp.int32)
    picked = pick(hidden, norm_gain[None, :], blocks, fsdp, rows)
    x = lax.all_to_all(jnp.stack(picked), "fsdp", 0, 0, tiled=True)
    x = x.reshape(fsdp * tokens, rows)
    up2 = up * jnp.bfloat16(adapter_scale)
    cosine, sine_part = turn_tables(hidden, positions)
    out = None
    after = ()
    for chunk in range(chunks):
        owners = jnp.arange(tp_size, dtype=jnp.int32)[:, None] * (share // width)
        offsets = jnp.arange(steps, dtype=jnp.int32)[None, :] + chunk * steps
        (products,) = merge_pass(
            [(base, None)], down, up2, (owners + offsets).reshape(-1), tp_size * steps, width,
            [[x]], [(fsdp * tokens, 0, fsdp * tokens)], after=after,
        )
        products = products.reshape(fsdp * tokens, tp_size, piece).swapaxes(0, 1)
        mine = lax.psum_scatter(products, "tp", scatter_dimension=0, tiled=True)[0]
        mine = lax.psum_scatter(mine, "fsdp", scatter_dimension=0, tiled=True)
        out = turn(cosine, sine_part, [(mine, 0)], chunk * piece, share, out)
        after = (mine,)
    return out


def solution(mesh):
    fsdp, tp = mesh.shape["fsdp"], mesh.shape["tp"]
    if (fsdp, tp) == (4, 4):
        shards = line_shards
    else:
        shards = functools.partial(any_shards, fsdp, tp)
    placed = (
        P(("rep", "fsdp"), None),
        P(("rep", "fsdp", "tp"), None),
        P(("rep", "fsdp", "tp"), None),
        P("rep", None),
        P("rep"),
        P(("rep", "fsdp")),
    )
    return jax.shard_map(
        shards, mesh=mesh, in_specs=placed, out_specs=P(("rep", "fsdp"), "tp"), check_vma=False
    )
```

time: 237 us -> 171 us (0.72)
  starting transfers between devices: 72.4 us -> 27.1 us
  Pallas kernels: 91.9 us -> 78.2 us
  other arithmetic: 9.01 us -> 1.54 us
  local copies, waits for them, and re-layouts: 4 us -> 11.2 us
  waiting for transfers between devices: 58.2 us -> 52.3 us
    ppermute x47 -> x27, starting transfers between devices: 72.4 us -> 27.1 us  [the longest x3 7.33 us: line_shards(): x1, x2, x3 = (over('fsdp', 1)(p1), over('fsdp', 2)(p2), over('fsdp', 3)(p3))]
    pallas_call x20 -> x23, Pallas kernels: 90.6 us -> 75.1 us  [the longest x8 56.6 us: merge_pass(): pl.pallas_call(functools.partial(pass_kernel, len(bases), [len(line) for...]
    ppermute x47 -> x27, waiting for transfers between devices: 58.2 us -> 52.3 us  [the longest x4 30.4 us: to_z2(): far_z[i] = over_z2(operand)]
    unnamed x7 -> x30, local copies, waits for them, and re-layouts: 3.21 us -> 8.82 us
    convert_element_type x12 -> x0, other arithmetic: 3.62 us -> none  [added(): return total.astype(jnp.bfloat16)]
  transfers between devices with their start and end apart: 47 -> 27, of which waited for: 17 -> 8; matrix products, arithmetic and copies ran while one was open for 3% -> 1% of each run, Pallas kernels for 13% -> 41%
where the time goes in v2:
time: 171 us
  Pallas kernels  78.2 us (46%)
  waiting for transfers between devices  52.3 us (31%)
  starting transfers between devices  27.1 us (16%)
  local copies, waits for them, and re-layouts  11.2 us (7%)
    pallas_call x8, Pallas kernels, merge_pass(): pl.pallas_call(functools.partial(pass_kernel, len(bases), [len(line) for...  56.6 us
    ppermute x4, waiting for transfers between devices, to_z2(): far_z[i] = over_z2(operand)  30.4 us
    ppermute x3, waiting for transfers between devices, line_shards(): x1, x2, x3 = (over('fsdp', 1)(p1), over('fsdp', 2)(p2), over('fsdp', 3)(p3))  11 us
    pallas_call x2, Pallas kernels, take_tiles(): pl.pallas_call(take_kernel, grid_spec=pltpu.PrefetchScalarGridSpec(num_sc...  10.1 us
    unnamed x30, local copies, waits for them, and re-layouts  8.82 us
    ppermute x3, starting transfers between devices, line_shards(): x1, x2, x3 = (over('fsdp', 1)(p1), over('fsdp', 2)(p2), over('fsdp', 3)(p3))  7.33 us
    ppermute x4, starting transfers between devices, to_z1(): near_z[i] = over_z1(operand)  6.69 us
    ppermute x4, starting transfers between devices, send_first(): far_y[i] = over_y(value)  6.33 us
  transfers between devices with their start and end apart: 27, of which 8 were waited for; matrix products, arithmetic and copies ran while one was open for 1% of the time, Pallas kernels for 41%

profile of v2, /device:TPU:0, one launch (start us, length us, event | category | flops | bytes accessed | tf_op | source)
XLA Modules:
  0.0 170.6 jit_solution(16591396391112659286)
XLA Ops:
  2.0 3.1 %pick_features.1 = (bf16[128,1024]{1,0:T(8,128)(2,1)}, bf16[128,1024]{1,0:T(8,128)(2,1)}, bf16[128,1024]{1,0:T(8,128)(2,1)}, bf16[128,1024]{1,0:T(8,128)(2,1)}, bf16[128,1024]{1,0:T(8,128)(2,1)}) custom-call(s32[5]{0:T(128)} %stack.55.table, bf16[128,16384]{1,0:T(8,128)(2,1)} %refs_4_.1, bf16[128,16384]{1,0:T(8,128)(2,1)} %refs_4_.1, ...), custom_call_target="tpu_custom_call" | custom-call | tf_op jit(solution)/shard_map/pick_features/pallas_call | solution.py:83
  6.1 3.1 %take_tiles.2.refs_0_ = bf16[1024,1024]{1,0:T(8,128)(2,1)} custom-call(s32[1]{0:T(128)} %bitcast.4.table, bf16[1024,16384]{1,0:T(8,128)(2,1)} %refs_0_.17, bf16[128,1024]{1,0:T(8,128)(2,1)S(1)} %copy-done.3), custom_call_target="tpu_custom_call" | custom-call | tf_op jit(solution)/shard_map/take_tiles/pallas_call | solution.py:302
  9.7 3.0 %collective-permute-start.2 = (bf16[128,1024]{1,0:T(8,128)(2,1)S(1)}, bf16[128,1024]{1,0:T(8,128)(2,1)S(1)}, u32[]{:S(2)}, u32[]{:S(2)}) collective-permute-start(bf16[128,1024]{1,0:T(8,128)(2,1)S(1)} %copy-done.13), channel_id=1, source_target_pairs={{0,8},{8,0},{16,24},{24,16},{1,9},{9,1},{17,25},{25,17},{2,10},{10... | collective-permute-start | bytes 786440 | tf_op jit(solution)/shard_map/ppermute | solution.py:414
  12.7 2.5 %collective-permute-start.4 = (bf16[128,1024]{1,0:T(8,128)(2,1)S(1)}, bf16[128,1024]{1,0:T(8,128)(2,1)S(1)}, u32[]{:S(2)}, u32[]{:S(2)}) collective-permute-start(bf16[128,1024]{1,0:T(8,128)(2,1)S(1)} %copy-done.12), channel_id=1, source_target_pairs={{0,24},{8,16},{16,8},{24,0},{1,25},{9,17},{17,9},{25,1},{2,26},{10... | collective-permute-start | bytes 786440 | tf_op jit(solution)/shard_map/ppermute | solution.py:414
  15.6 7.0 %take_tiles.3.refs_6_ = bf16[1024,3072]{1,0:T(8,128)(2,1)} custom-call(s32[3]{0:T(128)S(1)} %pad_add_fusion.table, bf16[1024,16384]{1,0:T(8,128)(2,1)} %refs_0_.17, bf16[1024,1024]{1,0:T(8,128)(2,1)} %take_tiles.2.refs_0_, bf16[2048,32]{1,0:T(8,128)(2,1)S(1)} %copy.17.refs_1_.refs_4_.refs_2_), custom_call_target="tpu_custom_call" | custom-call | tf_op jit(solution)/shard_map/take_tiles/pallas_call | solution.py:302
  23.1 4.0 %collective-permute-done.4.refs_9_.refs_2_.refs_6_.refs_7_ = bf16[128,1024]{1,0:T(8,128)(2,1)S(1)} collective-permute-done((bf16[128,1024]{1,0:T(8,128)(2,1)S(1)}, bf16[128,1024]{1,0:T(8,128)(2,1)S(1)}, u32[]{:S(2)}, u32[]{:S(2)}) %collective-permute-start.4) | collective-permute-done | bytes 262176 | tf_op jit(solution)/shard_map/ppermute | solution.py:414
  27.3 1.9 %collective-permute-done.3.refs_8_.refs_1_.refs_5_.refs_6_ = bf16[128,1024]{1,0:T(8,128)(2,1)S(1)} collective-permute-done((bf16[128,1024]{1,0:T(8,128)(2,1)S(1)}, bf16[128,1024]{1,0:T(8,128)(2,1)S(1)}, u32[]{:S(2)}, u32[]{:S(2)}) %collective-permute-start.3) | collective-permute-done | bytes 262176 | tf_op jit(solution)/shard_map/ppermute | solution.py:415
  29.3 4.3 %collective-permute-done.5.refs_10_.refs_3_.refs_7_.refs_8_ = bf16[128,1024]{1,0:T(8,128)(2,1)S(1)} collective-permute-done((bf16[128,1024]{1,0:T(8,128)(2,1)S(1)}, bf16[128,1024]{1,0:T(8,128)(2,1)S(1)}, u32[]{:S(2)}, u32[]{:S(2)}) %collective-permute-start.5) | collective-permute-done | bytes 262176 | tf_op jit(solution)/shard_map/ppermute | solution.py:415
  33.5 9.4 %merge_pass.8 = (bf16[2048,1024]{1,0:T(8,128)(2,1)S(1)}, bf16[1024,2048]{1,0:T(8,128)(2,1)}, bf16[1024,2048]{1,0:T(8,128)(2,1)}) custom-call(s32[6]{0:T(128)S(1)} %concatenate.13.table, bf16[1024,16384]{1,0:T(8,128)(2,1)} %refs_0_.17, bf16[1024,16384]{1,0:T(8,128)(2,1)} %refs_0_.17, bf16[1024,16384]{1,0:T(8,128)(2,1)} %refs_0_.17, ...), custom_call_target="tpu_custom_call" | custom-call | bytes 8388608 | tf_op jit(solution)/shard_map/merge_pass/pallas_call | solution.py:248
  42.9 2.0 %copy-done.6 = bf16[2048,1024]{1,0:T(8,128)(2,1)} copy-done((bf16[2048,1024]{1,0:T(8,128)(2,1)}, bf16[2048,1024]{1,0:T(8,128)(2,1)S(1)}, u32[]{:S(2)}) %copy-start.6) | copy-done | bytes 4194328
  45.4 1.8 %collective-permute-start.8 = (bf16[128,1024]{1,0:T(8,128)(2,1)}, bf16[128,1024]{1,0:T(8,128)(2,1)S(1)}, u32[]{:S(2)}, u32[]{:S(2)}) collective-permute-start(bf16[128,1024]{1,0:T(8,128)(2,1)} %get-tuple-element.47), channel_id=1, source_target_pairs={{0,16},{8,24},{16,0},{24,8},{1,17},{9,25},{17,1},{25,9},{2,18},{10... | collective-permute-start | bytes 786440 | tf_op jit(solution)/shard_map/ppermute | solution.py:414
  47.4 2.2 %copy-done.7 = bf16[2048,1024]{1,0:T(8,128)(2,1)S(1)} copy-done((bf16[2048,1024]{1,0:T(8,128)(2,1)S(1)}, bf16[2048,1024]{1,0:T(8,128)(2,1)}, u32[]{:S(2)}) %copy-start.7) | copy-done | bytes 4194328
  49.5 2.4 %project.1 = (bf16[256,1024]{1,0:T(8,128)(2,1)S(1)}, bf16[256,1024]{1,0:T(8,128)(2,1)S(1)}) custom-call(bf16[2048,1024]{1,0:T(8,128)(2,1)S(1)} %copy-done.7, bf16[128,1024]{1,0:T(8,128)(2,1)S(1)} %collective-permute-done.2.refs_7_.refs_0_.refs_4_.refs_5_, bf16[128,1024]{1,0:T(8,128)(2,1)S(1)} %collective-permute-done.3.refs_8_.refs_1_.refs_5_.refs_6_, ...), custom_call_target="tpu_custom_call" | custom-call | flops 1610612736 | bytes 4194304 | tf_op jit(solution)/shard_map/project/pallas_call | solution.py:281
  53.5 7.0 %collective-permute-done.8.refs_11_ = bf16[128,1024]{1,0:T(8,128)(2,1)S(1)} collective-permute-done((bf16[128,1024]{1,0:T(8,128)(2,1)}, bf16[128,1024]{1,0:T(8,128)(2,1)S(1)}, u32[]{:S(2)}, u32[]{:S(2)}) %collective-permute-start.8) | collective-permute-done | bytes 262176 | tf_op jit(solution)/shard_map/ppermute | solution.py:414
  60.5 6.5 %merge_pass.9 = (bf16[2048,1024]{1,0:T(8,128)(2,1)S(1)}, bf16[256,1024]{1,0:T(8,128)(2,1)S(1)}, bf16[256,1024]{1,0:T(8,128)(2,1)S(1)}) custom-call(s32[2]{0:T(128)S(1)} %iota_add_fusion.3.table, bf16[1024,16384]{1,0:T(8,128)(2,1)} %refs_0_.17, bf16[1024,3072]{1,0:T(8,128)(2,1)} %collective-permute-done.7.refs_1_, ...), custom_call_target="tpu_custom_call" | custom-call | flops 1610612736 | bytes 8388608 | tf_op jit(solution)/shard_map/merge_pass/pallas_call | solution.py:248
  67.0 1.6 collective-permute-start.14
  68.6 7.0 %merge_pass.10 = (bf16[256,1024]{1,0:T(8,128)(2,1)S(1)}, bf16[256,1024]{1,0:T(8,128)(2,1)S(1)}, bf16[128,1024]{1,0:T(8,128)(2,1)S(1)}, bf16[128,1024]{1,0:T(8,128)(2,1)S(1)}) custom-call(s32[2]{0:T(128)S(1)} %iota_add_fusion.4.table, bf16[1024,16384]{1,0:T(8,128)(2,1)} %refs_0_.17, ...), custom_call_target="tpu_custom_call", output_to_operand_aliasing={{0}: (14, {})} | custom-call | flops 2147483648 | bytes 8388608 | tf_op jit(solution)/shard_map/merge_pass/pallas_call | solution.py:248
  77.1 6.2 %merge_pass.11 = (bf16[2048,1024]{1,0:T(8,128)(2,1)S(1)}, bf16[256,1024]{1,0:T(8,128)(2,1)S(1)}, bf16[256,1024]{1,0:T(8,128)(2,1)S(1)}) custom-call(s32[2]{0:T(128)S(1)} %iota_add_fusion.5.table, bf16[1024,16384]{1,0:T(8,128)(2,1)} %refs_0_.17, bf16[1024,3072]{1,0:T(8,128)(2,1)} %collective-permute-done.7.refs_1_, ...), custom_call_target="tpu_custom_call" | custom-call | flops 1610612736 | bytes 8388608 | tf_op jit(solution)/shard_map/merge_pass/pallas_call | solution.py:248
  83.3 1.6 collective-permute-start.15
  84.9 7.1 %merge_pass.12 = (bf16[256,1024]{1,0:T(8,128)(2,1)S(1)}, bf16[256,1024]{1,0:T(8,128)(2,1)S(1)}, bf16[128,1024]{1,0:T(8,128)(2,1)S(1)}, bf16[128,1024]{1,0:T(8,128)(2,1)S(1)}) custom-call(s32[2]{0:T(128)S(1)} %iota_add_fusion.1.table, bf16[1024,16384]{1,0:T(8,128)(2,1)} %refs_0_.17, ...), custom_call_target="tpu_custom_call", output_to_operand_aliasing={{0}: (14, {})} | custom-call | flops 2147483648 | bytes 8388608 | tf_op jit(solution)/shard_map/merge_pass/pallas_call | solution.py:248
  92.9 1.8 %collective-permute-start.17 = (bf16[256,1024]{1,0:T(8,128)(2,1)S(1)}, bf16[256,1024]{1,0:T(8,128)(2,1)S(1)}, u32[]{:S(2)}, u32[]{:S(2)}) collective-permute-start(bf16[256,1024]{1,0:T(8,128)(2,1)S(1)} %add_terms.9.refs_3_), channel_id=1, source_target_pairs={{0,8},{8,0},{16,24},{24,16},{1,9},{9,1},{17,25},{25,17},{2,10},{10... | collective-permute-start | bytes 1572872 | tf_op jit(solution)/shard_map/ppermute | solution.py:490
  94.9 1.6 collective-permute-start.18
  96.6 6.2 %merge_pass.13 = (bf16[2048,1024]{1,0:T(8,128)(2,1)S(1)}, bf16[256,1024]{1,0:T(8,128)(2,1)S(1)}, bf16[256,1024]{1,0:T(8,128)(2,1)S(1)}) custom-call(s32[2]{0:T(128)S(1)} %iota_add_fusion.2.table, bf16[1024,16384]{1,0:T(8,128)(2,1)} %refs_0_.17, bf16[1024,2048]{1,0:T(8,128)(2,1)} %collective-permute-done.11.refs_1_, ...), custom_call_target="tpu_custom_call" | custom-call | flops 1610612736 | bytes 8388608 | tf_op jit(solution)/shard_map/merge_pass/pallas_call | solution.py:248
  102.8 1.6 collective-permute-start.20
  104.4 7.2 %merge_pass.14 = (bf16[256,1024]{1,0:T(8,128)(2,1)S(1)}, bf16[256,1024]{1,0:T(8,128)(2,1)S(1)}, bf16[128,1024]{1,0:T(8,128)(2,1)S(1)}, bf16[128,1024]{1,0:T(8,128)(2,1)S(1)}) custom-call(s32[2]{0:T(128)S(1)} %iota_add_fusion.7.table, bf16[1024,16384]{1,0:T(8,128)(2,1)} %refs_0_.17, ...), custom_call_target="tpu_custom_call", output_to_operand_aliasing={{0}: (14, {})} | custom-call | flops 2147483648 | bytes 8388608 | tf_op jit(solution)/shard_map/merge_pass/pallas_call | solution.py:248
  113.4 2.0 %collective-permute-start.23 = (bf16[256,1024]{1,0:T(8,128)(2,1)S(1)}, bf16[256,1024]{1,0:T(8,128)(2,1)S(1)}, u32[]{:S(2)}, u32[]{:S(2)}) collective-permute-start(bf16[256,1024]{1,0:T(8,128)(2,1)S(1)} %add_terms.11.refs_4_), channel_id=1, source_target_pairs={{0,8},{8,0},{16,24},{24,16},{1,9},{9,1},{17,25},{25,17},{2,10},{10... | collective-permute-start | bytes 1572872 | tf_op jit(solution)/shard_map/ppermute | solution.py:490
  118.1 7.0 %merge_pass.15 = (bf16[256,1024]{1,0:T(8,128)(2,1)S(1)}, bf16[256,1024]{1,0:T(8,128)(2,1)S(1)}, bf16[128,1024]{1,0:T(8,128)(2,1)S(1)}, bf16[128,1024]{1,0:T(8,128)(2,1)S(1)}) custom-call(s32[2]{0:T(128)S(1)} %iota_add_fusion.table, bf16[1024,16384]{1,0:T(8,128)(2,1)} %refs_0_.17, ...), custom_call_target="tpu_custom_call", output_to_operand_aliasing={{0}: (14, {})} | custom-call | flops 2147483648 | bytes 8388608 | tf_op jit(solution)/shard_map/merge_pass/pallas_call | solution.py:248
  127.0 2.5 %collective-permute-start.21 = (bf16[256,1024]{1,0:T(8,128)(2,1)S(1)}, bf16[256,1024]{1,0:T(8,128)(2,1)S(1)}, u32[]{:S(2)}, u32[]{:S(2)}) collective-permute-start(bf16[256,1024]{1,0:T(8,128)(2,1)S(1)} %add_terms.13.refs_5_), channel_id=1, source_target_pairs={{0,8},{8,0},{16,24},{24,16},{1,9},{9,1},{17,25},{25,17},{2,10},{10... | collective-permute-start | bytes 1572872 | tf_op jit(solution)/shard_map/ppermute | solution.py:490
  129.5 2.9 %collective-permute-done.24.refs_3_ = bf16[128,1024]{1,0:T(8,128)(2,1)S(1)} collective-permute-done((bf16[128,1024]{1,0:T(8,128)(2,1)S(1)}, bf16[128,1024]{1,0:T(8,128)(2,1)S(1)}, u32[]{:S(2)}, u32[]{:S(2)}) %collective-permute-start.24) | collective-permute-done | bytes 262176 | tf_op jit(solution)/shard_map/ppermute | solution.py:495
  133.4 4.6 %collective-permute-done.22.refs_1_ = bf16[256,1024]{1,0:T(8,128)(2,1)S(1)} collective-permute-done((bf16[256,1024]{1,0:T(8,128)(2,1)S(1)}, bf16[256,1024]{1,0:T(8,128)(2,1)S(1)}, u32[]{:S(2)}, u32[]{:S(2)}) %collective-permute-start.22) | collective-permute-done | bytes 524320 | tf_op jit(solution)/shard_map/ppermute | solution.py:485
  139.5 14.1 %collective-permute-done.25.refs_3_ = bf16[128,1024]{1,0:T(8,128)(2,1)S(1)} collective-permute-done((bf16[128,1024]{1,0:T(8,128)(2,1)S(1)}, bf16[128,1024]{1,0:T(8,128)(2,1)S(1)}, u32[]{:S(2)}, u32[]{:S(2)}) %collective-permute-start.25) | collective-permute-done | bytes 262176 | tf_op jit(solution)/shard_map/ppermute | solution.py:495
  156.1 13.5 %collective-permute-done.26.refs_3_ = bf16[128,1024]{1,0:T(8,128)(2,1)S(1)} collective-permute-done((bf16[128,1024]{1,0:T(8,128)(2,1)S(1)}, bf16[128,1024]{1,0:T(8,128)(2,1)S(1)}, u32[]{:S(2)}, u32[]{:S(2)}) %collective-permute-start.26) | collective-permute-done | bytes 262176 | tf_op jit(solution)/shard_map/ppermute | solution.py:495
  (97 shorter events, 21.6 us)
Async XLA Ops:
  9.1 24.4 %collective-permute-start = (bf16[1024,1024]{1,0:T(8,128)(2,1)}, bf16[1024,1024]{1,0:T(8,128)(2,1)}, u32[]{:S(2)}, u32[]{:S(2)}) collective-permute-start(bf16[1024,1024]{1,0:T(8,128)(2,1)} %take_tiles.2.refs_0_), channel_id=1, source_target_pairs={{0,2},{2,0},{4,6},{6,4},{1,3},{3,1},{5,7},{7,5},{8,10},{10,8},{12,... | collective-permute-start | bytes 6291464 | tf_op jit(solution)/shard_map/ppermute | solution.py:432
  9.6 5.6 %collective-permute-start.1 = (bf16[1024,32]{0,1:T(8,128)(2,1)S(1)}, bf16[1024,32]{0,1:T(8,128)(2,1)S(1)}, u32[]{:S(2)}, u32[]{:S(2)}) collective-permute-start(bf16[1024,32]{0,1:T(8,128)(2,1)S(1)} %copy-done.11), channel_id=1, source_target_pairs={{0,2},{2,0},{4,6},{6,4},{1,3},{3,1},{5,7},{7,5},{8,10},{10,8},{12,... | collective-permute-start | bytes 196616 | tf_op jit(solution)/shard_map/ppermute | solution.py:418
  9.7 13.0 %collective-permute-start.2 = (bf16[128,1024]{1,0:T(8,128)(2,1)S(1)}, bf16[128,1024]{1,0:T(8,128)(2,1)S(1)}, u32[]{:S(2)}, u32[]{:S(2)}) collective-permute-start(bf16[128,1024]{1,0:T(8,128)(2,1)S(1)} %copy-done.13), channel_id=1, source_target_pairs={{0,8},{8,0},{16,24},{24,16},{1,9},{9,1},{17,25},{25,17},{2,10},{10... | collective-permute-start | bytes 786440 | tf_op jit(solution)/shard_map/ppermute | solution.py:414
  12.7 14.5 %collective-permute-start.4 = (bf16[128,1024]{1,0:T(8,128)(2,1)S(1)}, bf16[128,1024]{1,0:T(8,128)(2,1)S(1)}, u32[]{:S(2)}, u32[]{:S(2)}) collective-permute-start(bf16[128,1024]{1,0:T(8,128)(2,1)S(1)} %copy-done.12), channel_id=1, source_target_pairs={{0,24},{8,16},{16,8},{24,0},{1,25},{9,17},{17,9},{25,1},{2,26},{10... | collective-permute-start | bytes 786440 | tf_op jit(solution)/shard_map/ppermute | solution.py:414
  15.5 11.6 %copy-start.10 = (bf16[32,16384]{1,0:T(8,128)(2,1)S(1)}, bf16[32,16384]{1,0:T(8,128)(2,1)}, u32[]{:S(2)}) copy-start(bf16[32,16384]{1,0:T(8,128)(2,1)} %param.9) | copy-start | bytes 3145732
  15.5 18.0 %copy-start.4 = (bf16[128,1024]{1,0:T(8,128)(2,1)S(1)}, bf16[128,1024]{1,0:T(8,128)(2,1)}, u32[]{:S(2)}) copy-start(bf16[128,1024]{1,0:T(8,128)(2,1)} %get-tuple-element.41.refs_0_.refs_11_.refs_4_.refs_8_.refs_9_) | copy-start | bytes 786436
  15.6 18.0 %copy-start.5 = (bf16[128,1024]{1,0:T(8,128)(2,1)S(1)}, bf16[128,1024]{1,0:T(8,128)(2,1)}, u32[]{:S(2)}) copy-start(bf16[128,1024]{1,0:T(8,128)(2,1)} %get-tuple-element.44.refs_12_.refs_5_.refs_9_.refs_10_) | copy-start | bytes 786436
  22.6 37.9 %collective-permute-start.7 = (bf16[1024,3072]{1,0:T(8,128)(2,1)}, bf16[1024,3072]{1,0:T(8,128)(2,1)}, u32[]{:S(2)}, u32[]{:S(2)}) collective-permute-start(bf16[1024,3072]{1,0:T(8,128)(2,1)} %take_tiles.3.refs_6_), channel_id=1, source_target_pairs={{0,2},{2,0},{4,6},{6,4},{1,3},{3,1},{5,7},{7,5},{8,10},{10,8},{12,... | collective-permute-start | bytes 18874376 | tf_op jit(solution)/shard_map/ppermute | solution.py:432
  22.6 6.6 %collective-permute-start.3 = (bf16[128,1024]{1,0:T(8,128)(2,1)S(1)}, bf16[128,1024]{1,0:T(8,128)(2,1)S(1)}, u32[]{:S(2)}, u32[]{:S(2)}) collective-permute-start(bf16[128,1024]{1,0:T(8,128)(2,1)S(1)} %collective-permute-done.2.refs_7_.refs_0_.refs_4_.refs_5_), channel_id=1, source_target_pairs={{0,2},{2,0},{4,6},{6,4},{1,3},{3,1},{5,7},{7,5},{8,10},{10,8},{12,... | collective-permute-start | bytes 786440 | tf_op jit(solution)/shard_map/ppermute | solution.py:415
  27.1 6.4 %collective-permute-start.5 = (bf16[128,1024]{1,0:T(8,128)(2,1)S(1)}, bf16[128,1024]{1,0:T(8,128)(2,1)S(1)}, u32[]{:S(2)}, u32[]{:S(2)}) collective-permute-start(bf16[128,1024]{1,0:T(8,128)(2,1)S(1)} %collective-permute-done.4.refs_9_.refs_2_.refs_6_.refs_7_), channel_id=1, source_target_pairs={{0,2},{2,0},{4,6},{6,4},{1,3},{3,1},{5,7},{7,5},{8,10},{10,8},{12,... | collective-permute-start | bytes 786440 | tf_op jit(solution)/shard_map/ppermute | solution.py:415
  33.5 13.7 %copy-start.14 = (s32[128]{0:T(128)S(1)}, s32[128]{0:T(128)}, u32[]{:S(2)}) copy-start(s32[128]{0:T(128)} %param.11) | copy-start | bytes 1540
  44.9 23.7 %collective-permute-start.6 = (bf16[1024,2048]{1,0:T(8,128)(2,1)}, bf16[1024,2048]{1,0:T(8,128)(2,1)}, u32[]{:S(2)}, u32[]{:S(2)}) collective-permute-start(bf16[1024,2048]{1,0:T(8,128)(2,1)} %get-tuple-element.45), channel_id=1, source_target_pairs={{0,2},{2,0},{4,6},{6,4},{1,3},{3,1},{5,7},{7,5},{8,10},{10,8},{12,... | collective-permute-start | bytes 12582920 | tf_op jit(solution)/shard_map/ppermute | solution.py:432
  45.1 39.8 %collective-permute-start.11 = (bf16[1024,2048]{1,0:T(8,128)(2,1)}, bf16[1024,2048]{1,0:T(8,128)(2,1)}, u32[]{:S(2)}, u32[]{:S(2)}) collective-permute-start(bf16[1024,2048]{1,0:T(8,128)(2,1)} %get-tuple-element.55), channel_id=1, source_target_pairs={{0,2},{2,0},{4,6},{6,4},{1,3},{3,1},{5,7},{7,5},{8,10},{10,8},{12,... | collective-permute-start | bytes 12582920 | tf_op jit(solution)/shard_map/ppermute | solution.py:432
  45.4 15.1 %collective-permute-start.8 = (bf16[128,1024]{1,0:T(8,128)(2,1)}, bf16[128,1024]{1,0:T(8,128)(2,1)S(1)}, u32[]{:S(2)}, u32[]{:S(2)}) collective-permute-start(bf16[128,1024]{1,0:T(8,128)(2,1)} %get-tuple-element.47), channel_id=1, source_target_pairs={{0,16},{8,24},{16,0},{24,8},{1,17},{9,25},{17,1},{25,9},{2,18},{10... | collective-permute-start | bytes 786440 | tf_op jit(solution)/shard_map/ppermute | solution.py:414
  52.0 24.2 %collective-permute-start.10 = (bf16[256,1024]{1,0:T(8,128)(2,1)S(1)}, bf16[256,1024]{1,0:T(8,128)(2,1)S(1)}, u32[]{:S(2)}, u32[]{:S(2)}) collective-permute-start(bf16[256,1024]{1,0:T(8,128)(2,1)S(1)} %get-tuple-element.49.refs_10_), channel_id=1, source_target_pairs={{0,4},{2,6},{4,0},{6,2},{1,5},{3,7},{5,1},{7,3},{8,12},{10,14},{12... | collective-permute-start | bytes 1572872 | tf_op jit(solution)/shard_map/ppermute | solution.py:471
  60.5 8.1 %collective-permute-start.9 = (bf16[128,1024]{1,0:T(8,128)(2,1)S(1)}, bf16[128,1024]{1,0:T(8,128)(2,1)S(1)}, u32[]{:S(2)}, u32[]{:S(2)}) collective-permute-start(bf16[128,1024]{1,0:T(8,128)(2,1)S(1)} %collective-permute-done.8.refs_11_), channel_id=1, source_target_pairs={{0,2},{2,0},{4,6},{6,4},{1,3},{3,1},{5,7},{7,5},{8,10},{10,8},{12,... | collective-permute-start | bytes 786440 | tf_op jit(solution)/shard_map/ppermute | solution.py:416
  67.0 25.6 %collective-permute-start.14 = (bf16[256,1024]{1,0:T(8,128)(2,1)S(1)}, bf16[256,1024]{1,0:T(8,128)(2,1)S(1)}, u32[]{:S(2)}, u32[]{:S(2)}) collective-permute-start(bf16[256,1024]{1,0:T(8,128)(2,1)S(1)} %get-tuple-element.50.refs_14_), channel_id=1, source_target_pairs={{0,4},{2,6},{4,0},{6,2},{1,5},{3,7},{5,1},{7,3},{8,12},{10,14},{12... | collective-permute-start | bytes 1572872 | tf_op jit(solution)/shard_map/ppermute | solution.py:471
  75.6 19.1 %collective-permute-start.12 = (bf16[256,1024]{1,0:T(8,128)(2,1)S(1)}, bf16[256,1024]{1,0:T(8,128)(2,1)S(1)}, u32[]{:S(2)}, u32[]{:S(2)}) collective-permute-start(bf16[256,1024]{1,0:T(8,128)(2,1)S(1)} %get-tuple-element.52.refs_2_), channel_id=1, source_target_pairs={{0,4},{2,6},{4,0},{6,2},{1,5},{3,7},{5,1},{7,3},{8,12},{10,14},{12... | collective-permute-start | bytes 1572872 | tf_op jit(solution)/shard_map/ppermute | solution.py:485
  76.5 18.3 %collective-permute-start.13 = (bf16[256,1024]{1,0:T(8,128)(2,1)S(1)}, bf16[256,1024]{1,0:T(8,128)(2,1)S(1)}, u32[]{:S(2)}, u32[]{:S(2)}) collective-permute-start(bf16[256,1024]{1,0:T(8,128)(2,1)S(1)} %add_terms.8.refs_10_), channel_id=1, source_target_pairs={{0,8},{8,0},{16,24},{24,16},{1,9},{9,1},{17,25},{25,17},{2,10},{10... | collective-permute-start | bytes 1572872 | tf_op jit(solution)/shard_map/ppermute | solution.py:490
  83.3 28.3 %collective-permute-start.15 = (bf16[256,1024]{1,0:T(8,128)(2,1)S(1)}, bf16[256,1024]{1,0:T(8,128)(2,1)S(1)}, u32[]{:S(2)}, u32[]{:S(2)}) collective-permute-start(bf16[256,1024]{1,0:T(8,128)(2,1)S(1)} %get-tuple-element.59.refs_14_), channel_id=1, source_target_pairs={{0,4},{2,6},{4,0},{6,2},{1,5},{3,7},{5,1},{7,3},{8,12},{10,14},{12... | collective-permute-start | bytes 1572872 | tf_op jit(solution)/shard_map/ppermute | solution.py:471
  92.0 24.5 %collective-permute-start.16 = (bf16[256,1024]{1,0:T(8,128)(2,1)S(1)}, bf16[256,1024]{1,0:T(8,128)(2,1)S(1)}, u32[]{:S(2)}, u32[]{:S(2)}) collective-permute-start(bf16[256,1024]{1,0:T(8,128)(2,1)S(1)} %get-tuple-element.61.refs_2_), channel_id=1, source_target_pairs={{0,4},{2,6},{4,0},{6,2},{1,5},{3,7},{5,1},{7,3},{8,12},{10,14},{12... | collective-permute-start | bytes 1572872 | tf_op jit(solution)/shard_map/ppermute | solution.py:485
  92.9 23.7 %collective-permute-start.17 = (bf16[256,1024]{1,0:T(8,128)(2,1)S(1)}, bf16[256,1024]{1,0:T(8,128)(2,1)S(1)}, u32[]{:S(2)}, u32[]{:S(2)}) collective-permute-start(bf16[256,1024]{1,0:T(8,128)(2,1)S(1)} %add_terms.9.refs_3_), channel_id=1, source_target_pairs={{0,8},{8,0},{16,24},{24,16},{1,9},{9,1},{17,25},{25,17},{2,10},{10... | collective-permute-start | bytes 1572872 | tf_op jit(solution)/shard_map/ppermute | solution.py:490
  94.9 18.5 %collective-permute-start.18 = (bf16[128,1024]{1,0:T(8,128)(2,1)S(1)}, bf16[128,1024]{1,0:T(8,128)(2,1)S(1)}, u32[]{:S(2)}, u32[]{:S(2)}) collective-permute-start(bf16[128,1024]{1,0:T(8,128)(2,1)S(1)} %add_terms.10.refs_10_), channel_id=1, source_target_pairs={{0,16},{8,24},{16,0},{24,8},{1,17},{9,25},{17,1},{25,9},{2,18},{10... | collective-permute-start | bytes 786440 | tf_op jit(solution)/shard_map/ppermute | solution.py:495
  102.8 23.9 %collective-permute-start.20 = (bf16[256,1024]{1,0:T(8,128)(2,1)S(1)}, bf16[256,1024]{1,0:T(8,128)(2,1)S(1)}, u32[]{:S(2)}, u32[]{:S(2)}) collective-permute-start(bf16[256,1024]{1,0:T(8,128)(2,1)S(1)} %get-tuple-element.62.refs_14_), channel_id=1, source_target_pairs={{0,4},{2,6},{4,0},{6,2},{1,5},{3,7},{5,1},{7,3},{8,12},{10,14},{12... | collective-permute-start | bytes 1572872 | tf_op jit(solution)/shard_map/ppermute | solution.py:471
  104.4 8.1 %copy-start.9 = (bf16[128,16384]{1,0:T(8,128)(2,1)S(1)}, bf16[128,16384]{1,0:T(8,128)(2,1)}, u32[]{:S(2)}) copy-start(bf16[128,16384]{1,0:T(8,128)(2,1)} %refs_4_.1) | copy-start | bytes 12582916
  111.6 26.3 %collective-permute-start.22 = (bf16[256,1024]{1,0:T(8,128)(2,1)S(1)}, bf16[256,1024]{1,0:T(8,128)(2,1)S(1)}, u32[]{:S(2)}, u32[]{:S(2)}) collective-permute-start(bf16[256,1024]{1,0:T(8,128)(2,1)S(1)} %get-tuple-element.64.refs_2_), channel_id=1, source_target_pairs={{0,4},{2,6},{4,0},{6,2},{1,5},{3,7},{5,1},{7,3},{8,12},{10,14},{12... | collective-permute-start | bytes 1572872 | tf_op jit(solution)/shard_map/ppermute | solution.py:485
  113.4 24.6 %collective-permute-start.23 = (bf16[256,1024]{1,0:T(8,128)(2,1)S(1)}, bf16[256,1024]{1,0:T(8,128)(2,1)S(1)}, u32[]{:S(2)}, u32[]{:S(2)}) collective-permute-start(bf16[256,1024]{1,0:T(8,128)(2,1)S(1)} %add_terms.11.refs_4_), channel_id=1, source_target_pairs={{0,8},{8,0},{16,24},{24,16},{1,9},{9,1},{17,25},{25,17},{2,10},{10... | collective-permute-start | bytes 1572872 | tf_op jit(solution)/shard_map/ppermute | solution.py:490
  118.0 14.3 %collective-permute-start.24 = (bf16[128,1024]{1,0:T(8,128)(2,1)S(1)}, bf16[128,1024]{1,0:T(8,128)(2,1)S(1)}, u32[]{:S(2)}, u32[]{:S(2)}) collective-permute-start(bf16[128,1024]{1,0:T(8,128)(2,1)S(1)} %add_terms.12.refs_14_), channel_id=1, source_target_pairs={{0,16},{8,24},{16,0},{24,8},{1,17},{9,25},{17,1},{25,9},{2,18},{10... | collective-permute-start | bytes 786440 | tf_op jit(solution)/shard_map/ppermute | solution.py:495
  125.1 29.4 %collective-permute-start.19 = (bf16[256,1024]{1,0:T(8,128)(2,1)S(1)}, bf16[256,1024]{1,0:T(8,128)(2,1)S(1)}, u32[]{:S(2)}, u32[]{:S(2)}) collective-permute-start(bf16[256,1024]{1,0:T(8,128)(2,1)S(1)} %get-tuple-element.71.refs_2_), channel_id=1, source_target_pairs={{0,4},{2,6},{4,0},{6,2},{1,5},{3,7},{5,1},{7,3},{8,12},{10,14},{12... | collective-permute-start | bytes 1572872 | tf_op jit(solution)/shard_map/ppermute | solution.py:485
  127.0 27.6 %collective-permute-start.21 = (bf16[256,1024]{1,0:T(8,128)(2,1)S(1)}, bf16[256,1024]{1,0:T(8,128)(2,1)S(1)}, u32[]{:S(2)}, u32[]{:S(2)}) collective-permute-start(bf16[256,1024]{1,0:T(8,128)(2,1)S(1)} %add_terms.13.refs_5_), channel_id=1, source_target_pairs={{0,8},{8,0},{16,24},{24,16},{1,9},{9,1},{17,25},{25,17},{2,10},{10... | collective-permute-start | bytes 1572872 | tf_op jit(solution)/shard_map/ppermute | solution.py:490
  139.4 14.1 %collective-permute-start.25 = (bf16[128,1024]{1,0:T(8,128)(2,1)S(1)}, bf16[128,1024]{1,0:T(8,128)(2,1)S(1)}, u32[]{:S(2)}, u32[]{:S(2)}) collective-permute-start(bf16[128,1024]{1,0:T(8,128)(2,1)S(1)} %add_terms.14.refs_5_), channel_id=1, source_target_pairs={{0,16},{8,24},{16,0},{24,8},{1,17},{9,25},{17,1},{25,9},{2,18},{10... | collective-permute-start | bytes 786440 | tf_op jit(solution)/shard_map/ppermute | solution.py:495
  156.0 13.6 %collective-permute-start.26 = (bf16[128,1024]{1,0:T(8,128)(2,1)S(1)}, bf16[128,1024]{1,0:T(8,128)(2,1)S(1)}, u32[]{:S(2)}, u32[]{:S(2)}) collective-permute-start(bf16[128,1024]{1,0:T(8,128)(2,1)S(1)} %add_terms.15.refs_5_), channel_id=1, source_target_pairs={{0,16},{8,24},{16,0},{24,8},{1,17},{9,25},{17,1},{25,9},{2,18},{10... | collective-permute-start | bytes 786440 | tf_op jit(solution)/shard_map/ppermute | solution.py:495
  (10 other events, 30.7 us)

commit v3 on v2

--- a/solution.py
+++ b/solution.py
@@ -89,7 +89,7 @@
             out_specs=[pl.BlockSpec((tokens, width), lambda step, table: (0, 0))] * count,
         ),
         out_shape=[like((tokens, width))] * count,
-        compiler_params=params(60),
+        compiler_params=params(12),
         name="pick_features",
     )(table, *([hidden] * count), *([norm_gain] * count))
 
@@ -238,12 +238,12 @@
         pltpu.VMEM((2, depth // BLOCK, width), jnp.float32),
     ]
     if keep:
-        out_shape.insert(0, like((depth, steps * width)))
+        out_shape.insert(0, pltpu.HBM((depth, steps * width), jnp.bfloat16))
         out_specs.insert(0, tile(depth, 0))
     else:
         scratch.insert(0, pltpu.VMEM((depth, width), jnp.bfloat16))
     if carry is not None:
-        out_shape += [like((block[0], steps * span))] * carried
+        out_shape += [pltpu.HBM((block[0], steps * span), jnp.bfloat16)] * carried
         out_specs += [pl.BlockSpec(block, lambda i, table: (0, i))] * carried
     return pl.pallas_call(
         functools.partial(
@@ -265,34 +265,6 @@
     )(table, *operands)
 
 
-def project_kernel(shape, after, outs, weight, *refs):
-    lines, refs = split_lines(refs, shape)
-    outs, x = refs[after : after + outs], refs[-1]
-    gather_features(lines, x)
-    store_rows(jnp.dot(x[...], weight[...], preferred_element_type=jnp.float32), outs)
-
-
-def project(weight, steps, lines, out_rows, after=()):
-    depth, columns = weight.shape
-    width = columns // steps
-    tokens = sum(line[0].shape[0] for line in lines)
-    pieces = [piece for line in lines for piece in line]
-    out_shape, out_specs = row_outs(out_rows, steps, width)
-    return pl.pallas_call(
-        functools.partial(project_kernel, [len(line) for line in lines], len(after), len(out_rows)),
-        grid=(steps,),
-        in_specs=[pl.BlockSpec((depth, width), lambda i: (0, i))]
-        + [pl.BlockSpec(piece.shape, lambda i: (0, 0)) for piece in pieces]
-        + [ANY] * len(after),
-        out_specs=out_specs,
-        out_shape=out_shape,
-        scratch_shapes=[pltpu.VMEM((tokens, depth), jnp.bfloat16)],
-        cost_estimate=cost(2 * tokens * depth * columns, 2 * depth * columns),
-        compiler_params=params(20),
-        name="project",
-    )(weight, *pieces, *after)
-
-
 def take_kernel(table, values, *refs):
     refs[-1][...] = values[...]
 
@@ -308,7 +280,7 @@
             + [ANY] * len(after),
             out_specs=pl.BlockSpec((rows, width), lambda i, table: (0, i)),
         ),
-        out_shape=like((rows, steps * width)),
+        out_shape=pltpu.HBM((rows, steps * width), jnp.bfloat16),
         compiler_params=params(40),
         name="take_tiles",
     )(table, values, *after)
@@ -413,7 +385,6 @@
     )
     x1, x2, x3 = over("fsdp", 1)(p1), over("fsdp", 2)(p2), over("fsdp", 3)(p3)
     first_lines = [[x1, over_core(x1)], [x3, over_core(x3)], [own_x, own_other]]
-    all_lines = [*first_lines, [x2, over_core(x2)]]
 
     down2 = jnp.concatenate([down, over_core(down)], axis=0)
     up2 = up * jnp.bfloat16(adapter_scale)
@@ -463,19 +434,12 @@
     weights, halves, far_y, mid_y = {}, {}, {}, {}
     near, own, far, near_z, far_z = {}, {}, {}, {}, {}
 
-    def weigh(i, after, carried=()):
-        (weights[i],) = run_pass(other_chip, i, "y", carried, keep=True, after=after)
-
-    def send_first(i, outs):
-        value, halves[i] = outs
+    def first(i, after, carried=()):
+        weights[i], value, halves[i] = run_pass(
+            other_chip, i, "y", carried, lines=first_lines, out_rows=first_rows, keep=True, after=after
+        )
         far_y[i] = over_y(value)
         return value
-
-    def first(i, after):
-        weights[i], *outs = run_pass(
-            other_chip, i, "y", (), lines=first_lines, out_rows=first_rows, keep=True, after=after
-        )
-        return send_first(i, outs)
 
     def second(i, after):
         half, near[i], own[i], far[i] = run_pass(
@@ -499,28 +463,27 @@
         terms = [(own[i], 0), (mid_y[i], 0), (near_z[i], 0), (far_z[i], 0)]
         return turn(cosine, sine_part, terms, i * piece, quarter, out, after)
 
-    early_xs = sum(first_lines, [])
-    weigh(0, (taken, *early_xs), [[("own", 1), ("y", 3)], [("own", 2), ("own", 3)]])
-    done = send_first(0, project(weights[0], steps, first_lines, first_rows))
-    done = first(1, (done,))
-    done = second(0, (done, received["own", 2][0]))
+    done = first(0, (taken,), [[("own", 1), ("y", 3)], [("own", 2), ("own", 3)]])
+    k1 = first(1, (done,))
+    done = first(2, (k1,))
+    all_lines = [*first_lines, [x2, over_core(lax.optimization_barrier((x2, k1))[0])]]
+    done = second(0, (done, received["own", 1][0], received["own", 2][0], far_y[0]))
     done = to_z1(0, (done,))
-    done = first(2, (done,))
-    done = second(1, (done,))
+    done = second(1, (done, far_y[1]))
     done = to_z1(1, (done,))
+    done = first(3, (done, far_y[2]))
     done = to_z2(0, (done,))
-    done = first(3, (done,))
     done = second(2, (done,))
-    done = to_z1(2, (done,))
     cosine, sine_part = turn_tables(lax.optimization_barrier((hidden, done))[0], positions)
     out = finish(0, None, (done,))
     done = to_z2(1, (out,))
-    done = second(3, (done,))
+    done = to_z1(2, (done,))
+    done = second(3, (done, far_y[3]))
     done = to_z1(3, (done,))
     out = finish(1, out, (done,))
     done = to_z2(2, (out,))
+    done = to_z2(3, (done,))
     out = finish(2, out, (done,))
-    done = to_z2(3, (out,))
     return finish(3, out, (done,))
 
 

time: 171 us -> 170 us (level)
  waiting for transfers between devices: 52.3 us -> 55.2 us
  starting transfers between devices: 27.1 us -> 24.9 us
    ppermute x4, waiting for transfers between devices: 30.4 us -> 37.8 us  [to_z2(): far_z[i] = over_z2(operand)]
    ppermute x3, waiting for transfers between devices: 11 us -> 5.42 us  [line_shards(): x1, x2, x3 = (over('fsdp', 1)(p1), over('fsdp', 2)(p2), over('fsdp', 3)(p3))]
    ppermute x5, waiting for transfers between devices: 0.04 us -> 5.37 us  [the longest x4 5.36 us: first(): far_y[i] = over_y(value)]
    ppermute x4, waiting for transfers between devices: 4.59 us -> 0.01 us  [second(): mid_y[i] = over_y(half)]
    ppermute x4, starting transfers between devices: 6.69 us -> 2.29 us  [to_z1(): near_z[i] = over_z1(operand)]
    ppermute x4, starting transfers between devices: 1.87 us -> 5.31 us  [to_z2(): far_z[i] = over_z2(operand)]
    pallas_call x8, Pallas kernels: 56.6 us -> 59.7 us  [merge_pass(): pl.pallas_call(functools.partial(pass_kernel, len(bases), [len(line) for...]
    pallas_call x1 -> x0, Pallas kernels: 2.4 us -> none  [project(): pl.pallas_call(functools.partial(project_kernel, [len(line) for line in l...]
  transfers between devices with their start and end apart: 27 -> 27, of which waited for: 8 -> 8; matrix products, arithmetic and copies ran while one was open for 1% -> 2% of each run, Pallas kernels for 41% -> 45%
where the time goes in v3:
time: 170 us; the launch traced here: 169 us
  Pallas kernels  77.2 us (45%)
  waiting for transfers between devices  55.2 us (32%)
  starting transfers between devices  24.9 us (15%)
  local copies, waits for them, and re-layouts  10.2 us (6%)
    pallas_call x8, Pallas kernels, merge_pass(): pl.pallas_call(functools.partial(pass_kernel, len(bases), [len(line) for...  59.7 us
    ppermute x4, waiting for transfers between devices, to_z2(): far_z[i] = over_z2(operand)  37.8 us
    pallas_call x2, Pallas kernels, take_tiles(): pl.pallas_call(take_kernel, grid_spec=pltpu.PrefetchScalarGridSpec(num_sc...  10.1 us
    unnamed x32, local copies, waits for them, and re-layouts  8.94 us
    ppermute x2, waiting for transfers between devices, line_shards(): first_lines = [[x1, over_core(x1)], [x3, over_core(x3)], [own_x, own_other]]  6.56 us
    ppermute x3, waiting for transfers between devices, line_shards(): x1, x2, x3 = (over('fsdp', 1)(p1), over('fsdp', 2)(p2), over('fsdp', 3)(p3))  5.42 us
    ppermute x4, waiting for transfers between devices, first(): far_y[i] = over_y(value)  5.36 us
    ppermute x4, starting transfers between devices, to_z2(): far_z[i] = over_z2(operand)  5.31 us
  transfers between devices with their start and end apart: 27, of which 8 were waited for; matrix products, arithmetic and copies ran while one was open for 2% of the time, Pallas kernels for 45%

profile of v3, /device:TPU:0, one launch (start us, length us, event | category | flops | bytes accessed | tf_op | source)
XLA Modules:
  0.0 169.4 jit_solution(2916895480216504435)
XLA Ops:
  1.3 2.2 %copy-done = bf16[128,16384]{1,0:T(8,128)(2,1)S(1)} copy-done((bf16[128,16384]{1,0:T(8,128)(2,1)S(1)}, bf16[128,16384]{1,0:T(8,128)(2,1)}, u32[]{:S(2)}) %copy-start) | copy-done | bytes 4194328
  3.5 1.3 pick_features.1
  4.8 2.6 %collective-permute-start.2 = (bf16[128,1024]{1,0:T(8,128)(2,1)S(1)}, bf16[128,1024]{1,0:T(8,128)(2,1)S(1)}, u32[]{:S(2)}, u32[]{:S(2)}) collective-permute-start(bf16[128,1024]{1,0:T(8,128)(2,1)S(1)} %get-tuple-element.43), channel_id=1, source_target_pairs={{0,8},{8,0},{16,24},{24,16},{1,9},{9,1},{17,25},{25,17},{2,10},{10... | collective-permute-start | bytes 786440 | tf_op jit(solution)/shard_map/ppermute | solution.py:386
  7.4 2.5 %collective-permute-start.4 = (bf16[128,1024]{1,0:T(8,128)(2,1)S(1)}, bf16[128,1024]{1,0:T(8,128)(2,1)S(1)}, u32[]{:S(2)}, u32[]{:S(2)}) collective-permute-start(bf16[128,1024]{1,0:T(8,128)(2,1)S(1)} %get-tuple-element.44), channel_id=1, source_target_pairs={{0,24},{8,16},{16,8},{24,0},{1,25},{9,17},{17,9},{25,1},{2,26},{10... | collective-permute-start | bytes 786440 | tf_op jit(solution)/shard_map/ppermute | solution.py:386
  9.9 3.1 %take_tiles.2.refs_0_ = bf16[1024,1024]{1,0:T(8,128)(2,1)} custom-call(s32[1]{0:T(128)} %bitcast.4.table, bf16[1024,16384]{1,0:T(8,128)(2,1)} %refs_0_.17, bf16[128,1024]{1,0:T(8,128)(2,1)S(1)} %get-tuple-element.42.refs_0_.refs_10_.refs_8_.refs_9_), custom_call_target="tpu_custom_call" | custom-call | tf_op jit(solution)/shard_map/take_tiles/pallas_call | solution.py:274
  13.3 1.6 copy-done.4
  14.9 7.0 %take_tiles.3.refs_12_ = bf16[1024,3072]{1,0:T(8,128)(2,1)} custom-call(s32[3]{0:T(128)S(1)} %pad_add_fusion.table, bf16[1024,16384]{1,0:T(8,128)(2,1)} %refs_0_.17, bf16[1024,1024]{1,0:T(8,128)(2,1)S(1)} %copy-done.4, bf16[2048,32]{1,0:T(8,128)(2,1)S(1)} %copy.17.refs_1_.refs_4_.refs_2_), custom_call_target="tpu_custom_call" | custom-call | tf_op jit(solution)/shard_map/take_tiles/pallas_call | solution.py:274
  23.2 5.8 %collective-permute-done.3.refs_7_.refs_5_.refs_6_ = bf16[128,1024]{1,0:T(8,128)(2,1)S(1)} collective-permute-done((bf16[128,1024]{1,0:T(8,128)(2,1)S(1)}, bf16[128,1024]{1,0:T(8,128)(2,1)S(1)}, u32[]{:S(2)}, u32[]{:S(2)}) %collective-permute-start.3) | collective-permute-done | bytes 262176 | tf_op jit(solution)/shard_map/ppermute | solution.py:387
  29.8 10.1 %merge_pass.8 = (bf16[2048,1024]{1,0:T(8,128)(2,1)}, bf16[256,1024]{1,0:T(8,128)(2,1)S(1)}, bf16[256,1024]{1,0:T(8,128)(2,1)S(1)}, bf16[1024,2048]{1,0:T(8,128)(2,1)}, bf16[1024,2048]{1,0:T(8,128)(2,1)}) custom-call(s32[6]{0:T(128)S(1)} %concatenate.13.table, bf16[1024,16384]{1,0:T(8,128)(2,1)} %refs_0_.17, bf16[1024,16384]{1,0:T(8,128)(2,1)} %refs_0_.17, ...), custom_call_target="tpu_custom_call" | custom-call | flops 1610612736 | bytes 8388608 | tf_op jit(solution)/shard_map/merge_pass/pallas_call | solution.py:248
  42.0 1.6 collective-permute-start.11
  44.7 6.9 %merge_pass.9 = (bf16[2048,1024]{1,0:T(8,128)(2,1)}, bf16[256,1024]{1,0:T(8,128)(2,1)S(1)}, bf16[256,1024]{1,0:T(8,128)(2,1)S(1)}) custom-call(s32[2]{0:T(128)S(1)} %iota_add_fusion.4.table, bf16[1024,16384]{1,0:T(8,128)(2,1)} %refs_0_.17, bf16[1024,3072]{1,0:T(8,128)(2,1)} %collective-permute-done.7.refs_1_, ...), custom_call_target="tpu_custom_call" | custom-call | flops 1610612736 | bytes 8388608 | tf_op jit(solution)/shard_map/merge_pass/pallas_call | solution.py:248
  51.6 5.4 %collective-permute-done.8.refs_11_ = bf16[128,1024]{1,0:T(8,128)(2,1)S(1)} collective-permute-done((bf16[128,1024]{1,0:T(8,128)(2,1)}, bf16[128,1024]{1,0:T(8,128)(2,1)S(1)}, u32[]{:S(2)}, u32[]{:S(2)}) %collective-permute-start.8) | collective-permute-done | bytes 262176 | tf_op jit(solution)/shard_map/ppermute | solution.py:386
  57.0 1.6 collective-permute-start.14
  58.6 6.9 %merge_pass.10 = (bf16[2048,1024]{1,0:T(8,128)(2,1)}, bf16[256,1024]{1,0:T(8,128)(2,1)S(1)}, bf16[256,1024]{1,0:T(8,128)(2,1)S(1)}) custom-call(s32[2]{0:T(128)S(1)} %iota_add_fusion.5.table, bf16[1024,16384]{1,0:T(8,128)(2,1)} %refs_0_.17, bf16[1024,3072]{1,0:T(8,128)(2,1)} %collective-permute-done.7.refs_1_, ...), custom_call_target="tpu_custom_call" | custom-call | flops 1610612736 | bytes 8388608 | tf_op jit(solution)/shard_map/merge_pass/pallas_call | solution.py:248
  66.4 7.3 %merge_pass.11 = (bf16[256,1024]{1,0:T(8,128)(2,1)S(1)}, bf16[256,1024]{1,0:T(8,128)(2,1)S(1)}, bf16[128,1024]{1,0:T(8,128)(2,1)S(1)}, bf16[128,1024]{1,0:T(8,128)(2,1)S(1)}) custom-call(s32[2]{0:T(128)S(1)} %iota_add_fusion.3.table, bf16[1024,16384]{1,0:T(8,128)(2,1)} %refs_0_.17, ...), custom_call_target="tpu_custom_call", output_to_operand_aliasing={{0}: (14, {})} | custom-call | flops 2147483648 | bytes 8388608 | tf_op jit(solution)/shard_map/merge_pass/pallas_call | solution.py:248
  73.6 1.3 collective-permute-start.12
  75.7 7.2 %merge_pass.12 = (bf16[256,1024]{1,0:T(8,128)(2,1)S(1)}, bf16[256,1024]{1,0:T(8,128)(2,1)S(1)}, bf16[128,1024]{1,0:T(8,128)(2,1)S(1)}, bf16[128,1024]{1,0:T(8,128)(2,1)S(1)}) custom-call(s32[2]{0:T(128)S(1)} %iota_add_fusion.1.table, bf16[1024,16384]{1,0:T(8,128)(2,1)} %refs_0_.17, ...), custom_call_target="tpu_custom_call", output_to_operand_aliasing={{0}: (14, {})} | custom-call | flops 2147483648 | bytes 8388608 | tf_op jit(solution)/shard_map/merge_pass/pallas_call | solution.py:248
  83.9 2.1 %collective-permute-start.17 = (bf16[256,1024]{1,0:T(8,128)(2,1)S(1)}, bf16[256,1024]{1,0:T(8,128)(2,1)S(1)}, u32[]{:S(2)}, u32[]{:S(2)}) collective-permute-start(bf16[256,1024]{1,0:T(8,128)(2,1)S(1)} %add_terms.9.refs_10_), channel_id=1, source_target_pairs={{0,8},{8,0},{16,24},{24,16},{1,9},{9,1},{17,25},{25,17},{2,10},{10... | collective-permute-start | bytes 1572872 | tf_op jit(solution)/shard_map/ppermute | solution.py:454
  86.0 7.2 %merge_pass.13 = (bf16[2048,1024]{1,0:T(8,128)(2,1)}, bf16[256,1024]{1,0:T(8,128)(2,1)S(1)}, bf16[256,1024]{1,0:T(8,128)(2,1)S(1)}) custom-call(s32[2]{0:T(128)S(1)} %iota_add_fusion.2.table, bf16[1024,16384]{1,0:T(8,128)(2,1)} %refs_0_.17, bf16[1024,2048]{1,0:T(8,128)(2,1)} %collective-permute-done.10.refs_15_.refs_1_, ...), custom_call_target="tpu_custom_call" | custom-call | flops 1610612736 | bytes 8388608 | tf_op jit(solution)/shard_map/merge_pass/pallas_call | solution.py:248
  93.2 1.3 collective-permute-start.19
  94.8 7.3 %merge_pass.14 = (bf16[256,1024]{1,0:T(8,128)(2,1)S(1)}, bf16[256,1024]{1,0:T(8,128)(2,1)S(1)}, bf16[128,1024]{1,0:T(8,128)(2,1)S(1)}, bf16[128,1024]{1,0:T(8,128)(2,1)S(1)}) custom-call(s32[2]{0:T(128)S(1)} %iota_add_fusion.7.table, bf16[1024,16384]{1,0:T(8,128)(2,1)} %refs_0_.17, ...), custom_call_target="tpu_custom_call", output_to_operand_aliasing={{0}: (14, {})} | custom-call | flops 2147483648 | bytes 8388608 | tf_op jit(solution)/shard_map/merge_pass/pallas_call | solution.py:248
  102.1 1.4 collective-permute-start.22
  104.5 4.1 %collective-permute-done.18.refs_3_ = bf16[128,1024]{1,0:T(8,128)(2,1)S(1)} collective-permute-done((bf16[128,1024]{1,0:T(8,128)(2,1)S(1)}, bf16[128,1024]{1,0:T(8,128)(2,1)S(1)}, u32[]{:S(2)}, u32[]{:S(2)}) %collective-permute-start.18) | collective-permute-done | bytes 262176 | tf_op jit(solution)/shard_map/ppermute | solution.py:459
  109.6 1.2 copy-done.2
  111.4 5.4 %collective-permute-done.19.refs_15_.refs_1_ = bf16[256,1024]{1,0:T(8,128)(2,1)S(1)} collective-permute-done((bf16[256,1024]{1,0:T(8,128)(2,1)S(1)}, bf16[256,1024]{1,0:T(8,128)(2,1)S(1)}, u32[]{:S(2)}, u32[]{:S(2)}) %collective-permute-start.19) | collective-permute-done | bytes 524320 | tf_op jit(solution)/shard_map/ppermute | solution.py:441
  116.8 7.0 %merge_pass.15 = (bf16[256,1024]{1,0:T(8,128)(2,1)S(1)}, bf16[256,1024]{1,0:T(8,128)(2,1)S(1)}, bf16[128,1024]{1,0:T(8,128)(2,1)S(1)}, bf16[128,1024]{1,0:T(8,128)(2,1)S(1)}) custom-call(s32[2]{0:T(128)S(1)} %iota_add_fusion.table, bf16[1024,16384]{1,0:T(8,128)(2,1)} %refs_0_.17, ...), custom_call_target="tpu_custom_call", output_to_operand_aliasing={{0}: (14, {})} | custom-call | flops 2147483648 | bytes 8388608 | tf_op jit(solution)/shard_map/merge_pass/pallas_call | solution.py:248
  124.1 1.6 collective-permute-start.20
  125.7 1.7 collective-permute-start.24
  127.4 13.2 %collective-permute-done.24.refs_3_ = bf16[128,1024]{1,0:T(8,128)(2,1)S(1)} collective-permute-done((bf16[128,1024]{1,0:T(8,128)(2,1)S(1)}, bf16[128,1024]{1,0:T(8,128)(2,1)S(1)}, u32[]{:S(2)}, u32[]{:S(2)}) %collective-permute-start.24) | collective-permute-done | bytes 262176 | tf_op jit(solution)/shard_map/ppermute | solution.py:459
  143.0 3.4 %collective-permute-start.26 = (bf16[128,1024]{1,0:T(8,128)(2,1)S(1)}, bf16[128,1024]{1,0:T(8,128)(2,1)S(1)}, u32[]{:S(2)}, u32[]{:S(2)}) collective-permute-start(bf16[128,1024]{1,0:T(8,128)(2,1)S(1)} %add_terms.14.refs_3_), channel_id=1, source_target_pairs={{0,16},{8,24},{16,0},{24,8},{1,17},{9,25},{17,1},{25,9},{2,18},{10... | collective-permute-start | bytes 786440 | tf_op jit(solution)/shard_map/ppermute | solution.py:459
  146.8 16.9 %collective-permute-done.26.refs_3_ = bf16[128,1024]{1,0:T(8,128)(2,1)S(1)} collective-permute-done((bf16[128,1024]{1,0:T(8,128)(2,1)S(1)}, bf16[128,1024]{1,0:T(8,128)(2,1)S(1)}, u32[]{:S(2)}, u32[]{:S(2)}) %collective-permute-start.26) | collective-permute-done | bytes 262176 | tf_op jit(solution)/shard_map/ppermute | solution.py:459
  164.7 3.6 %collective-permute-done.25.refs_3_ = bf16[128,1024]{1,0:T(8,128)(2,1)S(1)} collective-permute-done((bf16[128,1024]{1,0:T(8,128)(2,1)S(1)}, bf16[128,1024]{1,0:T(8,128)(2,1)S(1)}, u32[]{:S(2)}, u32[]{:S(2)}) %collective-permute-start.25) | collective-permute-done | bytes 262176 | tf_op jit(solution)/shard_map/ppermute | solution.py:459
  (98 shorter events, 17.5 us)
Async XLA Ops:
  0.0 13.0 %collective-permute-start.1 = (bf16[1024,32]{0,1:T(8,128)(2,1)}, bf16[1024,32]{0,1:T(8,128)(2,1)S(1)}, u32[]{:S(2)}, u32[]{:S(2)}) collective-permute-start(bf16[1024,32]{0,1:T(8,128)(2,1)} %param.8), channel_id=1, source_target_pairs={{0,2},{2,0},{4,6},{6,4},{1,3},{3,1},{5,7},{7,5},{8,10},{10,8},{12,... | collective-permute-start | bytes 196616 | tf_op jit(solution)/shard_map/ppermute | solution.py:389
  4.8 17.6 %collective-permute-start.2 = (bf16[128,1024]{1,0:T(8,128)(2,1)S(1)}, bf16[128,1024]{1,0:T(8,128)(2,1)S(1)}, u32[]{:S(2)}, u32[]{:S(2)}) collective-permute-start(bf16[128,1024]{1,0:T(8,128)(2,1)S(1)} %get-tuple-element.43), channel_id=1, source_target_pairs={{0,8},{8,0},{16,24},{24,16},{1,9},{9,1},{17,25},{25,17},{2,10},{10... | collective-permute-start | bytes 786440 | tf_op jit(solution)/shard_map/ppermute | solution.py:386
  7.4 15.1 %collective-permute-start.4 = (bf16[128,1024]{1,0:T(8,128)(2,1)S(1)}, bf16[128,1024]{1,0:T(8,128)(2,1)S(1)}, u32[]{:S(2)}, u32[]{:S(2)}) collective-permute-start(bf16[128,1024]{1,0:T(8,128)(2,1)S(1)} %get-tuple-element.44), channel_id=1, source_target_pairs={{0,24},{8,16},{16,8},{24,0},{1,25},{9,17},{17,9},{25,1},{2,26},{10... | collective-permute-start | bytes 786440 | tf_op jit(solution)/shard_map/ppermute | solution.py:386
  13.0 16.8 %collective-permute-start = (bf16[1024,1024]{1,0:T(8,128)(2,1)}, bf16[1024,1024]{1,0:T(8,128)(2,1)}, u32[]{:S(2)}, u32[]{:S(2)}) collective-permute-start(bf16[1024,1024]{1,0:T(8,128)(2,1)} %take_tiles.2.refs_0_), channel_id=1, source_target_pairs={{0,2},{2,0},{4,6},{6,4},{1,3},{3,1},{5,7},{7,5},{8,10},{10,8},{12,... | collective-permute-start | bytes 6291464 | tf_op jit(solution)/shard_map/ppermute | solution.py:403
  22.0 21.7 %collective-permute-start.7 = (bf16[1024,3072]{1,0:T(8,128)(2,1)}, bf16[1024,3072]{1,0:T(8,128)(2,1)}, u32[]{:S(2)}, u32[]{:S(2)}) collective-permute-start(bf16[1024,3072]{1,0:T(8,128)(2,1)} %take_tiles.3.refs_12_), channel_id=1, source_target_pairs={{0,2},{2,0},{4,6},{6,4},{1,3},{3,1},{5,7},{7,5},{8,10},{10,8},{12,... | collective-permute-start | bytes 18874376 | tf_op jit(solution)/shard_map/ppermute | solution.py:403
  22.5 6.5 %collective-permute-start.3 = (bf16[128,1024]{1,0:T(8,128)(2,1)S(1)}, bf16[128,1024]{1,0:T(8,128)(2,1)S(1)}, u32[]{:S(2)}, u32[]{:S(2)}) collective-permute-start(bf16[128,1024]{1,0:T(8,128)(2,1)S(1)} %collective-permute-done.2.refs_6_.refs_4_.refs_5_), channel_id=1, source_target_pairs={{0,2},{2,0},{4,6},{6,4},{1,3},{3,1},{5,7},{7,5},{8,10},{10,8},{12,... | collective-permute-start | bytes 786440 | tf_op jit(solution)/shard_map/ppermute | solution.py:387
  22.6 7.2 %collective-permute-start.5 = (bf16[128,1024]{1,0:T(8,128)(2,1)S(1)}, bf16[128,1024]{1,0:T(8,128)(2,1)S(1)}, u32[]{:S(2)}, u32[]{:S(2)}) collective-permute-start(bf16[128,1024]{1,0:T(8,128)(2,1)S(1)} %collective-permute-done.4.refs_8_.refs_6_.refs_7_), channel_id=1, source_target_pairs={{0,2},{2,0},{4,6},{6,4},{1,3},{3,1},{5,7},{7,5},{8,10},{10,8},{12,... | collective-permute-start | bytes 786440 | tf_op jit(solution)/shard_map/ppermute | solution.py:387
  29.8 12.2 %copy-start.15 = (s32[128]{0:T(128)S(1)}, s32[128]{0:T(128)}, u32[]{:S(2)}) copy-start(s32[128]{0:T(128)} %param.11) | copy-start | bytes 1540
  41.4 24.9 %collective-permute-start.6 = (bf16[1024,2048]{1,0:T(8,128)(2,1)}, bf16[1024,2048]{1,0:T(8,128)(2,1)}, u32[]{:S(2)}, u32[]{:S(2)}) collective-permute-start(bf16[1024,2048]{1,0:T(8,128)(2,1)} %get-tuple-element.46), channel_id=1, source_target_pairs={{0,2},{2,0},{4,6},{6,4},{1,3},{3,1},{5,7},{7,5},{8,10},{10,8},{12,... | collective-permute-start | bytes 12582920 | tf_op jit(solution)/shard_map/ppermute | solution.py:403
  41.6 24.8 %collective-permute-start.10 = (bf16[1024,2048]{1,0:T(8,128)(2,1)}, bf16[1024,2048]{1,0:T(8,128)(2,1)}, u32[]{:S(2)}, u32[]{:S(2)}) collective-permute-start(bf16[1024,2048]{1,0:T(8,128)(2,1)} %get-tuple-element.56), channel_id=1, source_target_pairs={{0,2},{2,0},{4,6},{6,4},{1,3},{3,1},{5,7},{7,5},{8,10},{10,8},{12,... | collective-permute-start | bytes 12582920 | tf_op jit(solution)/shard_map/ppermute | solution.py:403
  41.9 15.1 %collective-permute-start.8 = (bf16[128,1024]{1,0:T(8,128)(2,1)}, bf16[128,1024]{1,0:T(8,128)(2,1)S(1)}, u32[]{:S(2)}, u32[]{:S(2)}) collective-permute-start(bf16[128,1024]{1,0:T(8,128)(2,1)} %get-tuple-element.50), channel_id=1, source_target_pairs={{0,16},{8,24},{16,0},{24,8},{1,17},{9,25},{17,1},{25,9},{2,18},{10... | collective-permute-start | bytes 786440 | tf_op jit(solution)/shard_map/ppermute | solution.py:386
  42.0 23.5 %collective-permute-start.11 = (bf16[256,1024]{1,0:T(8,128)(2,1)}, bf16[256,1024]{1,0:T(8,128)(2,1)S(1)}, u32[]{:S(2)}, u32[]{:S(2)}) collective-permute-start(bf16[256,1024]{1,0:T(8,128)(2,1)} %copy-done.11), channel_id=1, source_target_pairs={{0,4},{2,6},{4,0},{6,2},{1,5},{3,7},{5,1},{7,3},{8,12},{10,14},{12... | collective-permute-start | bytes 1572872 | tf_op jit(solution)/shard_map/ppermute | solution.py:441
  57.0 9.3 %collective-permute-start.9 = (bf16[128,1024]{1,0:T(8,128)(2,1)S(1)}, bf16[128,1024]{1,0:T(8,128)(2,1)S(1)}, u32[]{:S(2)}, u32[]{:S(2)}) collective-permute-start(bf16[128,1024]{1,0:T(8,128)(2,1)S(1)} %collective-permute-done.8.refs_11_), channel_id=1, source_target_pairs={{0,2},{2,0},{4,6},{6,4},{1,3},{3,1},{5,7},{7,5},{8,10},{10,8},{12,... | collective-permute-start | bytes 786440 | tf_op jit(solution)/shard_map/ppermute | solution.py:469
  57.0 9.3 %copy-start.6 = (bf16[2048,1024]{1,0:T(8,128)(2,1)S(1)}, bf16[2048,1024]{1,0:T(8,128)(2,1)}, u32[]{:S(2)}) copy-start(bf16[2048,1024]{1,0:T(8,128)(2,1)} %get-tuple-element.53.refs_4_) | copy-start | bytes 12582916
  57.0 9.3 %copy-start.10 = (bf16[256,1024]{1,0:T(8,128)(2,1)S(1)}, bf16[256,1024]{1,0:T(8,128)(2,1)}, u32[]{:S(2)}) copy-start(bf16[256,1024]{1,0:T(8,128)(2,1)} %copy-done.9) | copy-start | bytes 1572868
  57.0 18.6 %collective-permute-start.14 = (bf16[256,1024]{1,0:T(8,128)(2,1)S(1)}, bf16[256,1024]{1,0:T(8,128)(2,1)S(1)}, u32[]{:S(2)}, u32[]{:S(2)}) collective-permute-start(bf16[256,1024]{1,0:T(8,128)(2,1)S(1)} %get-tuple-element.48.refs_10_), channel_id=1, source_target_pairs={{0,4},{2,6},{4,0},{6,2},{1,5},{3,7},{5,1},{7,3},{8,12},{10,14},{12... | collective-permute-start | bytes 1572872 | tf_op jit(solution)/shard_map/ppermute | solution.py:441
  65.6 20.5 %collective-permute-start.15 = (bf16[256,1024]{1,0:T(8,128)(2,1)S(1)}, bf16[256,1024]{1,0:T(8,128)(2,1)S(1)}, u32[]{:S(2)}, u32[]{:S(2)}) collective-permute-start(bf16[256,1024]{1,0:T(8,128)(2,1)S(1)} %get-tuple-element.55.refs_14_), channel_id=1, source_target_pairs={{0,4},{2,6},{4,0},{6,2},{1,5},{3,7},{5,1},{7,3},{8,12},{10,14},{12... | collective-permute-start | bytes 1572872 | tf_op jit(solution)/shard_map/ppermute | solution.py:441
  66.4 9.3 %copy-start.8 = (bf16[2048,1024]{1,0:T(8,128)(2,1)S(1)}, bf16[2048,1024]{1,0:T(8,128)(2,1)}, u32[]{:S(2)}) copy-start(bf16[2048,1024]{1,0:T(8,128)(2,1)} %get-tuple-element.60.refs_4_) | copy-start | bytes 12582916
  73.6 20.9 %collective-permute-start.12 = (bf16[256,1024]{1,0:T(8,128)(2,1)S(1)}, bf16[256,1024]{1,0:T(8,128)(2,1)S(1)}, u32[]{:S(2)}, u32[]{:S(2)}) collective-permute-start(bf16[256,1024]{1,0:T(8,128)(2,1)S(1)} %get-tuple-element.58.refs_2_), channel_id=1, source_target_pairs={{0,4},{2,6},{4,0},{6,2},{1,5},{3,7},{5,1},{7,3},{8,12},{10,14},{12... | collective-permute-start | bytes 1572872 | tf_op jit(solution)/shard_map/ppermute | solution.py:449
  75.3 19.2 %collective-permute-start.13 = (bf16[256,1024]{1,0:T(8,128)(2,1)S(1)}, bf16[256,1024]{1,0:T(8,128)(2,1)S(1)}, u32[]{:S(2)}, u32[]{:S(2)}) collective-permute-start(bf16[256,1024]{1,0:T(8,128)(2,1)S(1)} %add_terms.8.refs_14_), channel_id=1, source_target_pairs={{0,8},{8,0},{16,24},{24,16},{1,9},{9,1},{17,25},{25,17},{2,10},{10... | collective-permute-start | bytes 1572872 | tf_op jit(solution)/shard_map/ppermute | solution.py:454
  82.8 26.7 %collective-permute-start.16 = (bf16[256,1024]{1,0:T(8,128)(2,1)S(1)}, bf16[256,1024]{1,0:T(8,128)(2,1)S(1)}, u32[]{:S(2)}, u32[]{:S(2)}) collective-permute-start(bf16[256,1024]{1,0:T(8,128)(2,1)S(1)} %get-tuple-element.63.refs_2_), channel_id=1, source_target_pairs={{0,4},{2,6},{4,0},{6,2},{1,5},{3,7},{5,1},{7,3},{8,12},{10,14},{12... | collective-permute-start | bytes 1572872 | tf_op jit(solution)/shard_map/ppermute | solution.py:449
  83.9 25.6 %collective-permute-start.17 = (bf16[256,1024]{1,0:T(8,128)(2,1)S(1)}, bf16[256,1024]{1,0:T(8,128)(2,1)S(1)}, u32[]{:S(2)}, u32[]{:S(2)}) collective-permute-start(bf16[256,1024]{1,0:T(8,128)(2,1)S(1)} %add_terms.9.refs_10_), channel_id=1, source_target_pairs={{0,8},{8,0},{16,24},{24,16},{1,9},{9,1},{17,25},{25,17},{2,10},{10... | collective-permute-start | bytes 1572872 | tf_op jit(solution)/shard_map/ppermute | solution.py:454
  93.2 23.5 %collective-permute-start.19 = (bf16[256,1024]{1,0:T(8,128)(2,1)S(1)}, bf16[256,1024]{1,0:T(8,128)(2,1)S(1)}, u32[]{:S(2)}, u32[]{:S(2)}) collective-permute-start(bf16[256,1024]{1,0:T(8,128)(2,1)S(1)} %get-tuple-element.64.refs_3_), channel_id=1, source_target_pairs={{0,4},{2,6},{4,0},{6,2},{1,5},{3,7},{5,1},{7,3},{8,12},{10,14},{12... | collective-permute-start | bytes 1572872 | tf_op jit(solution)/shard_map/ppermute | solution.py:441
  94.7 13.8 %collective-permute-start.18 = (bf16[128,1024]{1,0:T(8,128)(2,1)S(1)}, bf16[128,1024]{1,0:T(8,128)(2,1)S(1)}, u32[]{:S(2)}, u32[]{:S(2)}) collective-permute-start(bf16[128,1024]{1,0:T(8,128)(2,1)S(1)} %add_terms.10.refs_14_), channel_id=1, source_target_pairs={{0,16},{8,24},{16,0},{24,8},{1,17},{9,25},{17,1},{25,9},{2,18},{10... | collective-permute-start | bytes 786440 | tf_op jit(solution)/shard_map/ppermute | solution.py:459
  102.1 39.5 %collective-permute-start.22 = (bf16[256,1024]{1,0:T(8,128)(2,1)S(1)}, bf16[256,1024]{1,0:T(8,128)(2,1)S(1)}, u32[]{:S(2)}, u32[]{:S(2)}) collective-permute-start(bf16[256,1024]{1,0:T(8,128)(2,1)S(1)} %get-tuple-element.65.refs_4_), channel_id=1, source_target_pairs={{0,4},{2,6},{4,0},{6,2},{1,5},{3,7},{5,1},{7,3},{8,12},{10,14},{12... | collective-permute-start | bytes 1572872 | tf_op jit(solution)/shard_map/ppermute | solution.py:449
  103.5 13.3 %copy-start.7 = (bf16[2048,1024]{1,0:T(8,128)(2,1)S(1)}, bf16[2048,1024]{1,0:T(8,128)(2,1)}, u32[]{:S(2)}) copy-start(bf16[2048,1024]{1,0:T(8,128)(2,1)} %get-tuple-element.67.refs_4_) | copy-start | bytes 12582916
  111.3 30.2 %collective-permute-start.23 = (bf16[256,1024]{1,0:T(8,128)(2,1)S(1)}, bf16[256,1024]{1,0:T(8,128)(2,1)S(1)}, u32[]{:S(2)}, u32[]{:S(2)}) collective-permute-start(bf16[256,1024]{1,0:T(8,128)(2,1)S(1)} %add_terms.12.refs_14_), channel_id=1, source_target_pairs={{0,8},{8,0},{16,24},{24,16},{1,9},{9,1},{17,25},{25,17},{2,10},{10... | collective-permute-start | bytes 1572872 | tf_op jit(solution)/shard_map/ppermute | solution.py:454
  124.0 22.4 %collective-permute-start.21 = (bf16[256,1024]{1,0:T(8,128)(2,1)S(1)}, bf16[256,1024]{1,0:T(8,128)(2,1)S(1)}, u32[]{:S(2)}, u32[]{:S(2)}) collective-permute-start(bf16[256,1024]{1,0:T(8,128)(2,1)S(1)} %add_terms.13.refs_5_), channel_id=1, source_target_pairs={{0,8},{8,0},{16,24},{24,16},{1,9},{9,1},{17,25},{25,17},{2,10},{10... | collective-permute-start | bytes 1572872 | tf_op jit(solution)/shard_map/ppermute | solution.py:454
  124.1 22.4 %collective-permute-start.20 = (bf16[256,1024]{1,0:T(8,128)(2,1)S(1)}, bf16[256,1024]{1,0:T(8,128)(2,1)S(1)}, u32[]{:S(2)}, u32[]{:S(2)}) collective-permute-start(bf16[256,1024]{1,0:T(8,128)(2,1)S(1)} %get-tuple-element.73.refs_2_), channel_id=1, source_target_pairs={{0,4},{2,6},{4,0},{6,2},{1,5},{3,7},{5,1},{7,3},{8,12},{10,14},{12... | collective-permute-start | bytes 1572872 | tf_op jit(solution)/shard_map/ppermute | solution.py:449
  125.7 14.9 %collective-permute-start.24 = (bf16[128,1024]{1,0:T(8,128)(2,1)S(1)}, bf16[128,1024]{1,0:T(8,128)(2,1)S(1)}, u32[]{:S(2)}, u32[]{:S(2)}) collective-permute-start(bf16[128,1024]{1,0:T(8,128)(2,1)S(1)} %add_terms.11.refs_2_), channel_id=1, source_target_pairs={{0,16},{8,24},{16,0},{24,8},{1,17},{9,25},{17,1},{25,9},{2,18},{10... | collective-permute-start | bytes 786440 | tf_op jit(solution)/shard_map/ppermute | solution.py:459
  143.0 20.7 %collective-permute-start.26 = (bf16[128,1024]{1,0:T(8,128)(2,1)S(1)}, bf16[128,1024]{1,0:T(8,128)(2,1)S(1)}, u32[]{:S(2)}, u32[]{:S(2)}) collective-permute-start(bf16[128,1024]{1,0:T(8,128)(2,1)S(1)} %add_terms.14.refs_3_), channel_id=1, source_target_pairs={{0,16},{8,24},{16,0},{24,8},{1,17},{9,25},{17,1},{25,9},{2,18},{10... | collective-permute-start | bytes 786440 | tf_op jit(solution)/shard_map/ppermute | solution.py:459
  146.7 21.7 %collective-permute-start.25 = (bf16[128,1024]{1,0:T(8,128)(2,1)S(1)}, bf16[128,1024]{1,0:T(8,128)(2,1)S(1)}, u32[]{:S(2)}, u32[]{:S(2)}) collective-permute-start(bf16[128,1024]{1,0:T(8,128)(2,1)S(1)} %add_terms.15.refs_5_), channel_id=1, source_target_pairs={{0,16},{8,24},{16,0},{24,8},{1,17},{9,25},{17,1},{25,9},{2,18},{10... | collective-permute-start | bytes 786440 | tf_op jit(solution)/shard_map/ppermute | solution.py:459
  (11 other events, 37.6 us)

commit v4 on v3

--- a/solution.py
+++ b/solution.py
@@ -474,17 +474,17 @@
     done = first(3, (done, far_y[2]))
     done = to_z2(0, (done,))
     done = second(2, (done,))
+    done = to_z1(2, (done,))
     cosine, sine_part = turn_tables(lax.optimization_barrier((hidden, done))[0], positions)
     out = finish(0, None, (done,))
     done = to_z2(1, (out,))
-    done = to_z1(2, (done,))
     done = second(3, (done, far_y[3]))
-    done = to_z1(3, (done,))
     out = finish(1, out, (done,))
-    done = to_z2(2, (out,))
+    done = to_z1(3, (out,))
+    done = to_z2(2, (done,))
     done = to_z2(3, (done,))
     out = finish(2, out, (done,))
-    return finish(3, out, (done,))
+    return finish(3, out, ())
 
 
 def any_shards(fsdp, tp_size, hidden, base, down, up, norm_gain, positions):

time: 170 us -> 160 us (0.941)
  waiting for transfers between devices: 55.2 us -> 47.9 us
  starting transfers between devices: 24.9 us -> 22.1 us
    ppermute x4, waiting for transfers between devices: 37.8 us -> 15.8 us  [to_z2(): far_z[i] = over_z2(operand)]
    ppermute x4, waiting for transfers between devices: 0.01 us -> 8.84 us  [second(): mid_y[i] = over_y(half)]
    ppermute x4, waiting for transfers between devices: 0.01 us -> 8.82 us  [to_z1(): near_z[i] = over_z1(operand)]
    ppermute x4, starting transfers between devices: 5.31 us -> 0.7 us  [to_z2(): far_z[i] = over_z2(operand)]
    ppermute x4, waiting for transfers between devices: 5.36 us -> 2.43 us  [first(): far_y[i] = over_y(value)]
  transfers between devices with their start and end apart: 27 -> 27, of which waited for: 8 -> 9; matrix products, arithmetic and copies ran while one was open for 2% -> 2% of each run, Pallas kernels for 45% -> 48%
where the time goes in v4:
time: 160 us; the launch traced here: 159 us
  Pallas kernels  77.2 us (48%)
  waiting for transfers between devices  47.9 us (30%)
  starting transfers between devices  22.1 us (14%)
  local copies, waits for them, and re-layouts  10.2 us (6%)
    pallas_call x8, Pallas kernels, merge_pass(): pl.pallas_call(functools.partial(pass_kernel, len(bases), [len(line) for...  59.8 us
    ppermute x4, waiting for transfers between devices, to_z2(): far_z[i] = over_z2(operand)  15.8 us
    pallas_call x2, Pallas kernels, take_tiles(): pl.pallas_call(take_kernel, grid_spec=pltpu.PrefetchScalarGridSpec(num_sc...  10.1 us
    unnamed x32, local copies, waits for them, and re-layouts  8.94 us
    ppermute x4, waiting for transfers between devices, second(): mid_y[i] = over_y(half)  8.84 us
    ppermute x4, waiting for transfers between devices, to_z1(): near_z[i] = over_z1(operand)  8.82 us
    ppermute x2, waiting for transfers between devices, line_shards(): first_lines = [[x1, over_core(x1)], [x3, over_core(x3)], [own_x, own_other]]  6.56 us
    ppermute x3, waiting for transfers between devices, line_shards(): x1, x2, x3 = (over('fsdp', 1)(p1), over('fsdp', 2)(p2), over('fsdp', 3)(p3))  5.43 us
  transfers between devices with their start and end apart: 27, of which 9 were waited for; matrix products, arithmetic and copies ran while one was open for 2% of the time, Pallas kernels for 48%

profile of v4, /device:TPU:0, one launch (start us, length us, event | category | flops | bytes accessed | tf_op | source)
XLA Modules:
  0.0 159.3 jit_solution(11542070100668887081)
XLA Ops:
  1.3 2.2 %copy-done = bf16[128,16384]{1,0:T(8,128)(2,1)S(1)} copy-done((bf16[128,16384]{1,0:T(8,128)(2,1)S(1)}, bf16[128,16384]{1,0:T(8,128)(2,1)}, u32[]{:S(2)}) %copy-start) | copy-done | bytes 4194328
  3.5 1.3 pick_features.1
  4.8 2.6 %collective-permute-start.2 = (bf16[128,1024]{1,0:T(8,128)(2,1)S(1)}, bf16[128,1024]{1,0:T(8,128)(2,1)S(1)}, u32[]{:S(2)}, u32[]{:S(2)}) collective-permute-start(bf16[128,1024]{1,0:T(8,128)(2,1)S(1)} %get-tuple-element.43), channel_id=1, source_target_pairs={{0,8},{8,0},{16,24},{24,16},{1,9},{9,1},{17,25},{25,17},{2,10},{10... | collective-permute-start | bytes 786440 | tf_op jit(solution)/shard_map/ppermute | solution.py:386
  7.4 2.5 %collective-permute-start.4 = (bf16[128,1024]{1,0:T(8,128)(2,1)S(1)}, bf16[128,1024]{1,0:T(8,128)(2,1)S(1)}, u32[]{:S(2)}, u32[]{:S(2)}) collective-permute-start(bf16[128,1024]{1,0:T(8,128)(2,1)S(1)} %get-tuple-element.44), channel_id=1, source_target_pairs={{0,24},{8,16},{16,8},{24,0},{1,25},{9,17},{17,9},{25,1},{2,26},{10... | collective-permute-start | bytes 786440 | tf_op jit(solution)/shard_map/ppermute | solution.py:386
  9.9 3.1 %take_tiles.2.refs_0_ = bf16[1024,1024]{1,0:T(8,128)(2,1)} custom-call(s32[1]{0:T(128)} %bitcast.4.table, bf16[1024,16384]{1,0:T(8,128)(2,1)} %refs_0_.17, bf16[128,1024]{1,0:T(8,128)(2,1)S(1)} %get-tuple-element.42.refs_0_.refs_10_.refs_8_.refs_9_), custom_call_target="tpu_custom_call" | custom-call | tf_op jit(solution)/shard_map/take_tiles/pallas_call | solution.py:274
  13.3 1.6 copy-done.4
  14.9 7.0 %take_tiles.3.refs_12_ = bf16[1024,3072]{1,0:T(8,128)(2,1)} custom-call(s32[3]{0:T(128)S(1)} %pad_add_fusion.table, bf16[1024,16384]{1,0:T(8,128)(2,1)} %refs_0_.17, bf16[1024,1024]{1,0:T(8,128)(2,1)S(1)} %copy-done.4, bf16[2048,32]{1,0:T(8,128)(2,1)S(1)} %copy.17.refs_1_.refs_4_.refs_2_), custom_call_target="tpu_custom_call" | custom-call | tf_op jit(solution)/shard_map/take_tiles/pallas_call | solution.py:274
  23.2 5.8 %collective-permute-done.3.refs_7_.refs_5_.refs_6_ = bf16[128,1024]{1,0:T(8,128)(2,1)S(1)} collective-permute-done((bf16[128,1024]{1,0:T(8,128)(2,1)S(1)}, bf16[128,1024]{1,0:T(8,128)(2,1)S(1)}, u32[]{:S(2)}, u32[]{:S(2)}) %collective-permute-start.3) | collective-permute-done | bytes 262176 | tf_op jit(solution)/shard_map/ppermute | solution.py:387
  29.8 10.1 %merge_pass.8 = (bf16[2048,1024]{1,0:T(8,128)(2,1)}, bf16[256,1024]{1,0:T(8,128)(2,1)S(1)}, bf16[256,1024]{1,0:T(8,128)(2,1)S(1)}, bf16[1024,2048]{1,0:T(8,128)(2,1)}, bf16[1024,2048]{1,0:T(8,128)(2,1)}) custom-call(s32[6]{0:T(128)S(1)} %concatenate.13.table, bf16[1024,16384]{1,0:T(8,128)(2,1)} %refs_0_.17, bf16[1024,16384]{1,0:T(8,128)(2,1)} %refs_0_.17, ...), custom_call_target="tpu_custom_call" | custom-call | flops 1610612736 | bytes 8388608 | tf_op jit(solution)/shard_map/merge_pass/pallas_call | solution.py:248
  42.0 1.6 collective-permute-start.11
  44.7 6.9 %merge_pass.9 = (bf16[2048,1024]{1,0:T(8,128)(2,1)}, bf16[256,1024]{1,0:T(8,128)(2,1)S(1)}, bf16[256,1024]{1,0:T(8,128)(2,1)S(1)}) custom-call(s32[2]{0:T(128)S(1)} %iota_add_fusion.4.table, bf16[1024,16384]{1,0:T(8,128)(2,1)} %refs_0_.17, bf16[1024,3072]{1,0:T(8,128)(2,1)} %collective-permute-done.7.refs_1_, ...), custom_call_target="tpu_custom_call" | custom-call | flops 1610612736 | bytes 8388608 | tf_op jit(solution)/shard_map/merge_pass/pallas_call | solution.py:248
  51.6 5.4 %collective-permute-done.8.refs_11_ = bf16[128,1024]{1,0:T(8,128)(2,1)S(1)} collective-permute-done((bf16[128,1024]{1,0:T(8,128)(2,1)}, bf16[128,1024]{1,0:T(8,128)(2,1)S(1)}, u32[]{:S(2)}, u32[]{:S(2)}) %collective-permute-start.8) | collective-permute-done | bytes 262176 | tf_op jit(solution)/shard_map/ppermute | solution.py:386
  57.0 1.6 collective-permute-start.14
  58.6 7.0 %merge_pass.10 = (bf16[2048,1024]{1,0:T(8,128)(2,1)}, bf16[256,1024]{1,0:T(8,128)(2,1)S(1)}, bf16[256,1024]{1,0:T(8,128)(2,1)S(1)}) custom-call(s32[2]{0:T(128)S(1)} %iota_add_fusion.5.table, bf16[1024,16384]{1,0:T(8,128)(2,1)} %refs_0_.17, bf16[1024,3072]{1,0:T(8,128)(2,1)} %collective-permute-done.7.refs_1_, ...), custom_call_target="tpu_custom_call" | custom-call | flops 1610612736 | bytes 8388608 | tf_op jit(solution)/shard_map/merge_pass/pallas_call | solution.py:248
  66.4 7.3 %merge_pass.11 = (bf16[256,1024]{1,0:T(8,128)(2,1)S(1)}, bf16[256,1024]{1,0:T(8,128)(2,1)S(1)}, bf16[128,1024]{1,0:T(8,128)(2,1)S(1)}, bf16[128,1024]{1,0:T(8,128)(2,1)S(1)}) custom-call(s32[2]{0:T(128)S(1)} %iota_add_fusion.3.table, bf16[1024,16384]{1,0:T(8,128)(2,1)} %refs_0_.17, ...), custom_call_target="tpu_custom_call", output_to_operand_aliasing={{0}: (14, {})} | custom-call | flops 2147483648 | bytes 8388608 | tf_op jit(solution)/shard_map/merge_pass/pallas_call | solution.py:248
  73.7 1.3 collective-permute-start.12
  75.7 7.1 %merge_pass.12 = (bf16[256,1024]{1,0:T(8,128)(2,1)S(1)}, bf16[256,1024]{1,0:T(8,128)(2,1)S(1)}, bf16[128,1024]{1,0:T(8,128)(2,1)S(1)}, bf16[128,1024]{1,0:T(8,128)(2,1)S(1)}) custom-call(s32[2]{0:T(128)S(1)} %iota_add_fusion.1.table, bf16[1024,16384]{1,0:T(8,128)(2,1)} %refs_0_.17, ...), custom_call_target="tpu_custom_call", output_to_operand_aliasing={{0}: (14, {})} | custom-call | flops 2147483648 | bytes 8388608 | tf_op jit(solution)/shard_map/merge_pass/pallas_call | solution.py:248
  84.0 2.1 %collective-permute-start.17 = (bf16[256,1024]{1,0:T(8,128)(2,1)S(1)}, bf16[256,1024]{1,0:T(8,128)(2,1)S(1)}, u32[]{:S(2)}, u32[]{:S(2)}) collective-permute-start(bf16[256,1024]{1,0:T(8,128)(2,1)S(1)} %add_terms.9.refs_10_), channel_id=1, source_target_pairs={{0,8},{8,0},{16,24},{24,16},{1,9},{9,1},{17,25},{25,17},{2,10},{10... | collective-permute-start | bytes 1572872 | tf_op jit(solution)/shard_map/ppermute | solution.py:454
  86.0 7.2 %merge_pass.13 = (bf16[2048,1024]{1,0:T(8,128)(2,1)}, bf16[256,1024]{1,0:T(8,128)(2,1)S(1)}, bf16[256,1024]{1,0:T(8,128)(2,1)S(1)}) custom-call(s32[2]{0:T(128)S(1)} %iota_add_fusion.2.table, bf16[1024,16384]{1,0:T(8,128)(2,1)} %refs_0_.17, bf16[1024,2048]{1,0:T(8,128)(2,1)} %collective-permute-done.10.refs_15_.refs_1_, ...), custom_call_target="tpu_custom_call" | custom-call | flops 1610612736 | bytes 8388608 | tf_op jit(solution)/shard_map/merge_pass/pallas_call | solution.py:248
  93.3 1.2 collective-permute-start.19
  94.8 7.3 %merge_pass.14 = (bf16[256,1024]{1,0:T(8,128)(2,1)S(1)}, bf16[256,1024]{1,0:T(8,128)(2,1)S(1)}, bf16[128,1024]{1,0:T(8,128)(2,1)S(1)}, bf16[128,1024]{1,0:T(8,128)(2,1)S(1)}) custom-call(s32[2]{0:T(128)S(1)} %iota_add_fusion.7.table, bf16[1024,16384]{1,0:T(8,128)(2,1)} %refs_0_.17, ...), custom_call_target="tpu_custom_call", output_to_operand_aliasing={{0}: (14, {})} | custom-call | flops 2147483648 | bytes 8388608 | tf_op jit(solution)/shard_map/merge_pass/pallas_call | solution.py:248
  103.5 5.1 %collective-permute-done.18.refs_3_ = bf16[128,1024]{1,0:T(8,128)(2,1)S(1)} collective-permute-done((bf16[128,1024]{1,0:T(8,128)(2,1)S(1)}, bf16[128,1024]{1,0:T(8,128)(2,1)S(1)}, u32[]{:S(2)}, u32[]{:S(2)}) %collective-permute-start.18) | collective-permute-done | bytes 262176 | tf_op jit(solution)/shard_map/ppermute | solution.py:459
  111.1 1.7 %collective-permute-start.24 = (bf16[256,1024]{1,0:T(8,128)(2,1)S(1)}, bf16[256,1024]{1,0:T(8,128)(2,1)S(1)}, u32[]{:S(2)}, u32[]{:S(2)}) collective-permute-start(bf16[256,1024]{1,0:T(8,128)(2,1)S(1)} %add_terms.11.refs_4_), channel_id=1, source_target_pairs={{0,8},{8,0},{16,24},{24,16},{1,9},{9,1},{17,25},{25,17},{2,10},{10... | collective-permute-start | bytes 1572872 | tf_op jit(solution)/shard_map/ppermute | solution.py:454
  112.8 1.5 collective-permute-start.23
  114.3 2.4 %collective-permute-done.19.refs_15_.refs_1_ = bf16[256,1024]{1,0:T(8,128)(2,1)S(1)} collective-permute-done((bf16[256,1024]{1,0:T(8,128)(2,1)S(1)}, bf16[256,1024]{1,0:T(8,128)(2,1)S(1)}, u32[]{:S(2)}, u32[]{:S(2)}) %collective-permute-start.19) | collective-permute-done | bytes 524320 | tf_op jit(solution)/shard_map/ppermute | solution.py:441
  116.8 7.0 %merge_pass.15 = (bf16[256,1024]{1,0:T(8,128)(2,1)S(1)}, bf16[256,1024]{1,0:T(8,128)(2,1)S(1)}, bf16[128,1024]{1,0:T(8,128)(2,1)S(1)}, bf16[128,1024]{1,0:T(8,128)(2,1)S(1)}) custom-call(s32[2]{0:T(128)S(1)} %iota_add_fusion.table, bf16[1024,16384]{1,0:T(8,128)(2,1)} %refs_0_.17, ...), custom_call_target="tpu_custom_call", output_to_operand_aliasing={{0}: (14, {})} | custom-call | flops 2147483648 | bytes 8388608 | tf_op jit(solution)/shard_map/merge_pass/pallas_call | solution.py:248
  123.7 1.6 collective-permute-start.20
  126.3 1.2 copy-done.3
  127.9 1.3 collective-permute-done.24.refs_2_
  130.0 8.8 %collective-permute-done.20.refs_1_ = bf16[256,1024]{1,0:T(8,128)(2,1)S(1)} collective-permute-done((bf16[256,1024]{1,0:T(8,128)(2,1)S(1)}, bf16[256,1024]{1,0:T(8,128)(2,1)S(1)}, u32[]{:S(2)}, u32[]{:S(2)}) %collective-permute-start.20) | collective-permute-done | bytes 524320 | tf_op jit(solution)/shard_map/ppermute | solution.py:449
  138.8 7.5 %collective-permute-done.22.refs_2_ = bf16[256,1024]{1,0:T(8,128)(2,1)S(1)} collective-permute-done((bf16[256,1024]{1,0:T(8,128)(2,1)S(1)}, bf16[256,1024]{1,0:T(8,128)(2,1)S(1)}, u32[]{:S(2)}, u32[]{:S(2)}) %collective-permute-start.22) | collective-permute-done | bytes 524320 | tf_op jit(solution)/shard_map/ppermute | solution.py:454
  147.6 10.7 %collective-permute-done.25.refs_3_ = bf16[128,1024]{1,0:T(8,128)(2,1)S(1)} collective-permute-done((bf16[128,1024]{1,0:T(8,128)(2,1)S(1)}, bf16[128,1024]{1,0:T(8,128)(2,1)S(1)}, u32[]{:S(2)}, u32[]{:S(2)}) %collective-permute-start.25) | collective-permute-done | bytes 262176 | tf_op jit(solution)/shard_map/ppermute | solution.py:459
  (98 shorter events, 18.0 us)
Async XLA Ops:
  0.0 13.0 %collective-permute-start.1 = (bf16[1024,32]{0,1:T(8,128)(2,1)}, bf16[1024,32]{0,1:T(8,128)(2,1)S(1)}, u32[]{:S(2)}, u32[]{:S(2)}) collective-permute-start(bf16[1024,32]{0,1:T(8,128)(2,1)} %param.8), channel_id=1, source_target_pairs={{0,2},{2,0},{4,6},{6,4},{1,3},{3,1},{5,7},{7,5},{8,10},{10,8},{12,... | collective-permute-start | bytes 196616 | tf_op jit(solution)/shard_map/ppermute | solution.py:389
  4.8 17.6 %collective-permute-start.2 = (bf16[128,1024]{1,0:T(8,128)(2,1)S(1)}, bf16[128,1024]{1,0:T(8,128)(2,1)S(1)}, u32[]{:S(2)}, u32[]{:S(2)}) collective-permute-start(bf16[128,1024]{1,0:T(8,128)(2,1)S(1)} %get-tuple-element.43), channel_id=1, source_target_pairs={{0,8},{8,0},{16,24},{24,16},{1,9},{9,1},{17,25},{25,17},{2,10},{10... | collective-permute-start | bytes 786440 | tf_op jit(solution)/shard_map/ppermute | solution.py:386
  7.4 15.1 %collective-permute-start.4 = (bf16[128,1024]{1,0:T(8,128)(2,1)S(1)}, bf16[128,1024]{1,0:T(8,128)(2,1)S(1)}, u32[]{:S(2)}, u32[]{:S(2)}) collective-permute-start(bf16[128,1024]{1,0:T(8,128)(2,1)S(1)} %get-tuple-element.44), channel_id=1, source_target_pairs={{0,24},{8,16},{16,8},{24,0},{1,25},{9,17},{17,9},{25,1},{2,26},{10... | collective-permute-start | bytes 786440 | tf_op jit(solution)/shard_map/ppermute | solution.py:386
  13.0 16.8 %collective-permute-start = (bf16[1024,1024]{1,0:T(8,128)(2,1)}, bf16[1024,1024]{1,0:T(8,128)(2,1)}, u32[]{:S(2)}, u32[]{:S(2)}) collective-permute-start(bf16[1024,1024]{1,0:T(8,128)(2,1)} %take_tiles.2.refs_0_), channel_id=1, source_target_pairs={{0,2},{2,0},{4,6},{6,4},{1,3},{3,1},{5,7},{7,5},{8,10},{10,8},{12,... | collective-permute-start | bytes 6291464 | tf_op jit(solution)/shard_map/ppermute | solution.py:403
  22.0 21.6 %collective-permute-start.7 = (bf16[1024,3072]{1,0:T(8,128)(2,1)}, bf16[1024,3072]{1,0:T(8,128)(2,1)}, u32[]{:S(2)}, u32[]{:S(2)}) collective-permute-start(bf16[1024,3072]{1,0:T(8,128)(2,1)} %take_tiles.3.refs_12_), channel_id=1, source_target_pairs={{0,2},{2,0},{4,6},{6,4},{1,3},{3,1},{5,7},{7,5},{8,10},{10,8},{12,... | collective-permute-start | bytes 18874376 | tf_op jit(solution)/shard_map/ppermute | solution.py:403
  22.5 6.5 %collective-permute-start.3 = (bf16[128,1024]{1,0:T(8,128)(2,1)S(1)}, bf16[128,1024]{1,0:T(8,128)(2,1)S(1)}, u32[]{:S(2)}, u32[]{:S(2)}) collective-permute-start(bf16[128,1024]{1,0:T(8,128)(2,1)S(1)} %collective-permute-done.2.refs_6_.refs_4_.refs_5_), channel_id=1, source_target_pairs={{0,2},{2,0},{4,6},{6,4},{1,3},{3,1},{5,7},{7,5},{8,10},{10,8},{12,... | collective-permute-start | bytes 786440 | tf_op jit(solution)/shard_map/ppermute | solution.py:387
  22.6 7.2 %collective-permute-start.5 = (bf16[128,1024]{1,0:T(8,128)(2,1)S(1)}, bf16[128,1024]{1,0:T(8,128)(2,1)S(1)}, u32[]{:S(2)}, u32[]{:S(2)}) collective-permute-start(bf16[128,1024]{1,0:T(8,128)(2,1)S(1)} %collective-permute-done.4.refs_8_.refs_6_.refs_7_), channel_id=1, source_target_pairs={{0,2},{2,0},{4,6},{6,4},{1,3},{3,1},{5,7},{7,5},{8,10},{10,8},{12,... | collective-permute-start | bytes 786440 | tf_op jit(solution)/shard_map/ppermute | solution.py:387
  29.8 12.2 %copy-start.15 = (s32[128]{0:T(128)S(1)}, s32[128]{0:T(128)}, u32[]{:S(2)}) copy-start(s32[128]{0:T(128)} %param.11) | copy-start | bytes 1540
  41.4 24.9 %collective-permute-start.6 = (bf16[1024,2048]{1,0:T(8,128)(2,1)}, bf16[1024,2048]{1,0:T(8,128)(2,1)}, u32[]{:S(2)}, u32[]{:S(2)}) collective-permute-start(bf16[1024,2048]{1,0:T(8,128)(2,1)} %get-tuple-element.46), channel_id=1, source_target_pairs={{0,2},{2,0},{4,6},{6,4},{1,3},{3,1},{5,7},{7,5},{8,10},{10,8},{12,... | collective-permute-start | bytes 12582920 | tf_op jit(solution)/shard_map/ppermute | solution.py:403
  41.6 24.8 %collective-permute-start.10 = (bf16[1024,2048]{1,0:T(8,128)(2,1)}, bf16[1024,2048]{1,0:T(8,128)(2,1)}, u32[]{:S(2)}, u32[]{:S(2)}) collective-permute-start(bf16[1024,2048]{1,0:T(8,128)(2,1)} %get-tuple-element.56), channel_id=1, source_target_pairs={{0,2},{2,0},{4,6},{6,4},{1,3},{3,1},{5,7},{7,5},{8,10},{10,8},{12,... | collective-permute-start | bytes 12582920 | tf_op jit(solution)/shard_map/ppermute | solution.py:403
  41.9 15.1 %collective-permute-start.8 = (bf16[128,1024]{1,0:T(8,128)(2,1)}, bf16[128,1024]{1,0:T(8,128)(2,1)S(1)}, u32[]{:S(2)}, u32[]{:S(2)}) collective-permute-start(bf16[128,1024]{1,0:T(8,128)(2,1)} %get-tuple-element.50), channel_id=1, source_target_pairs={{0,16},{8,24},{16,0},{24,8},{1,17},{9,25},{17,1},{25,9},{2,18},{10... | collective-permute-start | bytes 786440 | tf_op jit(solution)/shard_map/ppermute | solution.py:386
  42.0 23.5 %collective-permute-start.11 = (bf16[256,1024]{1,0:T(8,128)(2,1)}, bf16[256,1024]{1,0:T(8,128)(2,1)S(1)}, u32[]{:S(2)}, u32[]{:S(2)}) collective-permute-start(bf16[256,1024]{1,0:T(8,128)(2,1)} %copy-done.11), channel_id=1, source_target_pairs={{0,4},{2,6},{4,0},{6,2},{1,5},{3,7},{5,1},{7,3},{8,12},{10,14},{12... | collective-permute-start | bytes 1572872 | tf_op jit(solution)/shard_map/ppermute | solution.py:441
  57.0 9.3 %collective-permute-start.9 = (bf16[128,1024]{1,0:T(8,128)(2,1)S(1)}, bf16[128,1024]{1,0:T(8,128)(2,1)S(1)}, u32[]{:S(2)}, u32[]{:S(2)}) collective-permute-start(bf16[128,1024]{1,0:T(8,128)(2,1)S(1)} %collective-permute-done.8.refs_11_), channel_id=1, source_target_pairs={{0,2},{2,0},{4,6},{6,4},{1,3},{3,1},{5,7},{7,5},{8,10},{10,8},{12,... | collective-permute-start | bytes 786440 | tf_op jit(solution)/shard_map/ppermute | solution.py:469
  57.0 9.3 %copy-start.7 = (bf16[2048,1024]{1,0:T(8,128)(2,1)S(1)}, bf16[2048,1024]{1,0:T(8,128)(2,1)}, u32[]{:S(2)}) copy-start(bf16[2048,1024]{1,0:T(8,128)(2,1)} %get-tuple-element.53.refs_4_) | copy-start | bytes 12582916
  57.0 9.3 %copy-start.10 = (bf16[256,1024]{1,0:T(8,128)(2,1)S(1)}, bf16[256,1024]{1,0:T(8,128)(2,1)}, u32[]{:S(2)}) copy-start(bf16[256,1024]{1,0:T(8,128)(2,1)} %copy-done.9) | copy-start | bytes 1572868
  57.0 18.6 %collective-permute-start.14 = (bf16[256,1024]{1,0:T(8,128)(2,1)S(1)}, bf16[256,1024]{1,0:T(8,128)(2,1)S(1)}, u32[]{:S(2)}, u32[]{:S(2)}) collective-permute-start(bf16[256,1024]{1,0:T(8,128)(2,1)S(1)} %get-tuple-element.48.refs_10_), channel_id=1, source_target_pairs={{0,4},{2,6},{4,0},{6,2},{1,5},{3,7},{5,1},{7,3},{8,12},{10,14},{12... | collective-permute-start | bytes 1572872 | tf_op jit(solution)/shard_map/ppermute | solution.py:441
  65.6 20.5 %collective-permute-start.15 = (bf16[256,1024]{1,0:T(8,128)(2,1)S(1)}, bf16[256,1024]{1,0:T(8,128)(2,1)S(1)}, u32[]{:S(2)}, u32[]{:S(2)}) collective-permute-start(bf16[256,1024]{1,0:T(8,128)(2,1)S(1)} %get-tuple-element.55.refs_14_), channel_id=1, source_target_pairs={{0,4},{2,6},{4,0},{6,2},{1,5},{3,7},{5,1},{7,3},{8,12},{10,14},{12... | collective-permute-start | bytes 1572872 | tf_op jit(solution)/shard_map/ppermute | solution.py:441
  66.4 9.3 %copy-start.8 = (bf16[2048,1024]{1,0:T(8,128)(2,1)S(1)}, bf16[2048,1024]{1,0:T(8,128)(2,1)}, u32[]{:S(2)}) copy-start(bf16[2048,1024]{1,0:T(8,128)(2,1)} %get-tuple-element.60.refs_4_) | copy-start | bytes 12582916
  73.7 20.8 %collective-permute-start.12 = (bf16[256,1024]{1,0:T(8,128)(2,1)S(1)}, bf16[256,1024]{1,0:T(8,128)(2,1)S(1)}, u32[]{:S(2)}, u32[]{:S(2)}) collective-permute-start(bf16[256,1024]{1,0:T(8,128)(2,1)S(1)} %get-tuple-element.58.refs_2_), channel_id=1, source_target_pairs={{0,4},{2,6},{4,0},{6,2},{1,5},{3,7},{5,1},{7,3},{8,12},{10,14},{12... | collective-permute-start | bytes 1572872 | tf_op jit(solution)/shard_map/ppermute | solution.py:449
  75.3 19.2 %collective-permute-start.13 = (bf16[256,1024]{1,0:T(8,128)(2,1)S(1)}, bf16[256,1024]{1,0:T(8,128)(2,1)S(1)}, u32[]{:S(2)}, u32[]{:S(2)}) collective-permute-start(bf16[256,1024]{1,0:T(8,128)(2,1)S(1)} %add_terms.8.refs_14_), channel_id=1, source_target_pairs={{0,8},{8,0},{16,24},{24,16},{1,9},{9,1},{17,25},{25,17},{2,10},{10... | collective-permute-start | bytes 1572872 | tf_op jit(solution)/shard_map/ppermute | solution.py:454
  82.8 26.7 %collective-permute-start.16 = (bf16[256,1024]{1,0:T(8,128)(2,1)S(1)}, bf16[256,1024]{1,0:T(8,128)(2,1)S(1)}, u32[]{:S(2)}, u32[]{:S(2)}) collective-permute-start(bf16[256,1024]{1,0:T(8,128)(2,1)S(1)} %get-tuple-element.63.refs_2_), channel_id=1, source_target_pairs={{0,4},{2,6},{4,0},{6,2},{1,5},{3,7},{5,1},{7,3},{8,12},{10,14},{12... | collective-permute-start | bytes 1572872 | tf_op jit(solution)/shard_map/ppermute | solution.py:449
  84.0 25.6 %collective-permute-start.17 = (bf16[256,1024]{1,0:T(8,128)(2,1)S(1)}, bf16[256,1024]{1,0:T(8,128)(2,1)S(1)}, u32[]{:S(2)}, u32[]{:S(2)}) collective-permute-start(bf16[256,1024]{1,0:T(8,128)(2,1)S(1)} %add_terms.9.refs_10_), channel_id=1, source_target_pairs={{0,8},{8,0},{16,24},{24,16},{1,9},{9,1},{17,25},{25,17},{2,10},{10... | collective-permute-start | bytes 1572872 | tf_op jit(solution)/shard_map/ppermute | solution.py:454
  93.3 23.5 %collective-permute-start.19 = (bf16[256,1024]{1,0:T(8,128)(2,1)S(1)}, bf16[256,1024]{1,0:T(8,128)(2,1)S(1)}, u32[]{:S(2)}, u32[]{:S(2)}) collective-permute-start(bf16[256,1024]{1,0:T(8,128)(2,1)S(1)} %get-tuple-element.64.refs_3_), channel_id=1, source_target_pairs={{0,4},{2,6},{4,0},{6,2},{1,5},{3,7},{5,1},{7,3},{8,12},{10,14},{12... | collective-permute-start | bytes 1572872 | tf_op jit(solution)/shard_map/ppermute | solution.py:441
  94.7 13.8 %collective-permute-start.18 = (bf16[128,1024]{1,0:T(8,128)(2,1)S(1)}, bf16[128,1024]{1,0:T(8,128)(2,1)S(1)}, u32[]{:S(2)}, u32[]{:S(2)}) collective-permute-start(bf16[128,1024]{1,0:T(8,128)(2,1)S(1)} %add_terms.10.refs_14_), channel_id=1, source_target_pairs={{0,16},{8,24},{16,0},{24,8},{1,17},{9,25},{17,1},{25,9},{2,18},{10... | collective-permute-start | bytes 786440 | tf_op jit(solution)/shard_map/ppermute | solution.py:459
  102.4 14.4 %copy-start.6 = (bf16[2048,1024]{1,0:T(8,128)(2,1)S(1)}, bf16[2048,1024]{1,0:T(8,128)(2,1)}, u32[]{:S(2)}) copy-start(bf16[2048,1024]{1,0:T(8,128)(2,1)} %get-tuple-element.68.refs_4_) | copy-start | bytes 12582916
  111.0 14.3 %collective-permute-start.21 = (bf16[128,1024]{1,0:T(8,128)(2,1)S(1)}, bf16[128,1024]{1,0:T(8,128)(2,1)S(1)}, u32[]{:S(2)}, u32[]{:S(2)}) collective-permute-start(bf16[128,1024]{1,0:T(8,128)(2,1)S(1)} %add_terms.12.refs_14_), channel_id=1, source_target_pairs={{0,16},{8,24},{16,0},{24,8},{1,17},{9,25},{17,1},{25,9},{2,18},{10... | collective-permute-start | bytes 786440 | tf_op jit(solution)/shard_map/ppermute | solution.py:459
  111.1 18.1 %collective-permute-start.24 = (bf16[256,1024]{1,0:T(8,128)(2,1)S(1)}, bf16[256,1024]{1,0:T(8,128)(2,1)S(1)}, u32[]{:S(2)}, u32[]{:S(2)}) collective-permute-start(bf16[256,1024]{1,0:T(8,128)(2,1)S(1)} %add_terms.11.refs_4_), channel_id=1, source_target_pairs={{0,8},{8,0},{16,24},{24,16},{1,9},{9,1},{17,25},{25,17},{2,10},{10... | collective-permute-start | bytes 1572872 | tf_op jit(solution)/shard_map/ppermute | solution.py:454
  112.8 16.4 %collective-permute-start.23 = (bf16[256,1024]{1,0:T(8,128)(2,1)S(1)}, bf16[256,1024]{1,0:T(8,128)(2,1)S(1)}, u32[]{:S(2)}, u32[]{:S(2)}) collective-permute-start(bf16[256,1024]{1,0:T(8,128)(2,1)S(1)} %get-tuple-element.66.refs_2_), channel_id=1, source_target_pairs={{0,4},{2,6},{4,0},{6,2},{1,5},{3,7},{5,1},{7,3},{8,12},{10,14},{12... | collective-permute-start | bytes 1572872 | tf_op jit(solution)/shard_map/ppermute | solution.py:449
  123.7 15.0 %collective-permute-start.20 = (bf16[256,1024]{1,0:T(8,128)(2,1)S(1)}, bf16[256,1024]{1,0:T(8,128)(2,1)S(1)}, u32[]{:S(2)}, u32[]{:S(2)}) collective-permute-start(bf16[256,1024]{1,0:T(8,128)(2,1)S(1)} %get-tuple-element.73.refs_5_), channel_id=1, source_target_pairs={{0,4},{2,6},{4,0},{6,2},{1,5},{3,7},{5,1},{7,3},{8,12},{10,14},{12... | collective-permute-start | bytes 1572872 | tf_op jit(solution)/shard_map/ppermute | solution.py:449
  127.8 18.4 %collective-permute-start.22 = (bf16[256,1024]{1,0:T(8,128)(2,1)S(1)}, bf16[256,1024]{1,0:T(8,128)(2,1)S(1)}, u32[]{:S(2)}, u32[]{:S(2)}) collective-permute-start(bf16[256,1024]{1,0:T(8,128)(2,1)S(1)} %add_terms.13.refs_3_), channel_id=1, source_target_pairs={{0,8},{8,0},{16,24},{24,16},{1,9},{9,1},{17,25},{25,17},{2,10},{10... | collective-permute-start | bytes 1572872 | tf_op jit(solution)/shard_map/ppermute | solution.py:454
  129.5 17.1 %collective-permute-start.26 = (bf16[128,1024]{1,0:T(8,128)(2,1)S(1)}, bf16[128,1024]{1,0:T(8,128)(2,1)S(1)}, u32[]{:S(2)}, u32[]{:S(2)}) collective-permute-start(bf16[128,1024]{1,0:T(8,128)(2,1)S(1)} %add_terms.14.refs_3_), channel_id=1, source_target_pairs={{0,16},{8,24},{16,0},{24,8},{1,17},{9,25},{17,1},{25,9},{2,18},{10... | collective-permute-start | bytes 786440 | tf_op jit(solution)/shard_map/ppermute | solution.py:459
  146.5 11.8 %collective-permute-start.25 = (bf16[128,1024]{1,0:T(8,128)(2,1)S(1)}, bf16[128,1024]{1,0:T(8,128)(2,1)S(1)}, u32[]{:S(2)}, u32[]{:S(2)}) collective-permute-start(bf16[128,1024]{1,0:T(8,128)(2,1)S(1)} %add_terms.15.refs_5_), channel_id=1, source_target_pairs={{0,16},{8,24},{16,0},{24,8},{1,17},{9,25},{17,1},{25,9},{2,18},{10... | collective-permute-start | bytes 786440 | tf_op jit(solution)/shard_map/ppermute | solution.py:459
  (11 other events, 36.5 us)

commit v5 on v4

--- a/solution.py
+++ b/solution.py
@@ -467,21 +467,21 @@
     k1 = first(1, (done,))
     done = first(2, (k1,))
     all_lines = [*first_lines, [x2, over_core(lax.optimization_barrier((x2, k1))[0])]]
-    done = second(0, (done, received["own", 1][0], received["own", 2][0], far_y[0]))
+    done = second(0, (done, received["own", 1][0], received["own", 2][0], far_y[0], far_y[1]))
     done = to_z1(0, (done,))
     done = second(1, (done, far_y[1]))
     done = to_z1(1, (done,))
-    done = first(3, (done, far_y[2]))
+    done = second(2, (done, far_y[2]))
     done = to_z2(0, (done,))
-    done = second(2, (done,))
     done = to_z1(2, (done,))
+    done = first(3, (done, near_z[1]))
     cosine, sine_part = turn_tables(lax.optimization_barrier((hidden, done))[0], positions)
     out = finish(0, None, (done,))
     done = to_z2(1, (out,))
-    done = second(3, (done, far_y[3]))
+    done = second(3, (done,))
+    done = to_z2(2, (done,))
     out = finish(1, out, (done,))
     done = to_z1(3, (out,))
-    done = to_z2(2, (done,))
     done = to_z2(3, (done,))
     out = finish(2, out, (done,))
     return finish(3, out, ())

time: 160 us -> 158 us (0.988)
  waiting for transfers between devices: 47.9 us -> 40 us
  starting transfers between devices: 22.1 us -> 25.6 us
  Pallas kernels: 77.2 us -> 79 us
    ppermute x4, waiting for transfers between devices: 8.84 us -> 2.02 us  [second(): mid_y[i] = over_y(half)]
    ppermute x4, waiting for transfers between devices: 8.82 us -> 15.4 us  [to_z1(): near_z[i] = over_z1(operand)]
    ppermute x4, waiting for transfers between devices: 15.8 us -> 10.1 us  [to_z2(): far_z[i] = over_z2(operand)]
    ppermute x4, starting transfers between devices: 0.7 us -> 3.66 us  [to_z2(): far_z[i] = over_z2(operand)]
    pallas_call x8, Pallas kernels: 2.01 us -> 3.94 us  [added(): pl.pallas_call(functools.partial(add_kernel, len(terms)), grid=(columns /...]
    ppermute x4, starting transfers between devices: 3.92 us -> 5.54 us  [to_z1(): near_z[i] = over_z1(operand)]
    unnamed x32 -> x36, local copies, waits for them, and re-layouts: 8.94 us -> 9.74 us
  transfers between devices with their start and end apart: 27 -> 27, of which waited for: 9 -> 9; matrix products, arithmetic and copies ran while one was open for 2% -> 2% of each run, Pallas kernels for 48% -> 50%
where the time goes in v5:
time: 158 us; the launch traced here: 157 us
  Pallas kernels  79 us (50%)
  waiting for transfers between devices  40 us (25%)
  starting transfers between devices  25.6 us (16%)
  local copies, waits for them, and re-layouts  11 us (7%)
    pallas_call x8, Pallas kernels, merge_pass(): pl.pallas_call(functools.partial(pass_kernel, len(bases), [len(line) for...  59.6 us
    ppermute x4, waiting for transfers between devices, to_z1(): near_z[i] = over_z1(operand)  15.4 us
    pallas_call x2, Pallas kernels, take_tiles(): pl.pallas_call(take_kernel, grid_spec=pltpu.PrefetchScalarGridSpec(num_sc...  10.1 us
    ppermute x4, waiting for transfers between devices, to_z2(): far_z[i] = over_z2(operand)  10.1 us
    unnamed x36, local copies, waits for them, and re-layouts  9.74 us
    ppermute x2, waiting for transfers between devices, line_shards(): first_lines = [[x1, over_core(x1)], [x3, over_core(x3)], [own_x, own_other]]  6.56 us
    ppermute x4, starting transfers between devices, to_z1(): near_z[i] = over_z1(operand)  5.54 us
    ppermute x4, starting transfers between devices, second(): mid_y[i] = over_y(half)  5.17 us
  transfers between devices with their start and end apart: 27, of which 9 were waited for; matrix products, arithmetic and copies ran while one was open for 2% of the time, Pallas kernels for 50%

profile of v5, /device:TPU:0, one launch (start us, length us, event | category | flops | bytes accessed | tf_op | source)
XLA Modules:
  0.0 157.4 jit_solution(9955119179367317581)
XLA Ops:
  1.3 2.2 %copy-done = bf16[128,16384]{1,0:T(8,128)(2,1)S(1)} copy-done((bf16[128,16384]{1,0:T(8,128)(2,1)S(1)}, bf16[128,16384]{1,0:T(8,128)(2,1)}, u32[]{:S(2)}) %copy-start) | copy-done | bytes 4194328
  3.5 1.3 pick_features.1
  4.9 2.6 %collective-permute-start.2 = (bf16[128,1024]{1,0:T(8,128)(2,1)S(1)}, bf16[128,1024]{1,0:T(8,128)(2,1)S(1)}, u32[]{:S(2)}, u32[]{:S(2)}) collective-permute-start(bf16[128,1024]{1,0:T(8,128)(2,1)S(1)} %get-tuple-element.43), channel_id=1, source_target_pairs={{0,8},{8,0},{16,24},{24,16},{1,9},{9,1},{17,25},{25,17},{2,10},{10... | collective-permute-start | bytes 786440 | tf_op jit(solution)/shard_map/ppermute | solution.py:386
  7.4 2.5 %collective-permute-start.4 = (bf16[128,1024]{1,0:T(8,128)(2,1)S(1)}, bf16[128,1024]{1,0:T(8,128)(2,1)S(1)}, u32[]{:S(2)}, u32[]{:S(2)}) collective-permute-start(bf16[128,1024]{1,0:T(8,128)(2,1)S(1)} %get-tuple-element.44), channel_id=1, source_target_pairs={{0,24},{8,16},{16,8},{24,0},{1,25},{9,17},{17,9},{25,1},{2,26},{10... | collective-permute-start | bytes 786440 | tf_op jit(solution)/shard_map/ppermute | solution.py:386
  9.9 3.1 %take_tiles.2.refs_0_ = bf16[1024,1024]{1,0:T(8,128)(2,1)} custom-call(s32[1]{0:T(128)} %bitcast.4.table, bf16[1024,16384]{1,0:T(8,128)(2,1)} %refs_0_.17, bf16[128,1024]{1,0:T(8,128)(2,1)S(1)} %get-tuple-element.42.refs_0_.refs_10_.refs_8_.refs_9_), custom_call_target="tpu_custom_call" | custom-call | tf_op jit(solution)/shard_map/take_tiles/pallas_call | solution.py:274
  13.4 1.6 %copy-done.4 = bf16[1024,1024]{1,0:T(8,128)(2,1)S(1)} copy-done((bf16[1024,1024]{1,0:T(8,128)(2,1)S(1)}, bf16[1024,1024]{1,0:T(8,128)(2,1)}, u32[]{:S(2)}) %copy-start.4) | copy-done | bytes 2097176
  15.0 7.0 %take_tiles.3.refs_12_ = bf16[1024,3072]{1,0:T(8,128)(2,1)} custom-call(s32[3]{0:T(128)S(1)} %pad_add_fusion.table, bf16[1024,16384]{1,0:T(8,128)(2,1)} %refs_0_.17, bf16[1024,1024]{1,0:T(8,128)(2,1)S(1)} %copy-done.4, bf16[2048,32]{1,0:T(8,128)(2,1)S(1)} %copy.17.refs_1_.refs_4_.refs_2_), custom_call_target="tpu_custom_call" | custom-call | tf_op jit(solution)/shard_map/take_tiles/pallas_call | solution.py:274
  23.2 5.8 %collective-permute-done.3.refs_7_.refs_5_.refs_6_ = bf16[128,1024]{1,0:T(8,128)(2,1)S(1)} collective-permute-done((bf16[128,1024]{1,0:T(8,128)(2,1)S(1)}, bf16[128,1024]{1,0:T(8,128)(2,1)S(1)}, u32[]{:S(2)}, u32[]{:S(2)}) %collective-permute-start.3) | collective-permute-done | bytes 262176 | tf_op jit(solution)/shard_map/ppermute | solution.py:387
  29.8 10.0 %merge_pass.8 = (bf16[2048,1024]{1,0:T(8,128)(2,1)}, bf16[256,1024]{1,0:T(8,128)(2,1)S(1)}, bf16[256,1024]{1,0:T(8,128)(2,1)S(1)}, bf16[1024,2048]{1,0:T(8,128)(2,1)}, bf16[1024,2048]{1,0:T(8,128)(2,1)}) custom-call(s32[6]{0:T(128)S(1)} %concatenate.13.table, bf16[1024,16384]{1,0:T(8,128)(2,1)} %refs_0_.17, bf16[1024,16384]{1,0:T(8,128)(2,1)} %refs_0_.17, ...), custom_call_target="tpu_custom_call" | custom-call | flops 1610612736 | bytes 8388608 | tf_op jit(solution)/shard_map/merge_pass/pallas_call | solution.py:248
  42.0 1.6 %collective-permute-start.11 = (bf16[256,1024]{1,0:T(8,128)(2,1)}, bf16[256,1024]{1,0:T(8,128)(2,1)}, u32[]{:S(2)}, u32[]{:S(2)}) collective-permute-start(bf16[256,1024]{1,0:T(8,128)(2,1)} %copy-done.13), channel_id=1, source_target_pairs={{0,4},{2,6},{4,0},{6,2},{1,5},{3,7},{5,1},{7,3},{8,12},{10,14},{12... | collective-permute-start | bytes 1572872 | tf_op jit(solution)/shard_map/ppermute | solution.py:441
  44.6 7.0 %merge_pass.9 = (bf16[2048,1024]{1,0:T(8,128)(2,1)}, bf16[256,1024]{1,0:T(8,128)(2,1)}, bf16[256,1024]{1,0:T(8,128)(2,1)S(1)}) custom-call(s32[2]{0:T(128)S(1)} %iota_add_fusion.3.table, bf16[1024,16384]{1,0:T(8,128)(2,1)} %refs_0_.17, bf16[1024,3072]{1,0:T(8,128)(2,1)} %collective-permute-done.8.refs_1_, bf16[2048,32]{1,0:T(8,128)(2,1)S(1)} %copy.17.refs_1_.refs_4_.refs_2_, ...), custom_call_target="tpu_custom_call" | custom-call | flops 1610612736 | bytes 8388608 | tf_op jit(solution)/shard_map/merge_pass/pallas_call | solution.py:248
  52.9 4.1 %collective-permute-done.9.refs_11_ = bf16[128,1024]{1,0:T(8,128)(2,1)S(1)} collective-permute-done((bf16[128,1024]{1,0:T(8,128)(2,1)}, bf16[128,1024]{1,0:T(8,128)(2,1)S(1)}, u32[]{:S(2)}, u32[]{:S(2)}) %collective-permute-start.9) | collective-permute-done | bytes 262176 | tf_op jit(solution)/shard_map/ppermute | solution.py:386
  57.1 7.2 %merge_pass.10 = (bf16[2048,1024]{1,0:T(8,128)(2,1)}, bf16[256,1024]{1,0:T(8,128)(2,1)S(1)}, bf16[256,1024]{1,0:T(8,128)(2,1)S(1)}) custom-call(s32[2]{0:T(128)S(1)} %iota_add_fusion.4.table, bf16[1024,16384]{1,0:T(8,128)(2,1)} %refs_0_.17, bf16[1024,3072]{1,0:T(8,128)(2,1)} %collective-permute-done.8.refs_1_, ...), custom_call_target="tpu_custom_call" | custom-call | flops 1610612736 | bytes 8388608 | tf_op jit(solution)/shard_map/merge_pass/pallas_call | solution.py:248
  64.3 1.5 collective-permute-start.13
  65.8 1.9 %collective-permute-done.12.refs_18_.refs_15_.refs_1_ = bf16[256,1024]{1,0:T(8,128)(2,1)} collective-permute-done((bf16[256,1024]{1,0:T(8,128)(2,1)}, bf16[256,1024]{1,0:T(8,128)(2,1)}, u32[]{:S(2)}, u32[]{:S(2)}) %collective-permute-start.12) | collective-permute-done | bytes 524320 | tf_op jit(solution)/shard_map/ppermute | solution.py:441
  67.7 7.3 %merge_pass.11 = (bf16[256,1024]{1,0:T(8,128)(2,1)S(1)}, bf16[256,1024]{1,0:T(8,128)(2,1)S(1)}, bf16[128,1024]{1,0:T(8,128)(2,1)S(1)}, bf16[128,1024]{1,0:T(8,128)(2,1)S(1)}) custom-call(s32[2]{0:T(128)S(1)} %iota_add_fusion.1.table, bf16[1024,16384]{1,0:T(8,128)(2,1)} %refs_0_.17, ...), custom_call_target="tpu_custom_call", output_to_operand_aliasing={{0}: (14, {})} | custom-call | flops 2147483648 | bytes 8388608 | tf_op jit(solution)/shard_map/merge_pass/pallas_call | solution.py:248
  75.0 1.6 collective-permute-start.14
  77.7 2.7 %collective-permute-start.15 = (bf16[256,1024]{1,0:T(8,128)(2,1)S(1)}, bf16[256,1024]{1,0:T(8,128)(2,1)S(1)}, u32[]{:S(2)}, u32[]{:S(2)}) collective-permute-start(bf16[256,1024]{1,0:T(8,128)(2,1)S(1)} %add_terms.8.refs_14_), channel_id=1, source_target_pairs={{0,8},{8,0},{16,24},{24,16},{1,9},{9,1},{17,25},{25,17},{2,10},{10... | collective-permute-start | bytes 1572872 | tf_op jit(solution)/shard_map/ppermute | solution.py:454
  80.4 7.2 %merge_pass.12 = (bf16[256,1024]{1,0:T(8,128)(2,1)S(1)}, bf16[256,1024]{1,0:T(8,128)(2,1)S(1)}, bf16[128,1024]{1,0:T(8,128)(2,1)S(1)}, bf16[128,1024]{1,0:T(8,128)(2,1)S(1)}) custom-call(s32[2]{0:T(128)S(1)} %iota_add_fusion.2.table, bf16[1024,16384]{1,0:T(8,128)(2,1)} %refs_0_.17, ...), custom_call_target="tpu_custom_call", output_to_operand_aliasing={{0}: (14, {})} | custom-call | flops 2147483648 | bytes 8388608 | tf_op jit(solution)/shard_map/merge_pass/pallas_call | solution.py:248
  87.7 1.3 add_terms.9.refs_14_
  90.0 7.0 %merge_pass.13 = (bf16[256,1024]{1,0:T(8,128)(2,1)S(1)}, bf16[256,1024]{1,0:T(8,128)(2,1)S(1)}, bf16[128,1024]{1,0:T(8,128)(2,1)S(1)}, bf16[128,1024]{1,0:T(8,128)(2,1)S(1)}) custom-call(s32[2]{0:T(128)S(1)} %iota_add_fusion.5.table, bf16[1024,16384]{1,0:T(8,128)(2,1)} %refs_0_.17, ...), custom_call_target="tpu_custom_call", output_to_operand_aliasing={{0}: (14, {})} | custom-call | flops 2147483648 | bytes 8388608 | tf_op jit(solution)/shard_map/merge_pass/pallas_call | solution.py:248
  97.0 1.6 %collective-permute-start.22 = (bf16[256,1024]{1,0:T(8,128)(2,1)S(1)}, bf16[256,1024]{1,0:T(8,128)(2,1)S(1)}, u32[]{:S(2)}, u32[]{:S(2)}) collective-permute-start(bf16[256,1024]{1,0:T(8,128)(2,1)S(1)} %get-tuple-element.65.refs_3_), channel_id=1, source_target_pairs={{0,4},{2,6},{4,0},{6,2},{1,5},{3,7},{5,1},{7,3},{8,12},{10,14},{12... | collective-permute-start | bytes 1572872 | tf_op jit(solution)/shard_map/ppermute | solution.py:449
  98.8 3.0 %collective-permute-start.18 = (bf16[128,1024]{1,0:T(8,128)(2,1)S(1)}, bf16[128,1024]{1,0:T(8,128)(2,1)S(1)}, u32[]{:S(2)}, u32[]{:S(2)}) collective-permute-start(bf16[128,1024]{1,0:T(8,128)(2,1)S(1)} %add_terms.10.refs_2_), channel_id=1, source_target_pairs={{0,16},{8,24},{16,0},{24,8},{1,17},{9,25},{17,1},{25,9},{2,18},{10... | collective-permute-start | bytes 786440 | tf_op jit(solution)/shard_map/ppermute | solution.py:459
  102.9 5.5 %collective-permute-done.16.refs_11_.refs_2_ = bf16[256,1024]{1,0:T(8,128)(2,1)S(1)} collective-permute-done((bf16[256,1024]{1,0:T(8,128)(2,1)S(1)}, bf16[256,1024]{1,0:T(8,128)(2,1)S(1)}, u32[]{:S(2)}, u32[]{:S(2)}) %collective-permute-start.16) | collective-permute-done | bytes 524320 | tf_op jit(solution)/shard_map/ppermute | solution.py:454
  108.5 6.9 %merge_pass.14 = (bf16[2048,1024]{1,0:T(8,128)(2,1)}, bf16[256,1024]{1,0:T(8,128)(2,1)S(1)}, bf16[256,1024]{1,0:T(8,128)(2,1)S(1)}) custom-call(s32[2]{0:T(128)S(1)} %iota_add_fusion.7.table, bf16[1024,16384]{1,0:T(8,128)(2,1)} %refs_0_.17, bf16[1024,2048]{1,0:T(8,128)(2,1)} %collective-permute-done.6.refs_15_.refs_1_, ...), custom_call_target="tpu_custom_call" | custom-call | flops 1610612736 | bytes 8388608 | tf_op jit(solution)/shard_map/merge_pass/pallas_call | solution.py:248
  118.1 1.2 copy-done.2
  119.6 7.0 %merge_pass.15 = (bf16[256,1024]{1,0:T(8,128)(2,1)S(1)}, bf16[256,1024]{1,0:T(8,128)(2,1)S(1)}, bf16[128,1024]{1,0:T(8,128)(2,1)S(1)}, bf16[128,1024]{1,0:T(8,128)(2,1)S(1)}) custom-call(s32[2]{0:T(128)S(1)} %iota_add_fusion.table, bf16[1024,16384]{1,0:T(8,128)(2,1)} %refs_0_.17, ...), custom_call_target="tpu_custom_call", output_to_operand_aliasing={{0}: (14, {})} | custom-call | flops 2147483648 | bytes 8388608 | tf_op jit(solution)/shard_map/merge_pass/pallas_call | solution.py:248
  126.6 1.4 collective-permute-start.19
  131.5 1.9 %collective-permute-start.24 = (bf16[256,1024]{1,0:T(8,128)(2,1)S(1)}, bf16[256,1024]{1,0:T(8,128)(2,1)S(1)}, u32[]{:S(2)}, u32[]{:S(2)}) collective-permute-start(bf16[256,1024]{1,0:T(8,128)(2,1)S(1)} %add_terms.14.refs_3_), channel_id=1, source_target_pairs={{0,8},{8,0},{16,24},{24,16},{1,9},{9,1},{17,25},{25,17},{2,10},{10... | collective-permute-start | bytes 1572872 | tf_op jit(solution)/shard_map/ppermute | solution.py:454
  133.8 2.0 %collective-permute-done.19.refs_1_ = bf16[256,1024]{1,0:T(8,128)(2,1)S(1)} collective-permute-done((bf16[256,1024]{1,0:T(8,128)(2,1)S(1)}, bf16[256,1024]{1,0:T(8,128)(2,1)S(1)}, u32[]{:S(2)}, u32[]{:S(2)}) %collective-permute-start.19) | collective-permute-done | bytes 524320 | tf_op jit(solution)/shard_map/ppermute | solution.py:449
  135.9 9.8 %collective-permute-done.24.refs_2_ = bf16[256,1024]{1,0:T(8,128)(2,1)S(1)} collective-permute-done((bf16[256,1024]{1,0:T(8,128)(2,1)S(1)}, bf16[256,1024]{1,0:T(8,128)(2,1)S(1)}, u32[]{:S(2)}, u32[]{:S(2)}) %collective-permute-start.24) | collective-permute-done | bytes 524320 | tf_op jit(solution)/shard_map/ppermute | solution.py:454
  147.0 9.4 %collective-permute-done.25.refs_3_ = bf16[128,1024]{1,0:T(8,128)(2,1)S(1)} collective-permute-done((bf16[128,1024]{1,0:T(8,128)(2,1)S(1)}, bf16[128,1024]{1,0:T(8,128)(2,1)S(1)}, u32[]{:S(2)}, u32[]{:S(2)}) %collective-permute-start.25) | collective-permute-done | bytes 262176 | tf_op jit(solution)/shard_map/ppermute | solution.py:459
  (102 shorter events, 20.7 us)
Async XLA Ops:
  0.0 13.1 %collective-permute-start.1 = (bf16[1024,32]{0,1:T(8,128)(2,1)}, bf16[1024,32]{0,1:T(8,128)(2,1)S(1)}, u32[]{:S(2)}, u32[]{:S(2)}) collective-permute-start(bf16[1024,32]{0,1:T(8,128)(2,1)} %param.8), channel_id=1, source_target_pairs={{0,2},{2,0},{4,6},{6,4},{1,3},{3,1},{5,7},{7,5},{8,10},{10,8},{12,... | collective-permute-start | bytes 196616 | tf_op jit(solution)/shard_map/ppermute | solution.py:389
  4.9 17.6 %collective-permute-start.2 = (bf16[128,1024]{1,0:T(8,128)(2,1)S(1)}, bf16[128,1024]{1,0:T(8,128)(2,1)S(1)}, u32[]{:S(2)}, u32[]{:S(2)}) collective-permute-start(bf16[128,1024]{1,0:T(8,128)(2,1)S(1)} %get-tuple-element.43), channel_id=1, source_target_pairs={{0,8},{8,0},{16,24},{24,16},{1,9},{9,1},{17,25},{25,17},{2,10},{10... | collective-permute-start | bytes 786440 | tf_op jit(solution)/shard_map/ppermute | solution.py:386
  7.4 15.1 %collective-permute-start.4 = (bf16[128,1024]{1,0:T(8,128)(2,1)S(1)}, bf16[128,1024]{1,0:T(8,128)(2,1)S(1)}, u32[]{:S(2)}, u32[]{:S(2)}) collective-permute-start(bf16[128,1024]{1,0:T(8,128)(2,1)S(1)} %get-tuple-element.44), channel_id=1, source_target_pairs={{0,24},{8,16},{16,8},{24,0},{1,25},{9,17},{17,9},{25,1},{2,26},{10... | collective-permute-start | bytes 786440 | tf_op jit(solution)/shard_map/ppermute | solution.py:386
  13.0 16.8 %collective-permute-start = (bf16[1024,1024]{1,0:T(8,128)(2,1)}, bf16[1024,1024]{1,0:T(8,128)(2,1)}, u32[]{:S(2)}, u32[]{:S(2)}) collective-permute-start(bf16[1024,1024]{1,0:T(8,128)(2,1)} %take_tiles.2.refs_0_), channel_id=1, source_target_pairs={{0,2},{2,0},{4,6},{6,4},{1,3},{3,1},{5,7},{7,5},{8,10},{10,8},{12,... | collective-permute-start | bytes 6291464 | tf_op jit(solution)/shard_map/ppermute | solution.py:403
  22.0 21.6 %collective-permute-start.8 = (bf16[1024,3072]{1,0:T(8,128)(2,1)}, bf16[1024,3072]{1,0:T(8,128)(2,1)}, u32[]{:S(2)}, u32[]{:S(2)}) collective-permute-start(bf16[1024,3072]{1,0:T(8,128)(2,1)} %take_tiles.3.refs_12_), channel_id=1, source_target_pairs={{0,2},{2,0},{4,6},{6,4},{1,3},{3,1},{5,7},{7,5},{8,10},{10,8},{12,... | collective-permute-start | bytes 18874376 | tf_op jit(solution)/shard_map/ppermute | solution.py:403
  22.5 6.5 %collective-permute-start.3 = (bf16[128,1024]{1,0:T(8,128)(2,1)S(1)}, bf16[128,1024]{1,0:T(8,128)(2,1)S(1)}, u32[]{:S(2)}, u32[]{:S(2)}) collective-permute-start(bf16[128,1024]{1,0:T(8,128)(2,1)S(1)} %collective-permute-done.2.refs_6_.refs_4_.refs_5_), channel_id=1, source_target_pairs={{0,2},{2,0},{4,6},{6,4},{1,3},{3,1},{5,7},{7,5},{8,10},{10,8},{12,... | collective-permute-start | bytes 786440 | tf_op jit(solution)/shard_map/ppermute | solution.py:387
  22.6 7.2 %collective-permute-start.5 = (bf16[128,1024]{1,0:T(8,128)(2,1)S(1)}, bf16[128,1024]{1,0:T(8,128)(2,1)S(1)}, u32[]{:S(2)}, u32[]{:S(2)}) collective-permute-start(bf16[128,1024]{1,0:T(8,128)(2,1)S(1)} %collective-permute-done.4.refs_8_.refs_6_.refs_7_), channel_id=1, source_target_pairs={{0,2},{2,0},{4,6},{6,4},{1,3},{3,1},{5,7},{7,5},{8,10},{10,8},{12,... | collective-permute-start | bytes 786440 | tf_op jit(solution)/shard_map/ppermute | solution.py:387
  41.4 24.3 %collective-permute-start.6 = (bf16[1024,2048]{1,0:T(8,128)(2,1)}, bf16[1024,2048]{1,0:T(8,128)(2,1)}, u32[]{:S(2)}, u32[]{:S(2)}) collective-permute-start(bf16[1024,2048]{1,0:T(8,128)(2,1)} %get-tuple-element.46), channel_id=1, source_target_pairs={{0,2},{2,0},{4,6},{6,4},{1,3},{3,1},{5,7},{7,5},{8,10},{10,8},{12,... | collective-permute-start | bytes 12582920 | tf_op jit(solution)/shard_map/ppermute | solution.py:403
  41.6 24.2 %collective-permute-start.7 = (bf16[1024,2048]{1,0:T(8,128)(2,1)}, bf16[1024,2048]{1,0:T(8,128)(2,1)}, u32[]{:S(2)}, u32[]{:S(2)}) collective-permute-start(bf16[1024,2048]{1,0:T(8,128)(2,1)} %get-tuple-element.47), channel_id=1, source_target_pairs={{0,2},{2,0},{4,6},{6,4},{1,3},{3,1},{5,7},{7,5},{8,10},{10,8},{12,... | collective-permute-start | bytes 12582920 | tf_op jit(solution)/shard_map/ppermute | solution.py:403
  41.9 15.1 %collective-permute-start.9 = (bf16[128,1024]{1,0:T(8,128)(2,1)}, bf16[128,1024]{1,0:T(8,128)(2,1)S(1)}, u32[]{:S(2)}, u32[]{:S(2)}) collective-permute-start(bf16[128,1024]{1,0:T(8,128)(2,1)} %get-tuple-element.51), channel_id=1, source_target_pairs={{0,16},{8,24},{16,0},{24,8},{1,17},{9,25},{17,1},{25,9},{2,18},{10... | collective-permute-start | bytes 786440 | tf_op jit(solution)/shard_map/ppermute | solution.py:386
  42.0 10.9 %copy-start.17 = (s32[128]{0:T(128)S(1)}, s32[128]{0:T(128)}, u32[]{:S(2)}) copy-start(s32[128]{0:T(128)} %param.11) | copy-start | bytes 1540
  42.0 22.3 %collective-permute-start.11 = (bf16[256,1024]{1,0:T(8,128)(2,1)}, bf16[256,1024]{1,0:T(8,128)(2,1)}, u32[]{:S(2)}, u32[]{:S(2)}) collective-permute-start(bf16[256,1024]{1,0:T(8,128)(2,1)} %copy-done.13), channel_id=1, source_target_pairs={{0,4},{2,6},{4,0},{6,2},{1,5},{3,7},{5,1},{7,3},{8,12},{10,14},{12... | collective-permute-start | bytes 1572872 | tf_op jit(solution)/shard_map/ppermute | solution.py:441
  52.4 15.2 %collective-permute-start.12 = (bf16[256,1024]{1,0:T(8,128)(2,1)}, bf16[256,1024]{1,0:T(8,128)(2,1)}, u32[]{:S(2)}, u32[]{:S(2)}) collective-permute-start(bf16[256,1024]{1,0:T(8,128)(2,1)} %get-tuple-element.49.refs_10_), channel_id=1, source_target_pairs={{0,4},{2,6},{4,0},{6,2},{1,5},{3,7},{5,1},{7,3},{8,12},{10,14},{12... | collective-permute-start | bytes 1572872 | tf_op jit(solution)/shard_map/ppermute | solution.py:441
  57.0 8.7 %collective-permute-start.10 = (bf16[128,1024]{1,0:T(8,128)(2,1)S(1)}, bf16[128,1024]{1,0:T(8,128)(2,1)S(1)}, u32[]{:S(2)}, u32[]{:S(2)}) collective-permute-start(bf16[128,1024]{1,0:T(8,128)(2,1)S(1)} %collective-permute-done.9.refs_11_), channel_id=1, source_target_pairs={{0,2},{2,0},{4,6},{6,4},{1,3},{3,1},{5,7},{7,5},{8,10},{10,8},{12,... | collective-permute-start | bytes 786440 | tf_op jit(solution)/shard_map/ppermute | solution.py:469
  57.0 10.6 %copy-start.5 = (bf16[2048,1024]{1,0:T(8,128)(2,1)S(1)}, bf16[2048,1024]{1,0:T(8,128)(2,1)}, u32[]{:S(2)}) copy-start(bf16[2048,1024]{1,0:T(8,128)(2,1)} %get-tuple-element.56.refs_4_) | copy-start | bytes 12582916
  64.3 25.8 %collective-permute-start.13 = (bf16[256,1024]{1,0:T(8,128)(2,1)S(1)}, bf16[256,1024]{1,0:T(8,128)(2,1)S(1)}, u32[]{:S(2)}, u32[]{:S(2)}) collective-permute-start(bf16[256,1024]{1,0:T(8,128)(2,1)S(1)} %get-tuple-element.58.refs_14_), channel_id=1, source_target_pairs={{0,4},{2,6},{4,0},{6,2},{1,5},{3,7},{5,1},{7,3},{8,12},{10,14},{12... | collective-permute-start | bytes 1572872 | tf_op jit(solution)/shard_map/ppermute | solution.py:441
  67.7 12.8 %copy-start.6 = (bf16[2048,1024]{1,0:T(8,128)(2,1)S(1)}, bf16[2048,1024]{1,0:T(8,128)(2,1)}, u32[]{:S(2)}) copy-start(bf16[2048,1024]{1,0:T(8,128)(2,1)} %get-tuple-element.54.refs_4_) | copy-start | bytes 12582916
  67.7 12.8 %copy-start.12 = (bf16[256,1024]{1,0:T(8,128)(2,1)S(1)}, bf16[256,1024]{1,0:T(8,128)(2,1)}, u32[]{:S(2)}) copy-start(bf16[256,1024]{1,0:T(8,128)(2,1)} %copy-done.11) | copy-start | bytes 1572868
  75.0 23.7 %collective-permute-start.14 = (bf16[256,1024]{1,0:T(8,128)(2,1)S(1)}, bf16[256,1024]{1,0:T(8,128)(2,1)S(1)}, u32[]{:S(2)}, u32[]{:S(2)}) collective-permute-start(bf16[256,1024]{1,0:T(8,128)(2,1)S(1)} %get-tuple-element.60.refs_2_), channel_id=1, source_target_pairs={{0,4},{2,6},{4,0},{6,2},{1,5},{3,7},{5,1},{7,3},{8,12},{10,14},{12... | collective-permute-start | bytes 1572872 | tf_op jit(solution)/shard_map/ppermute | solution.py:449
  77.7 20.9 %collective-permute-start.15 = (bf16[256,1024]{1,0:T(8,128)(2,1)S(1)}, bf16[256,1024]{1,0:T(8,128)(2,1)S(1)}, u32[]{:S(2)}, u32[]{:S(2)}) collective-permute-start(bf16[256,1024]{1,0:T(8,128)(2,1)S(1)} %add_terms.8.refs_14_), channel_id=1, source_target_pairs={{0,8},{8,0},{16,24},{24,16},{1,9},{9,1},{17,25},{25,17},{2,10},{10... | collective-permute-start | bytes 1572872 | tf_op jit(solution)/shard_map/ppermute | solution.py:454
  89.0 19.4 %collective-permute-start.16 = (bf16[256,1024]{1,0:T(8,128)(2,1)S(1)}, bf16[256,1024]{1,0:T(8,128)(2,1)S(1)}, u32[]{:S(2)}, u32[]{:S(2)}) collective-permute-start(bf16[256,1024]{1,0:T(8,128)(2,1)S(1)} %add_terms.9.refs_14_), channel_id=1, source_target_pairs={{0,8},{8,0},{16,24},{24,16},{1,9},{9,1},{17,25},{25,17},{2,10},{10... | collective-permute-start | bytes 1572872 | tf_op jit(solution)/shard_map/ppermute | solution.py:454
  89.5 28.6 %collective-permute-start.17 = (bf16[256,1024]{1,0:T(8,128)(2,1)S(1)}, bf16[256,1024]{1,0:T(8,128)(2,1)S(1)}, u32[]{:S(2)}, u32[]{:S(2)}) collective-permute-start(bf16[256,1024]{1,0:T(8,128)(2,1)S(1)} %get-tuple-element.62.refs_2_), channel_id=1, source_target_pairs={{0,4},{2,6},{4,0},{6,2},{1,5},{3,7},{5,1},{7,3},{8,12},{10,14},{12... | collective-permute-start | bytes 1572872 | tf_op jit(solution)/shard_map/ppermute | solution.py:449
  97.0 31.1 %collective-permute-start.22 = (bf16[256,1024]{1,0:T(8,128)(2,1)S(1)}, bf16[256,1024]{1,0:T(8,128)(2,1)S(1)}, u32[]{:S(2)}, u32[]{:S(2)}) collective-permute-start(bf16[256,1024]{1,0:T(8,128)(2,1)S(1)} %get-tuple-element.65.refs_3_), channel_id=1, source_target_pairs={{0,4},{2,6},{4,0},{6,2},{1,5},{3,7},{5,1},{7,3},{8,12},{10,14},{12... | collective-permute-start | bytes 1572872 | tf_op jit(solution)/shard_map/ppermute | solution.py:449
  98.8 18.2 %collective-permute-start.18 = (bf16[128,1024]{1,0:T(8,128)(2,1)S(1)}, bf16[128,1024]{1,0:T(8,128)(2,1)S(1)}, u32[]{:S(2)}, u32[]{:S(2)}) collective-permute-start(bf16[128,1024]{1,0:T(8,128)(2,1)S(1)} %add_terms.10.refs_2_), channel_id=1, source_target_pairs={{0,16},{8,24},{16,0},{24,8},{1,17},{9,25},{17,1},{25,9},{2,18},{10... | collective-permute-start | bytes 786440 | tf_op jit(solution)/shard_map/ppermute | solution.py:459
  102.2 13.8 %copy-start.1 = (bf16[128,16384]{1,0:T(8,128)(2,1)S(1)}, bf16[128,16384]{1,0:T(8,128)(2,1)}, u32[]{:S(2)}) copy-start(bf16[128,16384]{1,0:T(8,128)(2,1)} %refs_4_.1) | copy-start | bytes 12582916
  102.2 25.9 %collective-permute-start.23 = (bf16[256,1024]{1,0:T(8,128)(2,1)S(1)}, bf16[256,1024]{1,0:T(8,128)(2,1)S(1)}, u32[]{:S(2)}, u32[]{:S(2)}) collective-permute-start(bf16[256,1024]{1,0:T(8,128)(2,1)S(1)} %add_terms.11.refs_10_), channel_id=1, source_target_pairs={{0,8},{8,0},{16,24},{24,16},{1,9},{9,1},{17,25},{25,17},{2,10},{10... | collective-permute-start | bytes 1572872 | tf_op jit(solution)/shard_map/ppermute | solution.py:454
  115.4 14.6 %collective-permute-start.20 = (bf16[256,1024]{1,0:T(8,128)(2,1)S(1)}, bf16[256,1024]{1,0:T(8,128)(2,1)S(1)}, u32[]{:S(2)}, u32[]{:S(2)}) collective-permute-start(bf16[256,1024]{1,0:T(8,128)(2,1)S(1)} %get-tuple-element.66.refs_4_), channel_id=1, source_target_pairs={{0,4},{2,6},{4,0},{6,2},{1,5},{3,7},{5,1},{7,3},{8,12},{10,14},{12... | collective-permute-start | bytes 1572872 | tf_op jit(solution)/shard_map/ppermute | solution.py:441
  119.5 9.4 %collective-permute-start.21 = (bf16[128,1024]{1,0:T(8,128)(2,1)S(1)}, bf16[128,1024]{1,0:T(8,128)(2,1)S(1)}, u32[]{:S(2)}, u32[]{:S(2)}) collective-permute-start(bf16[128,1024]{1,0:T(8,128)(2,1)S(1)} %add_terms.12.refs_14_), channel_id=1, source_target_pairs={{0,16},{8,24},{16,0},{24,8},{1,17},{9,25},{17,1},{25,9},{2,18},{10... | collective-permute-start | bytes 786440 | tf_op jit(solution)/shard_map/ppermute | solution.py:459
  126.6 9.2 %collective-permute-start.19 = (bf16[256,1024]{1,0:T(8,128)(2,1)S(1)}, bf16[256,1024]{1,0:T(8,128)(2,1)S(1)}, u32[]{:S(2)}, u32[]{:S(2)}) collective-permute-start(bf16[256,1024]{1,0:T(8,128)(2,1)S(1)} %get-tuple-element.73.refs_3_), channel_id=1, source_target_pairs={{0,4},{2,6},{4,0},{6,2},{1,5},{3,7},{5,1},{7,3},{8,12},{10,14},{12... | collective-permute-start | bytes 1572872 | tf_op jit(solution)/shard_map/ppermute | solution.py:449
  131.5 14.2 %collective-permute-start.24 = (bf16[256,1024]{1,0:T(8,128)(2,1)S(1)}, bf16[256,1024]{1,0:T(8,128)(2,1)S(1)}, u32[]{:S(2)}, u32[]{:S(2)}) collective-permute-start(bf16[256,1024]{1,0:T(8,128)(2,1)S(1)} %add_terms.14.refs_3_), channel_id=1, source_target_pairs={{0,8},{8,0},{16,24},{24,16},{1,9},{9,1},{17,25},{25,17},{2,10},{10... | collective-permute-start | bytes 1572872 | tf_op jit(solution)/shard_map/ppermute | solution.py:454
  133.4 12.6 %collective-permute-start.26 = (bf16[128,1024]{1,0:T(8,128)(2,1)S(1)}, bf16[128,1024]{1,0:T(8,128)(2,1)S(1)}, u32[]{:S(2)}, u32[]{:S(2)}) collective-permute-start(bf16[128,1024]{1,0:T(8,128)(2,1)S(1)} %add_terms.13.refs_5_), channel_id=1, source_target_pairs={{0,16},{8,24},{16,0},{24,8},{1,17},{9,25},{17,1},{25,9},{2,18},{10... | collective-permute-start | bytes 786440 | tf_op jit(solution)/shard_map/ppermute | solution.py:459
  145.9 10.5 %collective-permute-start.25 = (bf16[128,1024]{1,0:T(8,128)(2,1)S(1)}, bf16[128,1024]{1,0:T(8,128)(2,1)S(1)}, u32[]{:S(2)}, u32[]{:S(2)}) collective-permute-start(bf16[128,1024]{1,0:T(8,128)(2,1)S(1)} %add_terms.15.refs_5_), channel_id=1, source_target_pairs={{0,16},{8,24},{16,0},{24,8},{1,17},{9,25},{17,1},{25,9},{2,18},{10... | collective-permute-start | bytes 786440 | tf_op jit(solution)/shard_map/ppermute | solution.py:459
  (13 other events, 45.4 us)

commit v6 on v5

--- a/solution.py
+++ b/solution.py
@@ -478,10 +478,10 @@
     cosine, sine_part = turn_tables(lax.optimization_barrier((hidden, done))[0], positions)
     out = finish(0, None, (done,))
     done = to_z2(1, (out,))
-    done = second(3, (done,))
-    done = to_z2(2, (done,))
+    done = second(3, (done, near_z[2], mid_y[2]))
     out = finish(1, out, (done,))
     done = to_z1(3, (out,))
+    done = to_z2(2, (done,))
     done = to_z2(3, (done,))
     out = finish(2, out, (done,))
     return finish(3, out, ())

time: 158 us -> 164 us (1.038)
  waiting for transfers between devices: 40 us -> 45.5 us
    ppermute x4, waiting for transfers between devices: 2.02 us -> 5.42 us  [second(): mid_y[i] = over_y(half)]
    ppermute x4, waiting for transfers between devices: 10.1 us -> 11.7 us  [to_z2(): far_z[i] = over_z2(operand)]
  transfers between devices with their start and end apart: 27 -> 27, of which waited for: 9 -> 9; matrix products, arithmetic and copies ran while one was open for 2% -> 2% of each run, Pallas kernels for 50% -> 48%
where the time goes in v6:
time: 164 us; the launch traced here: 163 us
  Pallas kernels  78.9 us (48%)
  waiting for transfers between devices  45.5 us (28%)
  starting transfers between devices  26.1 us (16%)
  local copies, waits for them, and re-layouts  11 us (7%)
    pallas_call x8, Pallas kernels, merge_pass(): pl.pallas_call(functools.partial(pass_kernel, len(bases), [len(line) for...  59.6 us
    ppermute x4, waiting for transfers between devices, to_z1(): near_z[i] = over_z1(operand)  15.8 us
    ppermute x4, waiting for transfers between devices, to_z2(): far_z[i] = over_z2(operand)  11.7 us
    pallas_call x2, Pallas kernels, take_tiles(): pl.pallas_call(take_kernel, grid_spec=pltpu.PrefetchScalarGridSpec(num_sc...  10.1 us
    unnamed x36, local copies, waits for them, and re-layouts  9.74 us
    ppermute x2, waiting for transfers between devices, line_shards(): first_lines = [[x1, over_core(x1)], [x3, over_core(x3)], [own_x, own_other]]  6.56 us
    ppermute x4, waiting for transfers between devices, second(): mid_y[i] = over_y(half)  5.42 us
    ppermute x4, starting transfers between devices, to_z1(): near_z[i] = over_z1(operand)  5.26 us
  transfers between devices with their start and end apart: 27, of which 9 were waited for; matrix products, arithmetic and copies ran while one was open for 2% of the time, Pallas kernels for 48%

profile of v6, /device:TPU:0, one launch (start us, length us, event | category | flops | bytes accessed | tf_op | source)
XLA Modules:
  0.0 163.3 jit_solution(653792638440519703)
XLA Ops:
  1.3 2.2 %copy-done = bf16[128,16384]{1,0:T(8,128)(2,1)S(1)} copy-done((bf16[128,16384]{1,0:T(8,128)(2,1)S(1)}, bf16[128,16384]{1,0:T(8,128)(2,1)}, u32[]{:S(2)}) %copy-start) | copy-done | bytes 4194328
  3.5 1.3 pick_features.1
  4.9 2.6 %collective-permute-start.2 = (bf16[128,1024]{1,0:T(8,128)(2,1)S(1)}, bf16[128,1024]{1,0:T(8,128)(2,1)S(1)}, u32[]{:S(2)}, u32[]{:S(2)}) collective-permute-start(bf16[128,1024]{1,0:T(8,128)(2,1)S(1)} %get-tuple-element.43), channel_id=1, source_target_pairs={{0,8},{8,0},{16,24},{24,16},{1,9},{9,1},{17,25},{25,17},{2,10},{10... | collective-permute-start | bytes 786440 | tf_op jit(solution)/shard_map/ppermute | solution.py:386
  7.4 2.5 %collective-permute-start.4 = (bf16[128,1024]{1,0:T(8,128)(2,1)S(1)}, bf16[128,1024]{1,0:T(8,128)(2,1)S(1)}, u32[]{:S(2)}, u32[]{:S(2)}) collective-permute-start(bf16[128,1024]{1,0:T(8,128)(2,1)S(1)} %get-tuple-element.44), channel_id=1, source_target_pairs={{0,24},{8,16},{16,8},{24,0},{1,25},{9,17},{17,9},{25,1},{2,26},{10... | collective-permute-start | bytes 786440 | tf_op jit(solution)/shard_map/ppermute | solution.py:386
  9.9 3.1 %take_tiles.2.refs_0_ = bf16[1024,1024]{1,0:T(8,128)(2,1)} custom-call(s32[1]{0:T(128)} %bitcast.4.table, bf16[1024,16384]{1,0:T(8,128)(2,1)} %refs_0_.17, bf16[128,1024]{1,0:T(8,128)(2,1)S(1)} %get-tuple-element.42.refs_0_.refs_10_.refs_8_.refs_9_), custom_call_target="tpu_custom_call" | custom-call | tf_op jit(solution)/shard_map/take_tiles/pallas_call | solution.py:274
  13.4 1.6 copy-done.4
  15.0 7.0 %take_tiles.3.refs_12_ = bf16[1024,3072]{1,0:T(8,128)(2,1)} custom-call(s32[3]{0:T(128)S(1)} %pad_add_fusion.table, bf16[1024,16384]{1,0:T(8,128)(2,1)} %refs_0_.17, bf16[1024,1024]{1,0:T(8,128)(2,1)S(1)} %copy-done.4, bf16[2048,32]{1,0:T(8,128)(2,1)S(1)} %copy.17.refs_1_.refs_4_.refs_2_), custom_call_target="tpu_custom_call" | custom-call | tf_op jit(solution)/shard_map/take_tiles/pallas_call | solution.py:274
  23.2 5.8 %collective-permute-done.3.refs_7_.refs_5_.refs_6_ = bf16[128,1024]{1,0:T(8,128)(2,1)S(1)} collective-permute-done((bf16[128,1024]{1,0:T(8,128)(2,1)S(1)}, bf16[128,1024]{1,0:T(8,128)(2,1)S(1)}, u32[]{:S(2)}, u32[]{:S(2)}) %collective-permute-start.3) | collective-permute-done | bytes 262176 | tf_op jit(solution)/shard_map/ppermute | solution.py:387
  29.8 10.0 %merge_pass.8 = (bf16[2048,1024]{1,0:T(8,128)(2,1)}, bf16[256,1024]{1,0:T(8,128)(2,1)S(1)}, bf16[256,1024]{1,0:T(8,128)(2,1)S(1)}, bf16[1024,2048]{1,0:T(8,128)(2,1)}, bf16[1024,2048]{1,0:T(8,128)(2,1)}) custom-call(s32[6]{0:T(128)S(1)} %concatenate.13.table, bf16[1024,16384]{1,0:T(8,128)(2,1)} %refs_0_.17, bf16[1024,16384]{1,0:T(8,128)(2,1)} %refs_0_.17, ...), custom_call_target="tpu_custom_call" | custom-call | flops 1610612736 | bytes 8388608 | tf_op jit(solution)/shard_map/merge_pass/pallas_call | solution.py:248
  42.0 1.6 collective-permute-start.11
  44.6 7.0 %merge_pass.9 = (bf16[2048,1024]{1,0:T(8,128)(2,1)}, bf16[256,1024]{1,0:T(8,128)(2,1)}, bf16[256,1024]{1,0:T(8,128)(2,1)S(1)}) custom-call(s32[2]{0:T(128)S(1)} %iota_add_fusion.3.table, bf16[1024,16384]{1,0:T(8,128)(2,1)} %refs_0_.17, bf16[1024,3072]{1,0:T(8,128)(2,1)} %collective-permute-done.8.refs_1_, bf16[2048,32]{1,0:T(8,128)(2,1)S(1)} %copy.17.refs_1_.refs_4_.refs_2_, ...), custom_call_target="tpu_custom_call" | custom-call | flops 1610612736 | bytes 8388608 | tf_op jit(solution)/shard_map/merge_pass/pallas_call | solution.py:248
  52.9 4.1 %collective-permute-done.9.refs_11_ = bf16[128,1024]{1,0:T(8,128)(2,1)S(1)} collective-permute-done((bf16[128,1024]{1,0:T(8,128)(2,1)}, bf16[128,1024]{1,0:T(8,128)(2,1)S(1)}, u32[]{:S(2)}, u32[]{:S(2)}) %collective-permute-start.9) | collective-permute-done | bytes 262176 | tf_op jit(solution)/shard_map/ppermute | solution.py:386
  57.1 7.2 %merge_pass.10 = (bf16[2048,1024]{1,0:T(8,128)(2,1)}, bf16[256,1024]{1,0:T(8,128)(2,1)S(1)}, bf16[256,1024]{1,0:T(8,128)(2,1)S(1)}) custom-call(s32[2]{0:T(128)S(1)} %iota_add_fusion.4.table, bf16[1024,16384]{1,0:T(8,128)(2,1)} %refs_0_.17, bf16[1024,3072]{1,0:T(8,128)(2,1)} %collective-permute-done.8.refs_1_, ...), custom_call_target="tpu_custom_call" | custom-call | flops 1610612736 | bytes 8388608 | tf_op jit(solution)/shard_map/merge_pass/pallas_call | solution.py:248
  64.3 1.5 collective-permute-start.13
  65.8 1.9 %collective-permute-done.12.refs_18_.refs_15_.refs_1_ = bf16[256,1024]{1,0:T(8,128)(2,1)} collective-permute-done((bf16[256,1024]{1,0:T(8,128)(2,1)}, bf16[256,1024]{1,0:T(8,128)(2,1)}, u32[]{:S(2)}, u32[]{:S(2)}) %collective-permute-start.12) | collective-permute-done | bytes 524320 | tf_op jit(solution)/shard_map/ppermute | solution.py:441
  67.7 7.3 %merge_pass.11 = (bf16[256,1024]{1,0:T(8,128)(2,1)S(1)}, bf16[256,1024]{1,0:T(8,128)(2,1)S(1)}, bf16[128,1024]{1,0:T(8,128)(2,1)S(1)}, bf16[128,1024]{1,0:T(8,128)(2,1)S(1)}) custom-call(s32[2]{0:T(128)S(1)} %iota_add_fusion.1.table, bf16[1024,16384]{1,0:T(8,128)(2,1)} %refs_0_.17, ...), custom_call_target="tpu_custom_call", output_to_operand_aliasing={{0}: (14, {})} | custom-call | flops 2147483648 | bytes 8388608 | tf_op jit(solution)/shard_map/merge_pass/pallas_call | solution.py:248
  75.0 1.6 collective-permute-start.14
  77.7 2.7 %collective-permute-start.15 = (bf16[256,1024]{1,0:T(8,128)(2,1)S(1)}, bf16[256,1024]{1,0:T(8,128)(2,1)S(1)}, u32[]{:S(2)}, u32[]{:S(2)}) collective-permute-start(bf16[256,1024]{1,0:T(8,128)(2,1)S(1)} %add_terms.8.refs_14_), channel_id=1, source_target_pairs={{0,8},{8,0},{16,24},{24,16},{1,9},{9,1},{17,25},{25,17},{2,10},{10... | collective-permute-start | bytes 1572872 | tf_op jit(solution)/shard_map/ppermute | solution.py:454
  80.4 7.2 %merge_pass.12 = (bf16[256,1024]{1,0:T(8,128)(2,1)S(1)}, bf16[256,1024]{1,0:T(8,128)(2,1)S(1)}, bf16[128,1024]{1,0:T(8,128)(2,1)S(1)}, bf16[128,1024]{1,0:T(8,128)(2,1)S(1)}) custom-call(s32[2]{0:T(128)S(1)} %iota_add_fusion.2.table, bf16[1024,16384]{1,0:T(8,128)(2,1)} %refs_0_.17, ...), custom_call_target="tpu_custom_call", output_to_operand_aliasing={{0}: (14, {})} | custom-call | flops 2147483648 | bytes 8388608 | tf_op jit(solution)/shard_map/merge_pass/pallas_call | solution.py:248
  87.7 1.3 add_terms.9.refs_14_
  90.0 7.0 %merge_pass.13 = (bf16[256,1024]{1,0:T(8,128)(2,1)S(1)}, bf16[256,1024]{1,0:T(8,128)(2,1)S(1)}, bf16[128,1024]{1,0:T(8,128)(2,1)S(1)}, bf16[128,1024]{1,0:T(8,128)(2,1)S(1)}) custom-call(s32[2]{0:T(128)S(1)} %iota_add_fusion.5.table, bf16[1024,16384]{1,0:T(8,128)(2,1)} %refs_0_.17, ...), custom_call_target="tpu_custom_call", output_to_operand_aliasing={{0}: (14, {})} | custom-call | flops 2147483648 | bytes 8388608 | tf_op jit(solution)/shard_map/merge_pass/pallas_call | solution.py:248
  97.0 1.6 collective-permute-start.20
  98.8 3.0 %collective-permute-start.18 = (bf16[128,1024]{1,0:T(8,128)(2,1)S(1)}, bf16[128,1024]{1,0:T(8,128)(2,1)S(1)}, u32[]{:S(2)}, u32[]{:S(2)}) collective-permute-start(bf16[128,1024]{1,0:T(8,128)(2,1)S(1)} %add_terms.10.refs_2_), channel_id=1, source_target_pairs={{0,16},{8,24},{16,0},{24,8},{1,17},{9,25},{17,1},{25,9},{2,18},{10... | collective-permute-start | bytes 786440 | tf_op jit(solution)/shard_map/ppermute | solution.py:459
  102.9 5.5 %collective-permute-done.16.refs_11_.refs_2_ = bf16[256,1024]{1,0:T(8,128)(2,1)S(1)} collective-permute-done((bf16[256,1024]{1,0:T(8,128)(2,1)S(1)}, bf16[256,1024]{1,0:T(8,128)(2,1)S(1)}, u32[]{:S(2)}, u32[]{:S(2)}) %collective-permute-start.16) | collective-permute-done | bytes 524320 | tf_op jit(solution)/shard_map/ppermute | solution.py:454
  108.5 6.9 %merge_pass.14 = (bf16[2048,1024]{1,0:T(8,128)(2,1)}, bf16[256,1024]{1,0:T(8,128)(2,1)S(1)}, bf16[256,1024]{1,0:T(8,128)(2,1)S(1)}) custom-call(s32[2]{0:T(128)S(1)} %iota_add_fusion.7.table, bf16[1024,16384]{1,0:T(8,128)(2,1)} %refs_0_.17, bf16[1024,2048]{1,0:T(8,128)(2,1)} %collective-permute-done.6.refs_15_.refs_1_, ...), custom_call_target="tpu_custom_call" | custom-call | flops 1610612736 | bytes 8388608 | tf_op jit(solution)/shard_map/merge_pass/pallas_call | solution.py:248
  119.6 1.8 %collective-permute-done.19.refs_15_.refs_2_ = bf16[256,1024]{1,0:T(8,128)(2,1)S(1)} collective-permute-done((bf16[256,1024]{1,0:T(8,128)(2,1)S(1)}, bf16[256,1024]{1,0:T(8,128)(2,1)S(1)}, u32[]{:S(2)}, u32[]{:S(2)}) %collective-permute-start.19) | collective-permute-done | bytes 524320 | tf_op jit(solution)/shard_map/ppermute | solution.py:454
  121.4 7.0 %merge_pass.15 = (bf16[256,1024]{1,0:T(8,128)(2,1)S(1)}, bf16[256,1024]{1,0:T(8,128)(2,1)S(1)}, bf16[128,1024]{1,0:T(8,128)(2,1)S(1)}, bf16[128,1024]{1,0:T(8,128)(2,1)S(1)}) custom-call(s32[2]{0:T(128)S(1)} %iota_add_fusion.table, bf16[1024,16384]{1,0:T(8,128)(2,1)} %refs_0_.17, ...), custom_call_target="tpu_custom_call", output_to_operand_aliasing={{0}: (14, {})} | custom-call | flops 2147483648 | bytes 8388608 | tf_op jit(solution)/shard_map/merge_pass/pallas_call | solution.py:248
  131.5 1.6 collective-permute-start.24
  133.4 1.5 collective-permute-start.26
  134.9 5.4 %collective-permute-done.21.refs_1_ = bf16[256,1024]{1,0:T(8,128)(2,1)S(1)} collective-permute-done((bf16[256,1024]{1,0:T(8,128)(2,1)S(1)}, bf16[256,1024]{1,0:T(8,128)(2,1)S(1)}, u32[]{:S(2)}, u32[]{:S(2)}) %collective-permute-start.21) | collective-permute-done | bytes 524320 | tf_op jit(solution)/shard_map/ppermute | solution.py:449
  140.3 8.5 %collective-permute-done.24.refs_2_ = bf16[256,1024]{1,0:T(8,128)(2,1)S(1)} collective-permute-done((bf16[256,1024]{1,0:T(8,128)(2,1)S(1)}, bf16[256,1024]{1,0:T(8,128)(2,1)S(1)}, u32[]{:S(2)}, u32[]{:S(2)}) %collective-permute-start.24) | collective-permute-done | bytes 524320 | tf_op jit(solution)/shard_map/ppermute | solution.py:454
  150.6 11.7 %collective-permute-done.25.refs_3_ = bf16[128,1024]{1,0:T(8,128)(2,1)S(1)} collective-permute-done((bf16[128,1024]{1,0:T(8,128)(2,1)S(1)}, bf16[128,1024]{1,0:T(8,128)(2,1)S(1)}, u32[]{:S(2)}, u32[]{:S(2)}) %collective-permute-start.25) | collective-permute-done | bytes 262176 | tf_op jit(solution)/shard_map/ppermute | solution.py:459
  (102 shorter events, 22.0 us)
Async XLA Ops:
  0.0 13.1 %collective-permute-start.1 = (bf16[1024,32]{0,1:T(8,128)(2,1)}, bf16[1024,32]{0,1:T(8,128)(2,1)S(1)}, u32[]{:S(2)}, u32[]{:S(2)}) collective-permute-start(bf16[1024,32]{0,1:T(8,128)(2,1)} %param.8), channel_id=1, source_target_pairs={{0,2},{2,0},{4,6},{6,4},{1,3},{3,1},{5,7},{7,5},{8,10},{10,8},{12,... | collective-permute-start | bytes 196616 | tf_op jit(solution)/shard_map/ppermute | solution.py:389
  4.9 17.6 %collective-permute-start.2 = (bf16[128,1024]{1,0:T(8,128)(2,1)S(1)}, bf16[128,1024]{1,0:T(8,128)(2,1)S(1)}, u32[]{:S(2)}, u32[]{:S(2)}) collective-permute-start(bf16[128,1024]{1,0:T(8,128)(2,1)S(1)} %get-tuple-element.43), channel_id=1, source_target_pairs={{0,8},{8,0},{16,24},{24,16},{1,9},{9,1},{17,25},{25,17},{2,10},{10... | collective-permute-start | bytes 786440 | tf_op jit(solution)/shard_map/ppermute | solution.py:386
  7.4 15.1 %collective-permute-start.4 = (bf16[128,1024]{1,0:T(8,128)(2,1)S(1)}, bf16[128,1024]{1,0:T(8,128)(2,1)S(1)}, u32[]{:S(2)}, u32[]{:S(2)}) collective-permute-start(bf16[128,1024]{1,0:T(8,128)(2,1)S(1)} %get-tuple-element.44), channel_id=1, source_target_pairs={{0,24},{8,16},{16,8},{24,0},{1,25},{9,17},{17,9},{25,1},{2,26},{10... | collective-permute-start | bytes 786440 | tf_op jit(solution)/shard_map/ppermute | solution.py:386
  13.0 16.8 %collective-permute-start = (bf16[1024,1024]{1,0:T(8,128)(2,1)}, bf16[1024,1024]{1,0:T(8,128)(2,1)}, u32[]{:S(2)}, u32[]{:S(2)}) collective-permute-start(bf16[1024,1024]{1,0:T(8,128)(2,1)} %take_tiles.2.refs_0_), channel_id=1, source_target_pairs={{0,2},{2,0},{4,6},{6,4},{1,3},{3,1},{5,7},{7,5},{8,10},{10,8},{12,... | collective-permute-start | bytes 6291464 | tf_op jit(solution)/shard_map/ppermute | solution.py:403
  22.0 21.6 %collective-permute-start.8 = (bf16[1024,3072]{1,0:T(8,128)(2,1)}, bf16[1024,3072]{1,0:T(8,128)(2,1)}, u32[]{:S(2)}, u32[]{:S(2)}) collective-permute-start(bf16[1024,3072]{1,0:T(8,128)(2,1)} %take_tiles.3.refs_12_), channel_id=1, source_target_pairs={{0,2},{2,0},{4,6},{6,4},{1,3},{3,1},{5,7},{7,5},{8,10},{10,8},{12,... | collective-permute-start | bytes 18874376 | tf_op jit(solution)/shard_map/ppermute | solution.py:403
  22.5 6.5 %collective-permute-start.3 = (bf16[128,1024]{1,0:T(8,128)(2,1)S(1)}, bf16[128,1024]{1,0:T(8,128)(2,1)S(1)}, u32[]{:S(2)}, u32[]{:S(2)}) collective-permute-start(bf16[128,1024]{1,0:T(8,128)(2,1)S(1)} %collective-permute-done.2.refs_6_.refs_4_.refs_5_), channel_id=1, source_target_pairs={{0,2},{2,0},{4,6},{6,4},{1,3},{3,1},{5,7},{7,5},{8,10},{10,8},{12,... | collective-permute-start | bytes 786440 | tf_op jit(solution)/shard_map/ppermute | solution.py:387
  22.6 7.2 %collective-permute-start.5 = (bf16[128,1024]{1,0:T(8,128)(2,1)S(1)}, bf16[128,1024]{1,0:T(8,128)(2,1)S(1)}, u32[]{:S(2)}, u32[]{:S(2)}) collective-permute-start(bf16[128,1024]{1,0:T(8,128)(2,1)S(1)} %collective-permute-done.4.refs_8_.refs_6_.refs_7_), channel_id=1, source_target_pairs={{0,2},{2,0},{4,6},{6,4},{1,3},{3,1},{5,7},{7,5},{8,10},{10,8},{12,... | collective-permute-start | bytes 786440 | tf_op jit(solution)/shard_map/ppermute | solution.py:387
  41.4 24.3 %collective-permute-start.6 = (bf16[1024,2048]{1,0:T(8,128)(2,1)}, bf16[1024,2048]{1,0:T(8,128)(2,1)}, u32[]{:S(2)}, u32[]{:S(2)}) collective-permute-start(bf16[1024,2048]{1,0:T(8,128)(2,1)} %get-tuple-element.46), channel_id=1, source_target_pairs={{0,2},{2,0},{4,6},{6,4},{1,3},{3,1},{5,7},{7,5},{8,10},{10,8},{12,... | collective-permute-start | bytes 12582920 | tf_op jit(solution)/shard_map/ppermute | solution.py:403
  41.6 24.2 %collective-permute-start.7 = (bf16[1024,2048]{1,0:T(8,128)(2,1)}, bf16[1024,2048]{1,0:T(8,128)(2,1)}, u32[]{:S(2)}, u32[]{:S(2)}) collective-permute-start(bf16[1024,2048]{1,0:T(8,128)(2,1)} %get-tuple-element.47), channel_id=1, source_target_pairs={{0,2},{2,0},{4,6},{6,4},{1,3},{3,1},{5,7},{7,5},{8,10},{10,8},{12,... | collective-permute-start | bytes 12582920 | tf_op jit(solution)/shard_map/ppermute | solution.py:403
  41.9 15.1 %collective-permute-start.9 = (bf16[128,1024]{1,0:T(8,128)(2,1)}, bf16[128,1024]{1,0:T(8,128)(2,1)S(1)}, u32[]{:S(2)}, u32[]{:S(2)}) collective-permute-start(bf16[128,1024]{1,0:T(8,128)(2,1)} %get-tuple-element.51), channel_id=1, source_target_pairs={{0,16},{8,24},{16,0},{24,8},{1,17},{9,25},{17,1},{25,9},{2,18},{10... | collective-permute-start | bytes 786440 | tf_op jit(solution)/shard_map/ppermute | solution.py:386
  42.0 10.9 %copy-start.17 = (s32[128]{0:T(128)S(1)}, s32[128]{0:T(128)}, u32[]{:S(2)}) copy-start(s32[128]{0:T(128)} %param.11) | copy-start | bytes 1540
  42.0 22.3 %collective-permute-start.11 = (bf16[256,1024]{1,0:T(8,128)(2,1)}, bf16[256,1024]{1,0:T(8,128)(2,1)}, u32[]{:S(2)}, u32[]{:S(2)}) collective-permute-start(bf16[256,1024]{1,0:T(8,128)(2,1)} %copy-done.13), channel_id=1, source_target_pairs={{0,4},{2,6},{4,0},{6,2},{1,5},{3,7},{5,1},{7,3},{8,12},{10,14},{12... | collective-permute-start | bytes 1572872 | tf_op jit(solution)/shard_map/ppermute | solution.py:441
  52.4 15.2 %collective-permute-start.12 = (bf16[256,1024]{1,0:T(8,128)(2,1)}, bf16[256,1024]{1,0:T(8,128)(2,1)}, u32[]{:S(2)}, u32[]{:S(2)}) collective-permute-start(bf16[256,1024]{1,0:T(8,128)(2,1)} %get-tuple-element.49.refs_10_), channel_id=1, source_target_pairs={{0,4},{2,6},{4,0},{6,2},{1,5},{3,7},{5,1},{7,3},{8,12},{10,14},{12... | collective-permute-start | bytes 1572872 | tf_op jit(solution)/shard_map/ppermute | solution.py:441
  57.0 8.7 %collective-permute-start.10 = (bf16[128,1024]{1,0:T(8,128)(2,1)S(1)}, bf16[128,1024]{1,0:T(8,128)(2,1)S(1)}, u32[]{:S(2)}, u32[]{:S(2)}) collective-permute-start(bf16[128,1024]{1,0:T(8,128)(2,1)S(1)} %collective-permute-done.9.refs_11_), channel_id=1, source_target_pairs={{0,2},{2,0},{4,6},{6,4},{1,3},{3,1},{5,7},{7,5},{8,10},{10,8},{12,... | collective-permute-start | bytes 786440 | tf_op jit(solution)/shard_map/ppermute | solution.py:469
  57.0 10.6 %copy-start.5 = (bf16[2048,1024]{1,0:T(8,128)(2,1)S(1)}, bf16[2048,1024]{1,0:T(8,128)(2,1)}, u32[]{:S(2)}) copy-start(bf16[2048,1024]{1,0:T(8,128)(2,1)} %get-tuple-element.56.refs_4_) | copy-start | bytes 12582916
  64.3 25.8 %collective-permute-start.13 = (bf16[256,1024]{1,0:T(8,128)(2,1)S(1)}, bf16[256,1024]{1,0:T(8,128)(2,1)S(1)}, u32[]{:S(2)}, u32[]{:S(2)}) collective-permute-start(bf16[256,1024]{1,0:T(8,128)(2,1)S(1)} %get-tuple-element.58.refs_14_), channel_id=1, source_target_pairs={{0,4},{2,6},{4,0},{6,2},{1,5},{3,7},{5,1},{7,3},{8,12},{10,14},{12... | collective-permute-start | bytes 1572872 | tf_op jit(solution)/shard_map/ppermute | solution.py:441
  67.7 12.8 %copy-start.6 = (bf16[2048,1024]{1,0:T(8,128)(2,1)S(1)}, bf16[2048,1024]{1,0:T(8,128)(2,1)}, u32[]{:S(2)}) copy-start(bf16[2048,1024]{1,0:T(8,128)(2,1)} %get-tuple-element.54.refs_4_) | copy-start | bytes 12582916
  67.7 12.8 %copy-start.12 = (bf16[256,1024]{1,0:T(8,128)(2,1)S(1)}, bf16[256,1024]{1,0:T(8,128)(2,1)}, u32[]{:S(2)}) copy-start(bf16[256,1024]{1,0:T(8,128)(2,1)} %copy-done.11) | copy-start | bytes 1572868
  75.0 23.7 %collective-permute-start.14 = (bf16[256,1024]{1,0:T(8,128)(2,1)S(1)}, bf16[256,1024]{1,0:T(8,128)(2,1)S(1)}, u32[]{:S(2)}, u32[]{:S(2)}) collective-permute-start(bf16[256,1024]{1,0:T(8,128)(2,1)S(1)} %get-tuple-element.60.refs_2_), channel_id=1, source_target_pairs={{0,4},{2,6},{4,0},{6,2},{1,5},{3,7},{5,1},{7,3},{8,12},{10,14},{12... | collective-permute-start | bytes 1572872 | tf_op jit(solution)/shard_map/ppermute | solution.py:449
  77.7 20.9 %collective-permute-start.15 = (bf16[256,1024]{1,0:T(8,128)(2,1)S(1)}, bf16[256,1024]{1,0:T(8,128)(2,1)S(1)}, u32[]{:S(2)}, u32[]{:S(2)}) collective-permute-start(bf16[256,1024]{1,0:T(8,128)(2,1)S(1)} %add_terms.8.refs_14_), channel_id=1, source_target_pairs={{0,8},{8,0},{16,24},{24,16},{1,9},{9,1},{17,25},{25,17},{2,10},{10... | collective-permute-start | bytes 1572872 | tf_op jit(solution)/shard_map/ppermute | solution.py:454
  89.0 19.4 %collective-permute-start.16 = (bf16[256,1024]{1,0:T(8,128)(2,1)S(1)}, bf16[256,1024]{1,0:T(8,128)(2,1)S(1)}, u32[]{:S(2)}, u32[]{:S(2)}) collective-permute-start(bf16[256,1024]{1,0:T(8,128)(2,1)S(1)} %add_terms.9.refs_14_), channel_id=1, source_target_pairs={{0,8},{8,0},{16,24},{24,16},{1,9},{9,1},{17,25},{25,17},{2,10},{10... | collective-permute-start | bytes 1572872 | tf_op jit(solution)/shard_map/ppermute | solution.py:454
  89.5 28.6 %collective-permute-start.17 = (bf16[256,1024]{1,0:T(8,128)(2,1)S(1)}, bf16[256,1024]{1,0:T(8,128)(2,1)S(1)}, u32[]{:S(2)}, u32[]{:S(2)}) collective-permute-start(bf16[256,1024]{1,0:T(8,128)(2,1)S(1)} %get-tuple-element.62.refs_2_), channel_id=1, source_target_pairs={{0,4},{2,6},{4,0},{6,2},{1,5},{3,7},{5,1},{7,3},{8,12},{10,14},{12... | collective-permute-start | bytes 1572872 | tf_op jit(solution)/shard_map/ppermute | solution.py:449
  97.0 22.6 %collective-permute-start.20 = (bf16[256,1024]{1,0:T(8,128)(2,1)S(1)}, bf16[256,1024]{1,0:T(8,128)(2,1)S(1)}, u32[]{:S(2)}, u32[]{:S(2)}) collective-permute-start(bf16[256,1024]{1,0:T(8,128)(2,1)S(1)} %get-tuple-element.65.refs_3_), channel_id=1, source_target_pairs={{0,4},{2,6},{4,0},{6,2},{1,5},{3,7},{5,1},{7,3},{8,12},{10,14},{12... | collective-permute-start | bytes 1572872 | tf_op jit(solution)/shard_map/ppermute | solution.py:449
  98.8 18.2 %collective-permute-start.18 = (bf16[128,1024]{1,0:T(8,128)(2,1)S(1)}, bf16[128,1024]{1,0:T(8,128)(2,1)S(1)}, u32[]{:S(2)}, u32[]{:S(2)}) collective-permute-start(bf16[128,1024]{1,0:T(8,128)(2,1)S(1)} %add_terms.10.refs_2_), channel_id=1, source_target_pairs={{0,16},{8,24},{16,0},{24,8},{1,17},{9,25},{17,1},{25,9},{2,18},{10... | collective-permute-start | bytes 786440 | tf_op jit(solution)/shard_map/ppermute | solution.py:459
  102.2 13.8 %copy-start.1 = (bf16[128,16384]{1,0:T(8,128)(2,1)S(1)}, bf16[128,16384]{1,0:T(8,128)(2,1)}, u32[]{:S(2)}) copy-start(bf16[128,16384]{1,0:T(8,128)(2,1)} %refs_4_.1) | copy-start | bytes 12582916
  102.2 19.2 %collective-permute-start.19 = (bf16[256,1024]{1,0:T(8,128)(2,1)S(1)}, bf16[256,1024]{1,0:T(8,128)(2,1)S(1)}, u32[]{:S(2)}, u32[]{:S(2)}) collective-permute-start(bf16[256,1024]{1,0:T(8,128)(2,1)S(1)} %add_terms.11.refs_10_), channel_id=1, source_target_pairs={{0,8},{8,0},{16,24},{24,16},{1,9},{9,1},{17,25},{25,17},{2,10},{10... | collective-permute-start | bytes 1572872 | tf_op jit(solution)/shard_map/ppermute | solution.py:454
  115.4 14.6 %collective-permute-start.22 = (bf16[256,1024]{1,0:T(8,128)(2,1)S(1)}, bf16[256,1024]{1,0:T(8,128)(2,1)S(1)}, u32[]{:S(2)}, u32[]{:S(2)}) collective-permute-start(bf16[256,1024]{1,0:T(8,128)(2,1)S(1)} %get-tuple-element.66.refs_4_), channel_id=1, source_target_pairs={{0,4},{2,6},{4,0},{6,2},{1,5},{3,7},{5,1},{7,3},{8,12},{10,14},{12... | collective-permute-start | bytes 1572872 | tf_op jit(solution)/shard_map/ppermute | solution.py:441
  119.5 9.5 %collective-permute-start.23 = (bf16[128,1024]{1,0:T(8,128)(2,1)S(1)}, bf16[128,1024]{1,0:T(8,128)(2,1)S(1)}, u32[]{:S(2)}, u32[]{:S(2)}) collective-permute-start(bf16[128,1024]{1,0:T(8,128)(2,1)S(1)} %add_terms.12.refs_14_), channel_id=1, source_target_pairs={{0,16},{8,24},{16,0},{24,8},{1,17},{9,25},{17,1},{25,9},{2,18},{10... | collective-permute-start | bytes 786440 | tf_op jit(solution)/shard_map/ppermute | solution.py:459
  128.4 11.9 %collective-permute-start.21 = (bf16[256,1024]{1,0:T(8,128)(2,1)S(1)}, bf16[256,1024]{1,0:T(8,128)(2,1)S(1)}, u32[]{:S(2)}, u32[]{:S(2)}) collective-permute-start(bf16[256,1024]{1,0:T(8,128)(2,1)S(1)} %get-tuple-element.73.refs_5_), channel_id=1, source_target_pairs={{0,4},{2,6},{4,0},{6,2},{1,5},{3,7},{5,1},{7,3},{8,12},{10,14},{12... | collective-permute-start | bytes 1572872 | tf_op jit(solution)/shard_map/ppermute | solution.py:449
  131.5 17.2 %collective-permute-start.24 = (bf16[256,1024]{1,0:T(8,128)(2,1)S(1)}, bf16[256,1024]{1,0:T(8,128)(2,1)S(1)}, u32[]{:S(2)}, u32[]{:S(2)}) collective-permute-start(bf16[256,1024]{1,0:T(8,128)(2,1)S(1)} %add_terms.13.refs_3_), channel_id=1, source_target_pairs={{0,8},{8,0},{16,24},{24,16},{1,9},{9,1},{17,25},{25,17},{2,10},{10... | collective-permute-start | bytes 1572872 | tf_op jit(solution)/shard_map/ppermute | solution.py:454
  133.4 16.2 %collective-permute-start.26 = (bf16[128,1024]{1,0:T(8,128)(2,1)S(1)}, bf16[128,1024]{1,0:T(8,128)(2,1)S(1)}, u32[]{:S(2)}, u32[]{:S(2)}) collective-permute-start(bf16[128,1024]{1,0:T(8,128)(2,1)S(1)} %add_terms.14.refs_3_), channel_id=1, source_target_pairs={{0,16},{8,24},{16,0},{24,8},{1,17},{9,25},{17,1},{25,9},{2,18},{10... | collective-permute-start | bytes 786440 | tf_op jit(solution)/shard_map/ppermute | solution.py:459
  149.0 13.3 %collective-permute-start.25 = (bf16[128,1024]{1,0:T(8,128)(2,1)S(1)}, bf16[128,1024]{1,0:T(8,128)(2,1)S(1)}, u32[]{:S(2)}, u32[]{:S(2)}) collective-permute-start(bf16[128,1024]{1,0:T(8,128)(2,1)S(1)} %add_terms.15.refs_5_), channel_id=1, source_target_pairs={{0,16},{8,24},{16,0},{24,8},{1,17},{9,25},{17,1},{25,9},{2,18},{10... | collective-permute-start | bytes 786440 | tf_op jit(solution)/shard_map/ppermute | solution.py:459
  (13 other events, 47.2 us)
